TPU v7x, 32 devices: a whole 2x2x4 slice. The times are simulated.
32 devices in a mesh: lat: 4 (over y, core), lon: 8 (over z, x).
Axes of the slice: x: 2, y: 2, z: 4, core: 2. Of those that a mesh axis runs over, the one named last changes fastest.
Arguments:
- tracers: float32 [2, 4, 64, 2048], P(None, None, 'lat', 'lon'), may hold values from -6 to 6
- cotangent: float32 [2, 4, 64, 2048], P(None, None, 'lat', 'lon'), may hold values from -6 to 6
- land_mask: int32 [4, 64, 2048], P(None, 'lat', 'lon'), may hold values 0 or 1
- diffusion: float32 [3, 4, 64, 2048], P(None, None, 'lat', 'lon'), may hold values from 0.01 to 0.1
- velocity: float32 [2, 4, 64, 2048], P(None, None, 'lat', 'lon'), may hold values from -0.1 to 0.1
- weights: float32 [32, 128, 128], replicated, may hold values from -0.1875 to 0.1875
- atm_state: float32 [2, 4, 2048, 128], P(None, 'lat', 'lon'), may hold values from -6 to 6
- margins: int32 [3, 4, 8, 8, 64], P(None, 'lat', 'lon'), may hold values from -1 to 255, as said below
Outputs:
- final_tracers: float32 [2, 4, 64, 2048], P(None, None, 'lat', 'lon')
- adjoint_tracers: float32 [2, 4, 64, 2048], P(None, None, 'lat', 'lon')
- atm_gradient: float32 [2, 4, 2048, 128], P(None, 'lat', 'lon')
Inputs may be any that keep to these rules, and one draw needn't show every extreme that they name: margins[0, i, j, k, s] is a top-level block of ocean tile (i, k), or -1 where slot s from longitude tile j to longitude tile k in latitude row i is empty; margins[1] is an atmosphere block of tile (i, j) and margins[2] a weight block in every slot. Live slots lie anywhere among the 64. In each latitude row one receiving tile has all 64 slots live from every sender.
All inputs are finite; a program needn't handle non-finite values. No bound on the sum of `land_mask` on one device may be relied on, other than what follows from the above.
Results may differ from a plain program's by a relative error of at most 0.0003.
Values sent between devices are 32-bit elements; how exact they have to be, the bound alone decides.
No kernel may reach another device: no remote copies, remote signals or barrier semaphores. Data moves between devices by JAX's collectives and lax.ppermute only.
A program may use at most 64 MiB of HBM per device.

v0:
```python
import jax
import jax.numpy as jnp
from jax import lax
from jax.experimental import pallas as pl
from jax.experimental.pallas import tpu as pltpu
from jax.sharding import PartitionSpec as P

BLOCK = 128
STEPS = 4
HALO = STEPS
PER_LANES = BLOCK // HALO
GROUP = 8
f32 = jnp.float32
bf16 = jnp.bfloat16
VMEM_LIMIT = 32 * 1024 * 1024


def call(body, outs, scratch=(), flops=0, name=None, inputs=0, far=(), far_outs=(), aliases=None):
    outs = [s if isinstance(s, jax.ShapeDtypeStruct) else jax.ShapeDtypeStruct(s, f32) for s in outs]
    near = pl.BlockSpec(memory_space=pltpu.VMEM)
    aliases = aliases or {}
    kernel = pl.pallas_call(
        body,
        out_shape=outs,
        in_specs=[
            pl.BlockSpec(memory_space=pl.ANY)
            if n in aliases
            else pl.BlockSpec(memory_space=pltpu.HBM)
            if n in far
            else near
            for n in range(inputs)
        ],
        out_specs=[
            pl.BlockSpec(memory_space=pl.ANY) if n in aliases.values() or n in far_outs else near
            for n in range(len(outs))
        ],
        input_output_aliases=aliases,
        scratch_shapes=list(scratch),
        compiler_params=pltpu.CompilerParams(vmem_limit_bytes=VMEM_LIMIT),
        cost_estimate=pl.CostEstimate(flops=flops, bytes_accessed=1 << 20, transcendentals=0),
        name=name,
    )

    def run(*args):
        return kernel(
            *(pltpu.with_memory_space_constraint(x, pltpu.HBM) if n in far else x for n, x in enumerate(args))
        )

    return run


def lanes(shape):
    return lax.broadcasted_iota(jnp.int32, shape, len(shape) - 1)


def rows(shape):
    return lax.broadcasted_iota(jnp.int32, shape, len(shape) - 2)


def turn(x, shift, axis):
    shift %= x.shape[axis]
    return pltpu.roll(x, shift, axis) if shift else x


def swap(near, far, axis, wrap):
    count = lax.axis_size(axis)
    pairs = [[], []]
    for i in range(count if wrap else count - 1):
        j = (i + 1) % count
        pairs[i % 2] += [(i, j), (j, i)]
    far = lax.ppermute(far, axis, pairs[1])
    return lax.ppermute(near, axis, pairs[0]), far


def sort_swap(axis, after, before):
    odd = lax.rem(lax.axis_index(axis), 2) == 1
    return jnp.where(odd, before, after), jnp.where(odd, after, before)


def tile_fields(tracers, cotangent, land_mask, diffusion, velocity):
    levels = land_mask.shape[0]
    mask = [land_mask[level].astype(f32) for level in range(levels)]
    out = [tracers[f, level] for f in range(2) for level in range(levels)]
    out += [cotangent[f, level] for f in range(2) for level in range(levels)]
    out += [diffusion[0, level] * mask[level] for level in range(levels)]
    out += [velocity[0, level] * mask[level] for level in range(levels)]
    out += [diffusion[1, level] * mask[level] for level in range(levels)]
    out += [velocity[1, level] * mask[level] for level in range(levels)]
    out += [diffusion[2, level] * mask[level] * mask[level + 1] for level in range(levels - 1)]
    return out


def fetch(pairs, arrived):
    copies = [pltpu.make_async_copy(src, dst, arrived.at[n]) for n, (src, dst) in enumerate(pairs)]
    for copy in copies:
        copy.start()
    return copies


def pack_columns(*refs):
    inputs, (fields, near, far), scratch = refs[:7], refs[7:10], refs[12:]
    copies = fetch(zip(inputs, [*scratch[:5], *refs[10:12]]), scratch[5])
    for copy in copies[:5]:
        copy.wait()
    shape = near.shape[1:]
    lane = lanes(shape)
    west = [jnp.zeros(shape, f32) for _ in range(near.shape[0])]
    east = [jnp.zeros(shape, f32) for _ in range(near.shape[0])]
    for i, field in enumerate(tile_fields(*scratch[:5])):
        fields[i] = field
        part, at = divmod(i, PER_LANES)
        at *= HALO
        here = (lane >= at) & (lane < at + HALO)
        west[part] = jnp.where(here, turn(field[:, :BLOCK], at, 1), west[part])
        east[part] = jnp.where(here, turn(field[:, -BLOCK:], at + HALO, 1), east[part])
    for part in range(near.shape[0]):
        near[part], far[part] = sort_swap("lon", east[part], west[part])
    for copy in copies[5:]:
        copy.wait()


def unpack_columns(from_west, from_east, i):
    part, at = divmod(i, PER_LANES)
    at *= HALO
    lane = lanes(from_west[part].shape)
    east = turn(from_east[part], -at, 1)
    west = turn(from_west[part], -at - HALO, 1)
    return jnp.where(lane < HALO, east, jnp.where(lane >= BLOCK - HALO, west, 0.0))


def row_sources(fields, from_west, from_east):
    out = [(fields, (i, slice(None), slice(h * BLOCK, (h + 1) * BLOCK)))
           for i in range(fields.shape[0]) for h in range(fields.shape[2] // BLOCK)]
    for columns in (from_west, from_east):
        out += [(columns, (part,)) for part in range(columns.shape[0])]
    return out


def pack_rows(fields, near_columns, far_columns, sums, near, far, from_west, from_east, same_sums):
    for part in range(from_west.shape[0]):
        from_east[part], from_west[part] = sort_swap("lon", near_columns[part], far_columns[part])
    sources = [ref[at] for ref, at in row_sources(fields, from_west, from_east)]
    half = near.shape[0]
    row = rows((8, BLOCK))
    for i in range(half):
        first = sources[i]
        second = sources[i + half] if i + half < len(sources) else jnp.zeros_like(first)
        to_north = jnp.where(row < HALO, turn(first[-8:], HALO, 0), second[-8:])
        to_south = jnp.where(row < HALO, first[:8], turn(second[:8], HALO, 0))
        near[i], far[i] = sort_swap("lat", to_north, to_south)


def edge_rows(near, far, i):
    half = near.shape[0]
    from_north, from_south = sort_swap("lat", near[i % half], far[i % half])
    if i < half:
        from_south = turn(from_south, HALO, 0)
    else:
        from_north = turn(from_north, HALO, 0)
    return jnp.where(rows(from_north.shape) < HALO, from_north, from_south)


def widen(fields, from_west, from_east, near, far, wide):
    count, tile_lat, tile_lon = fields.shape
    halves = tile_lon // BLOCK
    parts = from_west.shape[0]
    corners = [edge_rows(near, far, count * halves + n) for n in range(2 * parts)]
    for i in range(count):
        wide[i, :tile_lat, :tile_lon] = fields[i]
        wide[i, :tile_lat, tile_lon:] = unpack_columns(from_west, from_east, i)
        for h in range(halves):
            wide[i, tile_lat:, h * BLOCK : (h + 1) * BLOCK] = edge_rows(near, far, i * halves + h)
        wide[i, tile_lat:, tile_lon:] = unpack_columns(corners[:parts], corners[parts:], i)


def eastward(x):
    return turn(x, -1, 1)


def westward(x):
    return turn(x, 1, 1)


def northward(x):
    return turn(x, -1, 0)


def southward(x):
    return turn(x, 1, 0)


def adjoint_step(coeffs, read, write):
    levels = coeffs.shape[1]
    above = None
    for level in range(levels):
        lam = read(level)
        step_x = eastward(lam) - lam
        step_y = northward(lam) - lam
        out = lam + coeffs[0, level] * step_x + westward(coeffs[1, level] * step_x)
        out = out + coeffs[2, level] * step_y + southward(coeffs[3, level] * step_y)
        if above is not None:
            out = out - above
        if level < levels - 1:
            above = coeffs[4, level] * (read(level + 1) - lam)
            out = out + above
        write(level, out)


def run_adjoint(
    fields, from_west, from_east, near, far, blocks, coeffs, start, lam_out, wide, state, own, sent
):
    levels = coeffs.shape[1]
    tile_lat, tile_lon = fields.shape[1:]
    halves = tile_lon // BLOCK
    widen(fields, from_west, from_east, near, far, wide)
    base = 4 * levels
    for f in range(2):
        for level in range(levels):
            start[f, level] = wide[f * levels + level]
    mask0 = None
    for level in range(levels):
        east_d, east_u = wide[base + level], wide[base + levels + level]
        north_d, north_u = wide[base + 2 * levels + level], wide[base + 3 * levels + level]
        mask = (east_d > 0.0).astype(f32)
        mask0 = mask if mask0 is None else mask0
        mask_e, mask_n = eastward(mask), northward(mask)
        east_k, east_v = east_d * mask_e, east_u * mask_e
        north_k, north_v = north_d * mask_n, north_u * mask_n
        coeffs[0, level] = jnp.maximum(east_v, 0.0) + east_k
        coeffs[1, level] = jnp.minimum(east_v, 0.0) - east_k
        coeffs[2, level] = jnp.maximum(north_v, 0.0) + north_k
        coeffs[3, level] = jnp.minimum(north_v, 0.0) - north_k
        coeffs[4, level] = wide[base + 4 * levels + level] if level < levels - 1 else jnp.zeros_like(mask)
        coeffs[5, level] = mask
    copies = []
    for f in range(2):
        surface = wide[(2 + f) * levels, :tile_lat, :tile_lon]
        for step in range(STEPS - 1):
            def read(level):
                return wide[(2 + f) * levels + level] if step == 0 else state[(step - 1) % 2, level]

            def write(level, lam):
                nonlocal surface
                if level == 0:
                    surface = surface + lam[:tile_lat, :tile_lon]
                if step == STEPS - 2:
                    lam_out[f, level] = lam
                else:
                    state[step % 2, level] = lam

            adjoint_step(coeffs, read, write)
        surface = surface * mask0[:tile_lat, :tile_lon]
        for h in range(halves):
            at = (f * halves + h) * tile_lat
            own[at : at + tile_lat] = surface[:, h * BLOCK : (h + 1) * BLOCK]
        field = pl.ds(f * halves * tile_lat, halves * tile_lat)
        copies += fetch([(own.at[field], blocks.at[k, field]) for k in range(blocks.shape[0])], sent.at[f])
    for copy in copies:
        copy.wait()


def sum_forcing(received, forcing, near, far):
    tile_lat = forcing.shape[1]
    halves = forcing.shape[2] // BLOCK - 1
    total = received[0]
    for j in range(1, received.shape[0]):
        total = total + received[j]
    lane = lanes((tile_lat, BLOCK))
    upper = total[2 * halves * tile_lat :]
    lower = jnp.where(lane[: tile_lat // 2] < BLOCK // 2, turn(upper, -2 * HALO, 1), turn(upper, 2 * HALO, 1))
    packed = jnp.concatenate([upper, lower], axis=0)
    for f in range(2):
        for h in range(halves):
            at = (f * halves + h) * tile_lat
            forcing[f, :, h * BLOCK : (h + 1) * BLOCK] = total[at : at + tile_lat]
        used = (lane < HALO) | (lane >= BLOCK - HALO)
        if f == 0:
            edge = packed
        else:
            edge = jnp.where(lane < HALO, turn(packed, -HALO, 1), turn(packed, HALO, 1))
        forcing[f, :, halves * BLOCK :] = jnp.where(used, edge, 0.0)
    row = rows((8, forcing.shape[2]))
    to_north = jnp.where(row < HALO, turn(forcing[0, tile_lat - 8 :], HALO, 0), forcing[1, tile_lat - 8 :])
    to_south = jnp.where(row < HALO, forcing[0, :8], turn(forcing[1, :8], HALO, 0))
    near[0], far[0] = sort_swap("lat", to_north, to_south)


def run_forward(coeffs, start, lam, forcing, near, far, final, adjoint_out, state):
    levels = coeffs.shape[1]
    tile_lat, tile_lon = final.shape[2:]
    for f in range(2):

        def write(level, out):
            adjoint_out[f, level] = out[:tile_lat, :tile_lon]

        adjoint_step(coeffs, lambda level: lam[f, level], write)
        force = jnp.concatenate([forcing[f], edge_rows(near, far, f)], axis=0)
        force = force * coeffs[5, 0]
        for step in range(STEPS):
            above = None
            for level in range(levels):
                read = (lambda n: start[f, n]) if step == 0 else (lambda n: state[(step - 1) % 2, n])
                theta = read(level)
                east_flux = coeffs[0, level] * theta + coeffs[1, level] * eastward(theta)
                north_flux = coeffs[2, level] * theta + coeffs[3, level] * northward(theta)
                out = theta - (east_flux - westward(east_flux)) - (north_flux - southward(north_flux))
                if level < levels - 1:
                    vertical = coeffs[4, level] * (theta - read(level + 1))
                    out = out - vertical
                if above is not None:
                    out = out + above
                above = vertical if level < levels - 1 else None
                if level == 0:
                    out = out + force
                if step == STEPS - 1:
                    final[f, level] = out[:tile_lat, :tile_lon]
                else:
                    state[step % 2, level] = out


def split(x):
    high = x.astype(bf16)
    return high, (x - high.astype(f32)).astype(bf16)


def weight_copies(weights, held, arrived):
    for g in range(held.shape[0]):
        yield pltpu.make_async_copy(weights.at[pl.ds(g * GROUP, GROUP)], held.at[g], arrived.at[g])


def fetch_weights(weights, held, arrived):
    for copy in weight_copies(weights, held, arrived):
        copy.start()


def held_part(weights, held, arrived):
    def part(r, g, u):
        if u == 0:

            @pl.when(r == 0)
            def _():
                pltpu.make_async_copy(weights.at[pl.ds(g * GROUP, GROUP)], held.at[g], arrived.at[g]).wait()

        return split(held[g, u])

    return part


def one_hot(where):
    return jnp.where(where, 1.0, 0.0).astype(bf16)


def places(slots, blocks):
    return 8 * (-(-2 * slots // (8 * blocks)) + 1)


def as_row(ids):
    return jnp.concatenate([ids[k : k + 1, :] for k in range(ids.shape[0])], axis=1)


def rank_slots(block_row, blocks):
    slots = block_row.shape[1]
    mine = rows((blocks, slots)) == block_row
    upper = one_hot(rows((slots, slots)) < lanes((slots, slots)))
    before = jnp.dot(one_hot(mine), upper, preferred_element_type=f32)
    return jnp.sum(jnp.where(mine, before, 0.0), axis=0, keepdims=True)


def find_slots(r, code, block_row, rank, capacity, column):
    slots = block_row.shape[1]
    place = rank.astype(jnp.int32) - r * capacity
    place = jnp.where((place >= 0) & (place < capacity), block_row * capacity + place, -1)
    for at in range(0, column.shape[0], BLOCK):
        here = rows((BLOCK, slots)) + at == place
        found = jnp.sum(jnp.where(here, code + 1.0, 0.0), axis=1, keepdims=True) - 1.0
        column[at : at + BLOCK] = jnp.broadcast_to(found, (BLOCK, BLOCK))


def couple(blocks, part, table, size, capacity, rounds, prepare, column, gather_first, transposed, result, scratch):
    vectors, products = scratch
    total_rows = column.shape[0]
    result[...] = jnp.zeros_like(result)

    def one_round(r, carry):
        prepare(r)
        eye = rows((BLOCK, BLOCK)) == lanes((BLOCK, BLOCK))
        place_hot = []
        for at in range(0, total_rows, BLOCK):
            found = column[at : at + BLOCK]
            first = jnp.floor((found + 0.5) * (1.0 / size))
            second = found - first * size
            gather, put = (first, second) if gather_first else (second, first)
            width = table.shape[0]
            gather = jnp.concatenate([gather] * (width // BLOCK), axis=1)
            hot = one_hot(gather == lanes((BLOCK, width)).astype(f32))
            vectors[at : at + BLOCK] = jnp.dot(hot, table, preferred_element_type=f32)
            put = jnp.sum(jnp.where(eye, put, 0.0), axis=0, keepdims=True)
            place_hot.append(one_hot(rows((result.shape[0], BLOCK)).astype(f32) == put))

        def group(g, carry):
            for u in range(GROUP):
                at = pl.multiple_of((g * GROUP + u) * capacity, 8)
                own = vectors[pl.ds(at, capacity)]
                left = jnp.concatenate([own[:, n * BLOCK : (n + 1) * BLOCK] for n in range(4)], axis=0)
                high, low = part(r, g, u)
                right = jnp.concatenate([high, low], axis=1 if transposed else 0)
                contract = (((1,), (0 if transposed else 1,)), ((), ()))
                product = lax.dot_general(left.astype(bf16), right, contract, preferred_element_type=f32)
                for f in range(2):
                    high_part = product[f * capacity : (f + 1) * capacity]
                    low_part = product[(f + 2) * capacity : (f + 3) * capacity, :BLOCK]
                    products[pl.ds(at, capacity), f * BLOCK : (f + 1) * BLOCK] = (
                        high_part[:, BLOCK:] + low_part
                    ) + high_part[:, :BLOCK]
            return carry

        lax.fori_loop(0, blocks // GROUP, group, 0)
        summed = jnp.dot(
            jnp.concatenate(place_hot, axis=1),
            jnp.concatenate(split(products[...]), axis=1),
            preferred_element_type=f32,
        )
        result[...] += summed[:, : 2 * BLOCK] + summed[:, 2 * BLOCK :]
        return carry

    lax.fori_loop(0, rounds, one_round, 0)


def slot_keys(ids, tile_lat, atm):
    lon_count, cap = ids.shape[3:]
    ocean, atm_ids, block_ids = (ids[n, 0, 0] for n in range(3))
    order = (ocean & 1) * tile_lat + (ocean >> 1) + rows((lon_count, cap)) * (2 * tile_lat)
    order = jnp.where(ocean >= 0, order, lon_count * 2 * tile_lat)
    return as_row((order * atm + atm_ids).astype(f32)), as_row(block_ids)


def weigh(atm_near, margins, weights, after, sums, found, keys, result, *scratch):
    scratch, (held, arrived) = scratch[:2], scratch[2:]
    fetch_weights(weights, held, arrived)
    lon_count = margins.shape[3]
    atm = atm_near.shape[2]
    blocks = weights.shape[0]
    tile_lat = 2 * sums.shape[1] // 9
    code, block_row = slot_keys(margins, tile_lat, atm)
    rank = rank_slots(block_row, blocks)
    keys[0:1] = code
    keys[1:2] = block_row.astype(f32)
    keys[2:3] = rank
    capacity = places(code.shape[1], blocks)
    rounds = jnp.max(rank).astype(jnp.int32) // capacity + 1
    parts = [split(atm_near[f, 0]) for f in range(2)]
    table = jnp.concatenate([parts[f][n] for n in range(2) for f in range(2)], axis=1)

    def prepare(r):
        find_slots(rounds - 1 - r, code, block_row, rank, capacity, found)

    part = held_part(weights, held, arrived)
    couple(blocks, part, table, atm, capacity, rounds, prepare, found, False, False, result, scratch)
    lane = lanes((tile_lat, BLOCK))

    def block_sums(k, f, h):
        at = (2 * k + h) * tile_lat
        return result[at : at + tile_lat, f * BLOCK : (f + 1) * BLOCK]

    for k in range(lon_count):
        edge = jnp.zeros((tile_lat, BLOCK), f32)
        for f in range(2):
            for h in range(2):
                sums[k, (2 * f + h) * tile_lat : (2 * f + h + 1) * tile_lat] = block_sums(k, f, h)
            at = f * HALO
            after = turn(block_sums((k + 1) % lon_count, f, 0), at, 1)
            before = turn(block_sums((k - 1) % lon_count, f, 1), -at, 1)
            edge = jnp.where((lane >= at) & (lane < at + HALO), after, edge)
            end = BLOCK - at
            edge = jnp.where((lane >= end - HALO) & (lane < end), before, edge)
        upper, lower = edge[: tile_lat // 2], edge[tile_lat // 2 :]
        near = lane[: tile_lat // 2]
        lower = jnp.where(near < BLOCK // 2, turn(lower, 2 * HALO, 1), turn(lower, -2 * HALO, 1))
        sums[k, 4 * tile_lat :] = jnp.where((near < 2 * HALO) | (near >= BLOCK - 2 * HALO), upper, lower)


def unweigh(gathered, found, keys, weights, gradient, result, column, *scratch):
    scratch, (held, arrived) = scratch[:2], scratch[2:]
    fetch_weights(weights, held, arrived)
    atm = gradient.shape[2]
    blocks = weights.shape[0]
    lon_count, ocean_blocks = gathered.shape[0], gathered.shape[1] // 2
    capacity = places(keys.shape[1], blocks)
    rounds = jnp.max(keys[2:3]).astype(jnp.int32) // capacity + 1
    parts = [
        split(
            jnp.concatenate(
                [gathered[k, f * ocean_blocks : (f + 1) * ocean_blocks] for k in range(lon_count)], axis=0
            )
        )
        for f in range(2)
    ]
    table = jnp.concatenate([parts[f][n] for n in range(2) for f in range(2)], axis=1)

    def prepare(r):
        @pl.when(r == 0)
        def _():
            column[...] = found[...]

        @pl.when(r > 0)
        def _():
            find_slots(r, keys[0:1], keys[1:2].astype(jnp.int32), keys[2:3], capacity, column)

    couple(
        blocks,
        held_part(weights, held, arrived),
        table,
        atm,
        capacity,
        rounds,
        prepare,
        column,
        True,
        True,
        result,
        scratch,
    )
    for f in range(2):
        gradient[f, 0] = result[:, f * BLOCK : (f + 1) * BLOCK]


def on_device(tracers, cotangent, land_mask, diffusion, velocity, weights, atm_state, margins):
    levels, tile_lat, tile_lon = land_mask.shape
    lon_count = lax.axis_size("lon")
    slots = lon_count * margins.shape[4]
    halves = tile_lon // BLOCK
    count = 9 * levels - 1
    parts = -(-count // PER_LANES)
    inputs = (tracers, cotangent, land_mask, diffusion, velocity)

    def in_vmem(s):
        return pltpu.VMEM(s.shape, s.dtype)

    message = (parts, tile_lat, BLOCK)
    fields, near, far, atm_near, margins_near = call(
        pack_columns,
        [
            (count, tile_lat, tile_lon),
            message,
            message,
            atm_state.shape,
            jax.ShapeDtypeStruct(margins.shape, margins.dtype),
        ],
        [*map(in_vmem, inputs), pltpu.SemaphoreType.DMA((7,))],
        name="pack_columns",
        inputs=7,
        far=range(7),
    )(*inputs, atm_state, margins)
    near_columns, far_columns = swap(near, far, "lon", True)

    blocks_of, atm = weights.shape[0], atm_state.shape[2]
    groups = blocks_of // GROUP
    sum_rows = 2 * halves * tile_lat + tile_lat // 2
    ocean_blocks = lon_count * halves * tile_lat
    held_rows = -(-places(slots, blocks_of) * blocks_of // BLOCK) * BLOCK

    def coupling_scratch(result_rows):
        return [
            pltpu.VMEM((result_rows, 2 * BLOCK), f32),
            pltpu.VMEM((held_rows, 4 * BLOCK), f32),
            pltpu.VMEM((held_rows, 2 * BLOCK), f32),
            pltpu.VMEM((groups, GROUP, BLOCK, BLOCK), f32),
            pltpu.SemaphoreType.DMA((groups,)),
        ]

    coupling_flops = 4 * slots * blocks_of * 2 * BLOCK * BLOCK * 2
    sums, found, keys = call(
        weigh,
        [(lon_count, sum_rows, BLOCK), (held_rows, BLOCK), (8, slots)],
        coupling_scratch(ocean_blocks),
        coupling_flops,
        name="weigh",
        inputs=4,
        far=(2,),
    )(atm_near, margins_near, weights, near)

    sources = count * halves + 2 * parts
    message = (-(-sources // 2), 8, BLOCK)
    columns = (parts, tile_lat, BLOCK)
    near, far, from_west, from_east, sums = call(
        pack_rows,
        [message, message, columns, columns, sums.shape],
        name="pack_rows",
        inputs=4,
        aliases={3: 4},
    )(fields, near_columns, far_columns, sums)
    received = lax.all_to_all(sums, "lon", split_axis=0, concat_axis=0, tiled=True)
    near_rows, far_rows = swap(near, far, "lat", False)

    wide = (tile_lat + 8, tile_lon + BLOCK)
    own = (2 * halves * tile_lat, BLOCK)
    blocks, coeffs, start, lam = call(
        run_adjoint,
        [(lon_count, *own), (6, levels, *wide), (2, levels, *wide), (2, levels, *wide)],
        [
            pltpu.VMEM((count, *wide), f32),
            pltpu.VMEM((2, levels, *wide), f32),
            pltpu.VMEM(own, f32),
            pltpu.SemaphoreType.DMA((2, lon_count)),
        ],
        name="run_adjoint",
        inputs=5,
        far_outs=(0,),
    )(fields, from_west, from_east, near_rows, far_rows)
    gathered = lax.all_to_all(blocks, "lon", split_axis=0, concat_axis=0, tiled=True)

    message = (1, 8, tile_lon + BLOCK)
    forcing, near, far = call(
        sum_forcing, [(2, tile_lat, tile_lon + BLOCK), message, message], name="sum_forcing", inputs=1
    )(received)
    near_rows, far_rows = swap(near, far, "lat", False)
    final, adjoint = call(
        run_forward,
        [tracers.shape, cotangent.shape],
        [pltpu.VMEM((2, levels, *wide), f32)],
        name="run_forward",
        inputs=6,
    )(coeffs, start, lam, forcing, near_rows, far_rows)

    (gradient,) = call(
        unweigh,
        [atm_state.shape],
        [coupling_scratch(atm)[0], in_vmem(found), *coupling_scratch(atm)[1:]],
        coupling_flops,
        name="unweigh",
        inputs=4,
        far=(3,),
    )(gathered, found, keys, weights)
    return (final, adjoint, gradient)


def solution(mesh):
    return jax.shard_map(
        on_device,
        mesh=mesh,
        in_specs=(
            P(None, None, "lat", "lon"),
            P(None, None, "lat", "lon"),
            P(None, "lat", "lon"),
            P(None, None, "lat", "lon"),
            P(None, None, "lat", "lon"),
            P(),
            P(None, "lat", "lon", None),
            P(None, "lat", "lon", None, None),
        ),
        out_specs=(
            P(None, None, "lat", "lon"),
            P(None, None, "lat", "lon"),
            P(None, "lat", "lon", None),
        ),
        check_vma=False,
    )
```

profile of v0, /device:TPU:1, one launch (start us, length us, event | category | flops | bytes accessed | tf_op | source)
XLA Modules:
  0.0 42.1 jit_solution(3058498834242545125)
XLA Ops:
  0.6 1.4 %pack_columns.1 = (f32[35,16,256]{2,1,0:T(8,128)S(1)}, f32[2,16,128]{2,1,0:T(8,128)S(1)}, f32[2,16,128]{2,1,0:T(8,128)S(1)}, f32[2,1,256,128]{3,2,1,0:T(8,128)S(1)}, s32[3,1,1,8,64]{4,3,2,1,0:T(8,128)S(1)}) custom-call(f32[2,4,16,256]{3,2,1,0:T(8,128)} %refs_0_.1, f32[2,4,16,256]{3,2,1,0:T(8,128)} %refs_1_.1, s32[4,16,256]{2,1,0:T(8,128)} %refs_2_.1, ...), custom_call_target="tpu_custom_call" | custom-call | bytes 1048576 | tf_op jit(solution)/shard_map/pack_columns/pallas_call | solution.py:45
  2.1 5.1 %collective-permute-start.1 = (f32[2,16,128]{2,1,0:T(8,128)S(1)}, f32[2,16,128]{2,1,0:T(8,128)S(1)}, u32[]{:S(2)}, u32[]{:S(2)}) collective-permute-start(f32[2,16,128]{2,1,0:T(8,128)S(1)} %get-tuple-element.27), channel_id=1, source_target_pairs={{1,2},{2,1},{3,4},{4,3},{5,6},{6,5},{7,0},{0,7},{9,10},{10,9},{11,... | collective-permute-start | bytes 49160 | tf_op jit(solution)/shard_map/ppermute | solution.py:71
  7.2 0.0 collective-permute-start
  7.2 4.0 %weigh.1 = (f32[8,72,128]{2,1,0:T(8,128)}, f32[1280,128]{1,0:T(8,128)S(1)}, f32[8,512]{1,0:T(8,128)S(1)}) custom-call(f32[2,1,256,128]{3,2,1,0:T(8,128)S(1)} %get-tuple-element.28.atm_near, s32[3,1,1,8,64]{4,3,2,1,0:T(8,128)S(1)} %get-tuple-element.29.margins, f32[32,128,128]{2,1,0:T(8,128)} %weights.3, f32[2,16,128]{2,1,0:T(8,128)S(1)} %get-tuple-element.26.after), custom_call_target="tpu_custom_call" | custom-call | flops 4294967296 | bytes 1048576 | tf_op jit(solution)/shard_map/weigh/pallas_call | solution.py:45
  11.3 0.0 collective-permute-done.1.far_columns
  11.3 0.0 collective-permute-done.near_columns
  11.3 3.4 %all-to-all-start = ((f32[8,72,128]{2,1,0:T(8,128)}), f32[8,72,128]{2,1,0:T(8,128)S(1)}, u32[]{:S(2)}, u32[]{:S(2)}) async-start(f32[8,72,128]{2,1,0:T(8,128)} %get-tuple-element.38), calls=%async_computation | async-start | bytes 589824 | tf_op jit(solution)/shard_map/all_to_all | solution.py:592
  14.8 1.2 %collective-permute-start.2 = (f32[37,8,128]{2,1,0:T(8,128)S(1)}, f32[37,8,128]{2,1,0:T(8,128)S(1)}, u32[]{:S(2)}, u32[]{:S(2)}) collective-permute-start(f32[37,8,128]{2,1,0:T(8,128)S(1)} %get-tuple-element.33), channel_id=1, source_target_pairs={{0,8},{8,0},{16,24},{24,16},{1,9},{9,1},{17,25},{25,17},{2,10},{10... | collective-permute-start | bytes 454664 | tf_op jit(solution)/shard_map/ppermute | solution.py:72
  16.0 3.0 %collective-permute-start.3 = (f32[37,8,128]{2,1,0:T(8,128)S(1)}, f32[37,8,128]{2,1,0:T(8,128)S(1)}, u32[]{:S(2)}, u32[]{:S(2)}) collective-permute-start(f32[37,8,128]{2,1,0:T(8,128)S(1)} %get-tuple-element.34), channel_id=1, source_target_pairs={{8,16},{16,8},{9,17},{17,9},{10,18},{18,10},{11,19},{19,11},{12,20... | collective-permute-start | bytes 454664 | tf_op jit(solution)/shard_map/ppermute | solution.py:71
  19.0 0.0 collective-permute-done.2.near
  19.0 3.7 %collective-permute-done.3.far = f32[37,8,128]{2,1,0:T(8,128)S(1)} collective-permute-done((f32[37,8,128]{2,1,0:T(8,128)S(1)}, f32[37,8,128]{2,1,0:T(8,128)S(1)}, u32[]{:S(2)}, u32[]{:S(2)}) %collective-permute-start.3) | collective-permute-done | bytes 151584 | tf_op jit(solution)/shard_map/ppermute | solution.py:71
  22.7 2.3 %run_adjoint.1 = (f32[8,64,128]{2,1,0:T(8,128)}, f32[6,4,24,384]{3,2,1,0:T(8,128)S(1)}, f32[2,4,24,384]{3,2,1,0:T(8,128)S(1)}, f32[2,4,24,384]{3,2,1,0:T(8,128)S(1)}) custom-call(f32[35,16,256]{2,1,0:T(8,128)S(1)} %get-tuple-element.25.fields, f32[2,16,128]{2,1,0:T(8,128)S(1)} %get-tuple-element.31.from_west, f32[2,16,128]{2,1,0:T(8,128)S(1)} %get-tuple-element.32.from_east, ...), custom_call_target="tpu_custom_call" | custom-call | bytes 1048576 | tf_op jit(solution)/shard_map/run_adjoint/pallas_call | solution.py:45
  25.1 0.0 all-to-all-done.received
  25.1 5.4 %all-to-all-start.1 = ((f32[8,64,128]{2,1,0:T(8,128)}), f32[8,64,128]{2,1,0:T(8,128)S(1)}, u32[]{:S(2)}, u32[]{:S(2)}) async-start(f32[8,64,128]{2,1,0:T(8,128)} %get-tuple-element.44), calls=%async_computation.1 | async-start | bytes 524288 | tf_op jit(solution)/shard_map/all_to_all | solution.py:610
  30.5 0.1 sum_forcing.1
  30.7 0.0 collective-permute-start.4
  30.7 3.3 %collective-permute-start.5 = (f32[1,8,384]{2,1,0:T(8,128)S(1)}, f32[1,8,384]{2,1,0:T(8,128)S(1)}, u32[]{:S(2)}, u32[]{:S(2)}) collective-permute-start(f32[1,8,384]{2,1,0:T(8,128)S(1)} %get-tuple-element.41), channel_id=1, source_target_pairs={{8,16},{16,8},{9,17},{17,9},{10,18},{18,10},{11,19},{19,11},{12,20... | collective-permute-start | bytes 36872 | tf_op jit(solution)/shard_map/ppermute | solution.py:71
  34.0 0.0 collective-permute-done.4.near
  34.0 2.0 %collective-permute-done.5.far = f32[1,8,384]{2,1,0:T(8,128)S(1)} collective-permute-done((f32[1,8,384]{2,1,0:T(8,128)S(1)}, f32[1,8,384]{2,1,0:T(8,128)S(1)}, u32[]{:S(2)}, u32[]{:S(2)}) %collective-permute-start.5) | collective-permute-done | bytes 12320 | tf_op jit(solution)/shard_map/ppermute | solution.py:71
  36.0 2.1 %run_forward.1 = (f32[2,4,16,256]{3,2,1,0:T(8,128)}, f32[2,4,16,256]{3,2,1,0:T(8,128)}) custom-call(f32[6,4,24,384]{3,2,1,0:T(8,128)S(1)} %get-tuple-element.35.coeffs, f32[2,4,24,384]{3,2,1,0:T(8,128)S(1)} %get-tuple-element.36.start, f32[2,4,24,384]{3,2,1,0:T(8,128)S(1)} %get-tuple-element.37.lam, f32[2,16,384]{2,1,0:T(8,128)S(1)} %get-tuple-element.39.forcing, ...), custom_call_target="tpu_custom_call" | custom-call | bytes 1048576 | tf_op jit(solution)/shard_map/run_forward/pallas_call | solution.py:45
  38.1 0.4 all-to-all-done.1.gathered
  38.5 3.6 %unweigh.1 = f32[2,1,256,128]{3,2,1,0:T(8,128)} custom-call(f32[8,64,128]{2,1,0:T(8,128)S(1)} %all-to-all-done.1.gathered, f32[1280,128]{1,0:T(8,128)S(1)} %get-tuple-element.45.found, f32[8,512]{1,0:T(8,128)S(1)} %get-tuple-element.46.keys, f32[32,128,128]{2,1,0:T(8,128)} %weights.3), custom_call_target="tpu_custom_call" | custom-call | flops 4294967296 | bytes 1048576 | tf_op jit(solution)/shard_map/unweigh/pallas_call | solution.py:45
  (1 shorter events, 0.0 us)
Async XLA Ops:
  2.1 9.2 %collective-permute-start.1 = (f32[2,16,128]{2,1,0:T(8,128)S(1)}, f32[2,16,128]{2,1,0:T(8,128)S(1)}, u32[]{:S(2)}, u32[]{:S(2)}) collective-permute-start(f32[2,16,128]{2,1,0:T(8,128)S(1)} %get-tuple-element.27), channel_id=1, source_target_pairs={{1,2},{2,1},{3,4},{4,3},{5,6},{6,5},{7,0},{0,7},{9,10},{10,9},{11,... | collective-permute-start | bytes 49160 | tf_op jit(solution)/shard_map/ppermute | solution.py:71
  7.2 4.0 %collective-permute-start = (f32[2,16,128]{2,1,0:T(8,128)S(1)}, f32[2,16,128]{2,1,0:T(8,128)S(1)}, u32[]{:S(2)}, u32[]{:S(2)}) collective-permute-start(f32[2,16,128]{2,1,0:T(8,128)S(1)} %get-tuple-element.26.after), channel_id=1, source_target_pairs={{0,1},{1,0},{2,3},{3,2},{4,5},{5,4},{6,7},{7,6},{8,9},{9,8},{10,11... | collective-permute-start | bytes 49160 | tf_op jit(solution)/shard_map/ppermute | solution.py:72
  11.3 13.8 %all-to-all-start = ((f32[8,72,128]{2,1,0:T(8,128)}), f32[8,72,128]{2,1,0:T(8,128)S(1)}, u32[]{:S(2)}, u32[]{:S(2)}) async-start(f32[8,72,128]{2,1,0:T(8,128)} %get-tuple-element.38), calls=%async_computation | async-start | bytes 589824 | tf_op jit(solution)/shard_map/all_to_all | solution.py:592
  14.8 4.2 %collective-permute-start.2 = (f32[37,8,128]{2,1,0:T(8,128)S(1)}, f32[37,8,128]{2,1,0:T(8,128)S(1)}, u32[]{:S(2)}, u32[]{:S(2)}) collective-permute-start(f32[37,8,128]{2,1,0:T(8,128)S(1)} %get-tuple-element.33), channel_id=1, source_target_pairs={{0,8},{8,0},{16,24},{24,16},{1,9},{9,1},{17,25},{25,17},{2,10},{10... | collective-permute-start | bytes 454664 | tf_op jit(solution)/shard_map/ppermute | solution.py:72
  16.0 6.8 %collective-permute-start.3 = (f32[37,8,128]{2,1,0:T(8,128)S(1)}, f32[37,8,128]{2,1,0:T(8,128)S(1)}, u32[]{:S(2)}, u32[]{:S(2)}) collective-permute-start(f32[37,8,128]{2,1,0:T(8,128)S(1)} %get-tuple-element.34), channel_id=1, source_target_pairs={{8,16},{16,8},{9,17},{17,9},{10,18},{18,10},{11,19},{19,11},{12,20... | collective-permute-start | bytes 454664 | tf_op jit(solution)/shard_map/ppermute | solution.py:71
  25.1 13.4 %all-to-all-start.1 = ((f32[8,64,128]{2,1,0:T(8,128)}), f32[8,64,128]{2,1,0:T(8,128)S(1)}, u32[]{:S(2)}, u32[]{:S(2)}) async-start(f32[8,64,128]{2,1,0:T(8,128)} %get-tuple-element.44), calls=%async_computation.1 | async-start | bytes 524288 | tf_op jit(solution)/shard_map/all_to_all | solution.py:610
  30.7 3.3 %collective-permute-start.4 = (f32[1,8,384]{2,1,0:T(8,128)S(1)}, f32[1,8,384]{2,1,0:T(8,128)S(1)}, u32[]{:S(2)}, u32[]{:S(2)}) collective-permute-start(f32[1,8,384]{2,1,0:T(8,128)S(1)} %get-tuple-element.40), channel_id=1, source_target_pairs={{0,8},{8,0},{16,24},{24,16},{1,9},{9,1},{17,25},{25,17},{2,10},{10... | collective-permute-start | bytes 36872 | tf_op jit(solution)/shard_map/ppermute | solution.py:72
  30.7 5.3 %collective-permute-start.5 = (f32[1,8,384]{2,1,0:T(8,128)S(1)}, f32[1,8,384]{2,1,0:T(8,128)S(1)}, u32[]{:S(2)}, u32[]{:S(2)}) collective-permute-start(f32[1,8,384]{2,1,0:T(8,128)S(1)} %get-tuple-element.41), channel_id=1, source_target_pairs={{8,16},{16,8},{9,17},{17,9},{10,18},{18,10},{11,19},{19,11},{12,20... | collective-permute-start | bytes 36872 | tf_op jit(solution)/shard_map/ppermute | solution.py:71
where the time goes:
time: 42.5 us; the launch traced here: 42.1 us
  starting transfers between devices  21.6 us (51%)
  Pallas kernels  13.7 us (32%)
  waiting for transfers between devices  6.09 us (14%)
  between operations  0.73 us (2%)
    pallas_call x7, Pallas kernels, run(): kernel(*(pltpu.with_memory_space_constraint(x, pltpu.HBM) if n in far els...  13.7 us
    ppermute x3, starting transfers between devices, swap(): far = lax.ppermute(far, axis, pairs[1])  11.5 us
    ppermute x3, waiting for transfers between devices, swap(): far = lax.ppermute(far, axis, pairs[1])  5.71 us
    all_to_all x1, starting transfers between devices, on_device(): lax.all_to_all(blocks, 'lon', split_axis=0, concat_axis=0, tiled=True)  5.43 us
    all_to_all x1, starting transfers between devices, on_device(): lax.all_to_all(sums, 'lon', split_axis=0, concat_axis=0, tiled=True)  3.43 us
    ppermute x3, starting transfers between devices, swap(): return (lax.ppermute(near, axis, pairs[0]), far)  1.19 us
  transfers between devices with their start and end apart: 8, of which 3 were waited for; matrix products, arithmetic and copies ran while one was open for 0% of the time, Pallas kernels for 20%

commit v1 on v0

--- a/solution.py
+++ b/solution.py
@@ -207,7 +207,7 @@
 
 
 def run_adjoint(
-    fields, from_west, from_east, near, far, blocks, coeffs, start, lam_out, wide, state, own, sent
+    fields, from_west, from_east, far, near, blocks, coeffs, start, lam_out, wide, state, own, sent
 ):
     levels = coeffs.shape[1]
     tile_lat, tile_lon = fields.shape[1:]
@@ -285,7 +285,7 @@
     near[0], far[0] = sort_swap("lat", to_north, to_south)
 
 
-def run_forward(coeffs, start, lam, forcing, near, far, final, adjoint_out, state):
+def run_forward(coeffs, start, lam, forcing, far, near, final, adjoint_out, state):
     levels = coeffs.shape[1]
     tile_lat, tile_lon = final.shape[2:]
     for f in range(2):
@@ -361,19 +361,37 @@
 def rank_slots(block_row, blocks):
     slots = block_row.shape[1]
     mine = rows((blocks, slots)) == block_row
-    upper = one_hot(rows((slots, slots)) < lanes((slots, slots)))
-    before = jnp.dot(one_hot(mine), upper, preferred_element_type=f32)
-    return jnp.sum(jnp.where(mine, before, 0.0), axis=0, keepdims=True)
-
-
-def find_slots(r, code, block_row, rank, capacity, column):
+    cuts = range(0, slots, BLOCK)
+    stacked = jnp.concatenate([one_hot(mine[:, at : at + BLOCK]) for at in cuts], axis=0)
+    shape = (BLOCK, 2 * BLOCK)
+    counts = jnp.dot(stacked, one_hot(rows(shape) < lanes(shape)), preferred_element_type=f32)
+    before, out = jnp.zeros((blocks, BLOCK), f32), []
+    for n, at in enumerate(cuts):
+        run = counts[n * blocks : (n + 1) * blocks]
+        here = jnp.where(mine[:, at : at + BLOCK], run[:, :BLOCK] + before, 0.0)
+        out.append(jnp.sum(here, axis=0, keepdims=True))
+        before = before + run[:, BLOCK:]
+    return jnp.concatenate(out, axis=1)
+
+
+def find_slots(r, code, block_row, rank, capacity, blocks, column):
     slots = block_row.shape[1]
-    place = rank.astype(jnp.int32) - r * capacity
-    place = jnp.where((place >= 0) & (place < capacity), block_row * capacity + place, -1)
-    for at in range(0, column.shape[0], BLOCK):
-        here = rows((BLOCK, slots)) + at == place
-        found = jnp.sum(jnp.where(here, code + 1.0, 0.0), axis=1, keepdims=True) - 1.0
-        column[at : at + BLOCK] = jnp.broadcast_to(found, (BLOCK, BLOCK))
+    mine = rows((blocks, slots)) == block_row
+    ranked = one_hot(rows((capacity, slots)) == rank.astype(jnp.int32) - r * capacity)
+    rest, found = code + 1.0, None
+    for base in (4096.0, 64.0, 1.0):
+        digit = jnp.floor(rest * (1.0 / base))
+        rest = rest - digit * base
+        part = lax.dot_general(
+            ranked,
+            jnp.where(mine, digit, 0.0).astype(bf16),
+            (((1,), (1,)), ((), ())),
+            preferred_element_type=f32,
+        )
+        found = part * base if found is None else found + part * base
+    found = found - 1.0
+    for w in range(blocks):
+        column[w * capacity : (w + 1) * capacity] = jnp.broadcast_to(found[:, w : w + 1], (capacity, BLOCK))
 
 
 def couple(blocks, part, table, size, capacity, rounds, prepare, column, gather_first, transposed, result, scratch):
@@ -452,7 +470,7 @@
     table = jnp.concatenate([parts[f][n] for n in range(2) for f in range(2)], axis=1)
 
     def prepare(r):
-        find_slots(rounds - 1 - r, code, block_row, rank, capacity, found)
+        find_slots(rounds - 1 - r, code, block_row, rank, capacity, blocks, found)
 
     part = held_part(weights, held, arrived)
     couple(blocks, part, table, atm, capacity, rounds, prepare, found, False, False, result, scratch)
@@ -504,7 +522,7 @@
 
         @pl.when(r > 0)
         def _():
-            find_slots(r, keys[0:1], keys[1:2].astype(jnp.int32), keys[2:3], capacity, column)
+            find_slots(r, keys[0:1], keys[1:2].astype(jnp.int32), keys[2:3], capacity, blocks, column)
 
     couple(
         blocks,
@@ -606,7 +624,7 @@
         name="run_adjoint",
         inputs=5,
         far_outs=(0,),
-    )(fields, from_west, from_east, near_rows, far_rows)
+    )(fields, from_west, from_east, far_rows, near_rows)
     gathered = lax.all_to_all(blocks, "lon", split_axis=0, concat_axis=0, tiled=True)
 
     message = (1, 8, tile_lon + BLOCK)
@@ -620,7 +638,7 @@
         [pltpu.VMEM((2, levels, *wide), f32)],
         name="run_forward",
         inputs=6,
-    )(coeffs, start, lam, forcing, near_rows, far_rows)
+    )(coeffs, start, lam, forcing, far_rows, near_rows)
 
     (gradient,) = call(
         unweigh,

time: 42.5 us -> 42.6 us (level)
  starting transfers between devices: 21.6 us -> 22.3 us
  waiting for transfers between devices: 6.09 us -> 5.48 us
    ppermute x3, starting transfers between devices: 11.5 us -> 13 us  [swap(): far = lax.ppermute(far, axis, pairs[1])]
    ppermute x3, starting transfers between devices: 1.19 us -> 0.14 us  [swap(): return (lax.ppermute(near, axis, pairs[0]), far)]
    ppermute x3, waiting for transfers between devices: 5.71 us -> 4.67 us  [swap(): far = lax.ppermute(far, axis, pairs[1])]
where the time goes in v1:
time: 42.6 us; the launch traced here: 42.2 us
  starting transfers between devices  22.3 us (52%)
  Pallas kernels  13.7 us (32%)
  waiting for transfers between devices  5.48 us (13%)
  between operations  0.73 us (2%)
    pallas_call x7, Pallas kernels, run(): kernel(*(pltpu.with_memory_space_constraint(x, pltpu.HBM) if n in far els...  13.7 us
    ppermute x3, starting transfers between devices, swap(): far = lax.ppermute(far, axis, pairs[1])  13 us
    all_to_all x1, starting transfers between devices, on_device(): lax.all_to_all(blocks, 'lon', split_axis=0, concat_axis=0, tiled=True)  5.73 us
    ppermute x3, waiting for transfers between devices, swap(): far = lax.ppermute(far, axis, pairs[1])  4.67 us
    all_to_all x1, starting transfers between devices, on_device(): lax.all_to_all(sums, 'lon', split_axis=0, concat_axis=0, tiled=True)  3.43 us
  transfers between devices with their start and end apart: 8, of which 3 were waited for; matrix products, arithmetic and copies ran while one was open for 0% of the time, Pallas kernels for 20%

profile of v1, /device:TPU:1, one launch (start us, length us, event | category | flops | bytes accessed | tf_op | source)
XLA Modules:
  0.0 42.2 jit_solution(4016109960309542241)
XLA Ops:
  0.6 1.4 %pack_columns.1 = (f32[35,16,256]{2,1,0:T(8,128)S(1)}, f32[2,16,128]{2,1,0:T(8,128)S(1)}, f32[2,16,128]{2,1,0:T(8,128)S(1)}, f32[2,1,256,128]{3,2,1,0:T(8,128)S(1)}, s32[3,1,1,8,64]{4,3,2,1,0:T(8,128)S(1)}) custom-call(f32[2,4,16,256]{3,2,1,0:T(8,128)} %refs_0_.1, f32[2,4,16,256]{3,2,1,0:T(8,128)} %refs_1_.1, s32[4,16,256]{2,1,0:T(8,128)} %refs_2_.1, ...), custom_call_target="tpu_custom_call" | custom-call | bytes 1048576 | tf_op jit(solution)/shard_map/pack_columns/pallas_call | solution.py:45
  2.1 5.1 %collective-permute-start.1 = (f32[2,16,128]{2,1,0:T(8,128)S(1)}, f32[2,16,128]{2,1,0:T(8,128)S(1)}, u32[]{:S(2)}, u32[]{:S(2)}) collective-permute-start(f32[2,16,128]{2,1,0:T(8,128)S(1)} %get-tuple-element.27), channel_id=1, source_target_pairs={{1,2},{2,1},{3,4},{4,3},{5,6},{6,5},{7,0},{0,7},{9,10},{10,9},{11,... | collective-permute-start | bytes 49160 | tf_op jit(solution)/shard_map/ppermute | solution.py:71
  7.2 0.0 collective-permute-start
  7.2 4.0 %weigh.1 = (f32[8,72,128]{2,1,0:T(8,128)}, f32[1280,128]{1,0:T(8,128)S(1)}, f32[8,512]{1,0:T(8,128)S(1)}) custom-call(f32[2,1,256,128]{3,2,1,0:T(8,128)S(1)} %get-tuple-element.28.atm_near, s32[3,1,1,8,64]{4,3,2,1,0:T(8,128)S(1)} %get-tuple-element.29.margins, f32[32,128,128]{2,1,0:T(8,128)} %weights.3, f32[2,16,128]{2,1,0:T(8,128)S(1)} %get-tuple-element.26.after), custom_call_target="tpu_custom_call" | custom-call | flops 4294967296 | bytes 1048576 | tf_op jit(solution)/shard_map/weigh/pallas_call | solution.py:45
  11.2 0.0 collective-permute-done.1.far_columns
  11.2 0.0 collective-permute-done.near_columns
  11.3 3.4 %all-to-all-start = ((f32[8,72,128]{2,1,0:T(8,128)}), f32[8,72,128]{2,1,0:T(8,128)S(1)}, u32[]{:S(2)}, u32[]{:S(2)}) async-start(f32[8,72,128]{2,1,0:T(8,128)} %get-tuple-element.38), calls=%async_computation | async-start | bytes 589824 | tf_op jit(solution)/shard_map/all_to_all | solution.py:610
  14.7 4.2 %collective-permute-start.2 = (f32[37,8,128]{2,1,0:T(8,128)S(1)}, f32[37,8,128]{2,1,0:T(8,128)S(1)}, u32[]{:S(2)}, u32[]{:S(2)}) collective-permute-start(f32[37,8,128]{2,1,0:T(8,128)S(1)} %get-tuple-element.33), channel_id=1, source_target_pairs={{8,16},{16,8},{9,17},{17,9},{10,18},{18,10},{11,19},{19,11},{12,20... | collective-permute-start | bytes 454664 | tf_op jit(solution)/shard_map/ppermute | solution.py:71
  19.0 0.1 collective-permute-start.3
  19.1 3.1 %collective-permute-done.2.far = f32[37,8,128]{2,1,0:T(8,128)S(1)} collective-permute-done((f32[37,8,128]{2,1,0:T(8,128)S(1)}, f32[37,8,128]{2,1,0:T(8,128)S(1)}, u32[]{:S(2)}, u32[]{:S(2)}) %collective-permute-start.2) | collective-permute-done | bytes 151584 | tf_op jit(solution)/shard_map/ppermute | solution.py:71
  22.1 0.0 collective-permute-done.3.near
  22.1 2.3 %run_adjoint.1 = (f32[8,64,128]{2,1,0:T(8,128)}, f32[6,4,24,384]{3,2,1,0:T(8,128)S(1)}, f32[2,4,24,384]{3,2,1,0:T(8,128)S(1)}, f32[2,4,24,384]{3,2,1,0:T(8,128)S(1)}) custom-call(f32[35,16,256]{2,1,0:T(8,128)S(1)} %get-tuple-element.25.fields, f32[2,16,128]{2,1,0:T(8,128)S(1)} %get-tuple-element.31.from_west, f32[2,16,128]{2,1,0:T(8,128)S(1)} %get-tuple-element.32.from_east, ...), custom_call_target="tpu_custom_call" | custom-call | bytes 1048576 | tf_op jit(solution)/shard_map/run_adjoint/pallas_call | solution.py:45
  24.5 0.0 all-to-all-done.received
  24.5 5.7 %all-to-all-start.1 = ((f32[8,64,128]{2,1,0:T(8,128)}), f32[8,64,128]{2,1,0:T(8,128)S(1)}, u32[]{:S(2)}, u32[]{:S(2)}) async-start(f32[8,64,128]{2,1,0:T(8,128)} %get-tuple-element.44), calls=%async_computation.1 | async-start | bytes 524288 | tf_op jit(solution)/shard_map/all_to_all | solution.py:628
  30.2 0.1 sum_forcing.1
  30.4 3.6 %collective-permute-start.4 = (f32[1,8,384]{2,1,0:T(8,128)S(1)}, f32[1,8,384]{2,1,0:T(8,128)S(1)}, u32[]{:S(2)}, u32[]{:S(2)}) collective-permute-start(f32[1,8,384]{2,1,0:T(8,128)S(1)} %get-tuple-element.40), channel_id=1, source_target_pairs={{8,16},{16,8},{9,17},{17,9},{10,18},{18,10},{11,19},{19,11},{12,20... | collective-permute-start | bytes 36872 | tf_op jit(solution)/shard_map/ppermute | solution.py:71
  34.0 0.1 collective-permute-start.5
  34.1 1.6 %collective-permute-done.4.far = f32[1,8,384]{2,1,0:T(8,128)S(1)} collective-permute-done((f32[1,8,384]{2,1,0:T(8,128)S(1)}, f32[1,8,384]{2,1,0:T(8,128)S(1)}, u32[]{:S(2)}, u32[]{:S(2)}) %collective-permute-start.4) | collective-permute-done | bytes 12320 | tf_op jit(solution)/shard_map/ppermute | solution.py:71
  35.7 0.0 collective-permute-done.5.near
  35.7 2.1 %run_forward.1 = (f32[2,4,16,256]{3,2,1,0:T(8,128)}, f32[2,4,16,256]{3,2,1,0:T(8,128)}) custom-call(f32[6,4,24,384]{3,2,1,0:T(8,128)S(1)} %get-tuple-element.35.coeffs, f32[2,4,24,384]{3,2,1,0:T(8,128)S(1)} %get-tuple-element.36.start, f32[2,4,24,384]{3,2,1,0:T(8,128)S(1)} %get-tuple-element.37.lam, f32[2,16,384]{2,1,0:T(8,128)S(1)} %get-tuple-element.39.forcing, ...), custom_call_target="tpu_custom_call" | custom-call | bytes 1048576 | tf_op jit(solution)/shard_map/run_forward/pallas_call | solution.py:45
  37.8 0.8 %all-to-all-done.1.gathered = f32[8,64,128]{2,1,0:T(8,128)S(1)} async-done(((f32[8,64,128]{2,1,0:T(8,128)}), f32[8,64,128]{2,1,0:T(8,128)S(1)}, u32[]{:S(2)}, u32[]{:S(2)}) %all-to-all-start.1) | async-done | bytes 262176 | tf_op jit(solution)/shard_map/all_to_all | solution.py:628
  38.6 3.6 %unweigh.1 = f32[2,1,256,128]{3,2,1,0:T(8,128)} custom-call(f32[8,64,128]{2,1,0:T(8,128)S(1)} %all-to-all-done.1.gathered, f32[1280,128]{1,0:T(8,128)S(1)} %get-tuple-element.45.found, f32[8,512]{1,0:T(8,128)S(1)} %get-tuple-element.46.keys, f32[32,128,128]{2,1,0:T(8,128)} %weights.3), custom_call_target="tpu_custom_call" | custom-call | flops 4294967296 | bytes 1048576 | tf_op jit(solution)/shard_map/unweigh/pallas_call | solution.py:45
  (1 shorter events, 0.0 us)
Async XLA Ops:
  2.1 9.1 %collective-permute-start.1 = (f32[2,16,128]{2,1,0:T(8,128)S(1)}, f32[2,16,128]{2,1,0:T(8,128)S(1)}, u32[]{:S(2)}, u32[]{:S(2)}) collective-permute-start(f32[2,16,128]{2,1,0:T(8,128)S(1)} %get-tuple-element.27), channel_id=1, source_target_pairs={{1,2},{2,1},{3,4},{4,3},{5,6},{6,5},{7,0},{0,7},{9,10},{10,9},{11,... | collective-permute-start | bytes 49160 | tf_op jit(solution)/shard_map/ppermute | solution.py:71
  7.2 4.0 %collective-permute-start = (f32[2,16,128]{2,1,0:T(8,128)S(1)}, f32[2,16,128]{2,1,0:T(8,128)S(1)}, u32[]{:S(2)}, u32[]{:S(2)}) collective-permute-start(f32[2,16,128]{2,1,0:T(8,128)S(1)} %get-tuple-element.26.after), channel_id=1, source_target_pairs={{0,1},{1,0},{2,3},{3,2},{4,5},{5,4},{6,7},{7,6},{8,9},{9,8},{10,11... | collective-permute-start | bytes 49160 | tf_op jit(solution)/shard_map/ppermute | solution.py:72
  11.3 13.2 %all-to-all-start = ((f32[8,72,128]{2,1,0:T(8,128)}), f32[8,72,128]{2,1,0:T(8,128)S(1)}, u32[]{:S(2)}, u32[]{:S(2)}) async-start(f32[8,72,128]{2,1,0:T(8,128)} %get-tuple-element.38), calls=%async_computation | async-start | bytes 589824 | tf_op jit(solution)/shard_map/all_to_all | solution.py:610
  14.7 7.4 %collective-permute-start.2 = (f32[37,8,128]{2,1,0:T(8,128)S(1)}, f32[37,8,128]{2,1,0:T(8,128)S(1)}, u32[]{:S(2)}, u32[]{:S(2)}) collective-permute-start(f32[37,8,128]{2,1,0:T(8,128)S(1)} %get-tuple-element.33), channel_id=1, source_target_pairs={{8,16},{16,8},{9,17},{17,9},{10,18},{18,10},{11,19},{19,11},{12,20... | collective-permute-start | bytes 454664 | tf_op jit(solution)/shard_map/ppermute | solution.py:71
  19.0 3.2 %collective-permute-start.3 = (f32[37,8,128]{2,1,0:T(8,128)S(1)}, f32[37,8,128]{2,1,0:T(8,128)S(1)}, u32[]{:S(2)}, u32[]{:S(2)}) collective-permute-start(f32[37,8,128]{2,1,0:T(8,128)S(1)} %get-tuple-element.34), channel_id=1, source_target_pairs={{0,8},{8,0},{16,24},{24,16},{1,9},{9,1},{17,25},{25,17},{2,10},{10... | collective-permute-start | bytes 454664 | tf_op jit(solution)/shard_map/ppermute | solution.py:72
  24.5 14.1 %all-to-all-start.1 = ((f32[8,64,128]{2,1,0:T(8,128)}), f32[8,64,128]{2,1,0:T(8,128)S(1)}, u32[]{:S(2)}, u32[]{:S(2)}) async-start(f32[8,64,128]{2,1,0:T(8,128)} %get-tuple-element.44), calls=%async_computation.1 | async-start | bytes 524288 | tf_op jit(solution)/shard_map/all_to_all | solution.py:628
  30.4 5.3 %collective-permute-start.4 = (f32[1,8,384]{2,1,0:T(8,128)S(1)}, f32[1,8,384]{2,1,0:T(8,128)S(1)}, u32[]{:S(2)}, u32[]{:S(2)}) collective-permute-start(f32[1,8,384]{2,1,0:T(8,128)S(1)} %get-tuple-element.40), channel_id=1, source_target_pairs={{8,16},{16,8},{9,17},{17,9},{10,18},{18,10},{11,19},{19,11},{12,20... | collective-permute-start | bytes 36872 | tf_op jit(solution)/shard_map/ppermute | solution.py:71
  34.0 1.7 %collective-permute-start.5 = (f32[1,8,384]{2,1,0:T(8,128)S(1)}, f32[1,8,384]{2,1,0:T(8,128)S(1)}, u32[]{:S(2)}, u32[]{:S(2)}) collective-permute-start(f32[1,8,384]{2,1,0:T(8,128)S(1)} %get-tuple-element.41), channel_id=1, source_target_pairs={{0,8},{8,0},{16,24},{24,16},{1,9},{9,1},{17,25},{25,17},{2,10},{10... | collective-permute-start | bytes 36872 | tf_op jit(solution)/shard_map/ppermute | solution.py:72

commit v2 on v1

--- a/solution.py
+++ b/solution.py
@@ -9,7 +9,7 @@
 STEPS = 4
 HALO = STEPS
 PER_LANES = BLOCK // HALO
-GROUP = 8
+GROUP = 16
 f32 = jnp.float32
 bf16 = jnp.bfloat16
 VMEM_LIMIT = 32 * 1024 * 1024
@@ -160,17 +160,18 @@
     return jnp.where(rows(from_north.shape) < HALO, from_north, from_south)
 
 
-def widen(fields, from_west, from_east, near, far, wide):
+def widen(fields, from_west, from_east, near, far, start, wide):
     count, tile_lat, tile_lon = fields.shape
     halves = tile_lon // BLOCK
     parts = from_west.shape[0]
     corners = [edge_rows(near, far, count * halves + n) for n in range(2 * parts)]
     for i in range(count):
-        wide[i, :tile_lat, :tile_lon] = fields[i]
-        wide[i, :tile_lat, tile_lon:] = unpack_columns(from_west, from_east, i)
+        out = start.at[i] if i < start.shape[0] else wide.at[i - start.shape[0]]
+        out[:tile_lat, :tile_lon] = fields[i]
+        out[:tile_lat, tile_lon:] = unpack_columns(from_west, from_east, i)
         for h in range(halves):
-            wide[i, tile_lat:, h * BLOCK : (h + 1) * BLOCK] = edge_rows(near, far, i * halves + h)
-        wide[i, tile_lat:, tile_lon:] = unpack_columns(corners[:parts], corners[parts:], i)
+            out[tile_lat:, h * BLOCK : (h + 1) * BLOCK] = edge_rows(near, far, i * halves + h)
+        out[tile_lat:, tile_lon:] = unpack_columns(corners[:parts], corners[parts:], i)
 
 
 def eastward(x):
@@ -189,10 +190,10 @@
     return turn(x, 1, 0)
 
 
-def adjoint_step(coeffs, read, write):
+def adjoint_step(coeffs, read, write, first, last):
     levels = coeffs.shape[1]
-    above = None
-    for level in range(levels):
+    above = coeffs[4, first - 1] * (read(first) - read(first - 1)) if first else None
+    for level in range(first, last):
         lam = read(level)
         step_x = eastward(lam) - lam
         step_y = northward(lam) - lam
@@ -206,17 +207,18 @@
         write(level, out)
 
 
+def surface_levels(step, levels):
+    return min(levels, STEPS - 1 - step)
+
+
 def run_adjoint(
-    fields, from_west, from_east, far, near, blocks, coeffs, start, lam_out, wide, state, own, sent
+    fields, from_west, from_east, far, near, blocks, coeffs, start, states, wide, own, sent
 ):
     levels = coeffs.shape[1]
     tile_lat, tile_lon = fields.shape[1:]
     halves = tile_lon // BLOCK
-    widen(fields, from_west, from_east, near, far, wide)
-    base = 4 * levels
-    for f in range(2):
-        for level in range(levels):
-            start[f, level] = wide[f * levels + level]
+    widen(fields, from_west, from_east, near, far, start, wide)
+    base = 0
     mask0 = None
     for level in range(levels):
         east_d, east_u = wide[base + level], wide[base + levels + level]
@@ -234,21 +236,17 @@
         coeffs[5, level] = mask
     copies = []
     for f in range(2):
-        surface = wide[(2 + f) * levels, :tile_lat, :tile_lon]
+        surface = start[(2 + f) * levels, :tile_lat, :tile_lon]
         for step in range(STEPS - 1):
+
             def read(level):
-                return wide[(2 + f) * levels + level] if step == 0 else state[(step - 1) % 2, level]
+                return states[f, step - 1, level] if step else start[(2 + f) * levels + level]
 
             def write(level, lam):
-                nonlocal surface
-                if level == 0:
-                    surface = surface + lam[:tile_lat, :tile_lon]
-                if step == STEPS - 2:
-                    lam_out[f, level] = lam
-                else:
-                    state[step % 2, level] = lam
-
-            adjoint_step(coeffs, read, write)
+                states[f, step, level] = lam
+
+            adjoint_step(coeffs, read, write, 0, surface_levels(step, levels))
+            surface = surface + states[f, step, 0, :tile_lat, :tile_lon]
         surface = surface * mask0[:tile_lat, :tile_lon]
         for h in range(halves):
             at = (f * halves + h) * tile_lat
@@ -257,6 +255,27 @@
         copies += fetch([(own.at[field], blocks.at[k, field]) for k in range(blocks.shape[0])], sent.at[f])
     for copy in copies:
         copy.wait()
+
+
+def finish_adjoint(coeffs, start, states, adjoint_out, rest):
+    levels = coeffs.shape[1]
+    tile_lat, tile_lon = adjoint_out.shape[2:]
+    for f in range(2):
+        for step in range(STEPS):
+            done = surface_levels(step, levels)
+
+            def read(level):
+                if not step:
+                    return start[(2 + f) * levels + level]
+                return (states if level < surface_levels(step - 1, levels) else rest)[f, step - 1, level]
+
+            def write(level, lam):
+                if step == STEPS - 1:
+                    adjoint_out[f, level] = lam[:tile_lat, :tile_lon]
+                else:
+                    rest[f, step, level] = lam
+
+            adjoint_step(coeffs, read, write, done, levels)
 
 
 def sum_forcing(received, forcing, near, far):
@@ -285,21 +304,16 @@
     near[0], far[0] = sort_swap("lat", to_north, to_south)
 
 
-def run_forward(coeffs, start, lam, forcing, far, near, final, adjoint_out, state):
+def run_forward(coeffs, start, forcing, far, near, final, state):
     levels = coeffs.shape[1]
     tile_lat, tile_lon = final.shape[2:]
     for f in range(2):
-
-        def write(level, out):
-            adjoint_out[f, level] = out[:tile_lat, :tile_lon]
-
-        adjoint_step(coeffs, lambda level: lam[f, level], write)
         force = jnp.concatenate([forcing[f], edge_rows(near, far, f)], axis=0)
         force = force * coeffs[5, 0]
         for step in range(STEPS):
             above = None
             for level in range(levels):
-                read = (lambda n: start[f, n]) if step == 0 else (lambda n: state[(step - 1) % 2, n])
+                read = (lambda n: start[f * levels + n]) if step == 0 else (lambda n: state[(step - 1) % 2, n])
                 theta = read(level)
                 east_flux = coeffs[0, level] * theta + coeffs[1, level] * eastward(theta)
                 north_flux = coeffs[2, level] * theta + coeffs[3, level] * northward(theta)
@@ -612,12 +626,12 @@
 
     wide = (tile_lat + 8, tile_lon + BLOCK)
     own = (2 * halves * tile_lat, BLOCK)
-    blocks, coeffs, start, lam = call(
+    adjoint_states = (2, STEPS - 1, levels, *wide)
+    blocks, coeffs, start, states = call(
         run_adjoint,
-        [(lon_count, *own), (6, levels, *wide), (2, levels, *wide), (2, levels, *wide)],
+        [(lon_count, *own), (6, levels, *wide), (4 * levels, *wide), adjoint_states],
         [
-            pltpu.VMEM((count, *wide), f32),
-            pltpu.VMEM((2, levels, *wide), f32),
+            pltpu.VMEM((count - 4 * levels, *wide), f32),
             pltpu.VMEM(own, f32),
             pltpu.SemaphoreType.DMA((2, lon_count)),
         ],
@@ -632,13 +646,20 @@
         sum_forcing, [(2, tile_lat, tile_lon + BLOCK), message, message], name="sum_forcing", inputs=1
     )(received)
     near_rows, far_rows = swap(near, far, "lat", False)
-    final, adjoint = call(
+    (adjoint,) = call(
+        finish_adjoint,
+        [cotangent.shape],
+        [pltpu.VMEM(adjoint_states, f32)],
+        name="finish_adjoint",
+        inputs=3,
+    )(coeffs, start, states)
+    (final,) = call(
         run_forward,
-        [tracers.shape, cotangent.shape],
+        [tracers.shape],
         [pltpu.VMEM((2, levels, *wide), f32)],
         name="run_forward",
-        inputs=6,
-    )(coeffs, start, lam, forcing, far_rows, near_rows)
+        inputs=5,
+    )(coeffs, start, forcing, far_rows, near_rows)
 
     (gradient,) = call(
         unweigh,

time: 42.6 us -> 44.5 us (1.045)
  the two profiles are of different devices: /device:TPU:1 before, /device:TPU:0 now
where the time goes in v2:
time: 44.5 us; the launch traced here: 44 us
  starting transfers between devices  21.2 us (48%)
  Pallas kernels  13.4 us (30%)
  waiting for transfers between devices  6.75 us (15%)
  local copies, waits for them, and re-layouts  1.93 us (4%)
  between operations  0.7 us (2%)
    pallas_call x8, Pallas kernels, run(): kernel(*(pltpu.with_memory_space_constraint(x, pltpu.HBM) if n in far els...  13.4 us
    ppermute x3, starting transfers between devices, swap(): far = lax.ppermute(far, axis, pairs[1])  7.36 us
    ppermute x3, starting transfers between devices, swap(): return (lax.ppermute(near, axis, pairs[0]), far)  6.85 us
    all_to_all x1, starting transfers between devices, on_device(): lax.all_to_all(blocks, 'lon', split_axis=0, concat_axis=0, tiled=True)  3.58 us
    all_to_all x1, starting transfers between devices, on_device(): lax.all_to_all(sums, 'lon', split_axis=0, concat_axis=0, tiled=True)  3.43 us
    all_to_all x1, waiting for transfers between devices, on_device(): lax.all_to_all(sums, 'lon', split_axis=0, concat_axis=0, tiled=True)  3.28 us
    all_to_all x1, waiting for transfers between devices, on_device(): lax.all_to_all(blocks, 'lon', split_axis=0, concat_axis=0, tiled=True)  2.44 us
    unnamed x4, local copies, waits for them, and re-layouts  1.93 us
  transfers between devices with their start and end apart: 8, of which 3 were waited for; matrix products, arithmetic and copies ran while one was open for 0% of the time, Pallas kernels for 19%

profile of v2, /device:TPU:0, one launch (start us, length us, event | category | flops | bytes accessed | tf_op | source)
XLA Modules:
  0.0 44.0 jit_solution(5332021386135207292)
XLA Ops:
  0.6 1.4 %pack_columns.1 = (f32[35,16,256]{2,1,0:T(8,128)S(1)}, f32[2,16,128]{2,1,0:T(8,128)S(1)}, f32[2,16,128]{2,1,0:T(8,128)S(1)}, f32[2,1,256,128]{3,2,1,0:T(8,128)S(1)}, s32[3,1,1,8,64]{4,3,2,1,0:T(8,128)S(1)}) custom-call(f32[2,4,16,256]{3,2,1,0:T(8,128)} %refs_0_.1, f32[2,4,16,256]{3,2,1,0:T(8,128)} %refs_1_.1, s32[4,16,256]{2,1,0:T(8,128)} %refs_2_.1, ...), custom_call_target="tpu_custom_call" | custom-call | bytes 1048576 | tf_op jit(solution)/shard_map/pack_columns/pallas_call | solution.py:45
  2.1 6.0 %collective-permute-start.1 = (f32[2,16,128]{2,1,0:T(8,128)S(1)}, f32[2,16,128]{2,1,0:T(8,128)S(1)}, u32[]{:S(2)}, u32[]{:S(2)}) collective-permute-start(f32[2,16,128]{2,1,0:T(8,128)S(1)} %get-tuple-element.25), channel_id=1, source_target_pairs={{1,2},{2,1},{3,4},{4,3},{5,6},{6,5},{7,0},{0,7},{9,10},{10,9},{11,... | collective-permute-start | bytes 49160 | tf_op jit(solution)/shard_map/ppermute | solution.py:71
  8.1 0.0 collective-permute-start
  8.1 3.7 %weigh.1 = (f32[8,72,128]{2,1,0:T(8,128)}, f32[1280,128]{1,0:T(8,128)S(1)}, f32[8,512]{1,0:T(8,128)S(1)}) custom-call(f32[2,1,256,128]{3,2,1,0:T(8,128)S(1)} %get-tuple-element.26.atm_near, s32[3,1,1,8,64]{4,3,2,1,0:T(8,128)S(1)} %get-tuple-element.27.margins, f32[32,128,128]{2,1,0:T(8,128)} %weights.3, f32[2,16,128]{2,1,0:T(8,128)S(1)} %get-tuple-element.24.after), custom_call_target="tpu_custom_call" | custom-call | flops 4294967296 | bytes 1048576 | tf_op jit(solution)/shard_map/weigh/pallas_call | solution.py:45
  11.8 0.8 %copy-done = f32[1280,128]{1,0:T(8,128)} copy-done((f32[1280,128]{1,0:T(8,128)}, f32[1280,128]{1,0:T(8,128)S(1)}, u32[]{:S(2)}) %copy-start) | copy-done | bytes 655384
  12.7 0.0 collective-permute-done.1.far_columns
  12.7 0.0 collective-permute-done.near_columns
  12.7 3.4 %all-to-all-start = ((f32[8,72,128]{2,1,0:T(8,128)}), f32[8,72,128]{2,1,0:T(8,128)S(1)}, u32[]{:S(2)}, u32[]{:S(2)}) async-start(f32[8,72,128]{2,1,0:T(8,128)} %get-tuple-element.35), calls=%async_computation | async-start | bytes 589824 | tf_op jit(solution)/shard_map/all_to_all | solution.py:624
  16.2 0.7 %collective-permute-start.2 = (f32[37,8,128]{2,1,0:T(8,128)S(1)}, f32[37,8,128]{2,1,0:T(8,128)S(1)}, u32[]{:S(2)}, u32[]{:S(2)}) collective-permute-start(f32[37,8,128]{2,1,0:T(8,128)S(1)} %get-tuple-element.31), channel_id=1, source_target_pairs={{8,16},{16,8},{9,17},{17,9},{10,18},{18,10},{11,19},{19,11},{12,20... | collective-permute-start | bytes 454664 | tf_op jit(solution)/shard_map/ppermute | solution.py:71
  16.8 2.9 %collective-permute-start.3 = (f32[37,8,128]{2,1,0:T(8,128)S(1)}, f32[37,8,128]{2,1,0:T(8,128)S(1)}, u32[]{:S(2)}, u32[]{:S(2)}) collective-permute-start(f32[37,8,128]{2,1,0:T(8,128)S(1)} %get-tuple-element.32), channel_id=1, source_target_pairs={{0,8},{8,0},{16,24},{24,16},{1,9},{9,1},{17,25},{25,17},{2,10},{10... | collective-permute-start | bytes 454664 | tf_op jit(solution)/shard_map/ppermute | solution.py:72
  19.8 0.0 collective-permute-done.2.far
  19.8 1.0 %collective-permute-done.3.near = f32[37,8,128]{2,1,0:T(8,128)S(1)} collective-permute-done((f32[37,8,128]{2,1,0:T(8,128)S(1)}, f32[37,8,128]{2,1,0:T(8,128)S(1)}, u32[]{:S(2)}, u32[]{:S(2)}) %collective-permute-start.3) | collective-permute-done | bytes 151584 | tf_op jit(solution)/shard_map/ppermute | solution.py:72
  20.8 1.6 %run_adjoint.1 = (f32[8,64,128]{2,1,0:T(8,128)}, f32[6,4,24,384]{3,2,1,0:T(8,128)S(1)}, f32[16,24,384]{2,1,0:T(8,128)S(1)}, f32[2,3,4,24,384]{4,3,2,1,0:T(8,128)S(1)}) custom-call(f32[35,16,256]{2,1,0:T(8,128)S(1)} %get-tuple-element.23.fields, f32[2,16,128]{2,1,0:T(8,128)S(1)} %get-tuple-element.29.from_west, ...), custom_call_target="tpu_custom_call" | custom-call | bytes 1048576 | tf_op jit(solution)/shard_map/run_adjoint/pallas_call | solution.py:45
  22.4 3.3 %all-to-all-done.received = f32[8,72,128]{2,1,0:T(8,128)S(1)} async-done(((f32[8,72,128]{2,1,0:T(8,128)}), f32[8,72,128]{2,1,0:T(8,128)S(1)}, u32[]{:S(2)}, u32[]{:S(2)}) %all-to-all-start) | async-done | bytes 294944 | tf_op jit(solution)/shard_map/all_to_all | solution.py:624
  25.7 3.6 %all-to-all-start.1 = ((f32[8,64,128]{2,1,0:T(8,128)}), f32[8,64,128]{2,1,0:T(8,128)S(1)}, u32[]{:S(2)}, u32[]{:S(2)}) async-start(f32[8,64,128]{2,1,0:T(8,128)} %get-tuple-element.40), calls=%async_computation.1 | async-start | bytes 524288 | tf_op jit(solution)/shard_map/all_to_all | solution.py:642
  29.3 0.1 sum_forcing.1
  29.4 0.7 %collective-permute-start.4 = (f32[1,8,384]{2,1,0:T(8,128)S(1)}, f32[1,8,384]{2,1,0:T(8,128)S(1)}, u32[]{:S(2)}, u32[]{:S(2)}) collective-permute-start(f32[1,8,384]{2,1,0:T(8,128)S(1)} %get-tuple-element.37), channel_id=1, source_target_pairs={{8,16},{16,8},{9,17},{17,9},{10,18},{18,10},{11,19},{19,11},{12,20... | collective-permute-start | bytes 36872 | tf_op jit(solution)/shard_map/ppermute | solution.py:71
  30.1 3.9 %collective-permute-start.5 = (f32[1,8,384]{2,1,0:T(8,128)S(1)}, f32[1,8,384]{2,1,0:T(8,128)S(1)}, u32[]{:S(2)}, u32[]{:S(2)}) collective-permute-start(f32[1,8,384]{2,1,0:T(8,128)S(1)} %get-tuple-element.38), channel_id=1, source_target_pairs={{0,8},{8,0},{16,24},{24,16},{1,9},{9,1},{17,25},{25,17},{2,10},{10... | collective-permute-start | bytes 36872 | tf_op jit(solution)/shard_map/ppermute | solution.py:72
  34.0 1.4 %finish_adjoint.1 = f32[2,4,16,256]{3,2,1,0:T(8,128)} custom-call(f32[6,4,24,384]{3,2,1,0:T(8,128)S(1)} %get-tuple-element.33.coeffs, f32[16,24,384]{2,1,0:T(8,128)S(1)} %get-tuple-element.34.start, f32[2,3,4,24,384]{4,3,2,1,0:T(8,128)S(1)} %get-tuple-element.39.states), custom_call_target="tpu_custom_call" | custom-call | bytes 1048576 | tf_op jit(solution)/shard_map/finish_adjoint/pallas_call | solution.py:45
  35.4 0.0 collective-permute-done.4.far
  35.4 1.6 %run_forward.1 = f32[2,4,16,256]{3,2,1,0:T(8,128)} custom-call(f32[6,4,24,384]{3,2,1,0:T(8,128)S(1)} %get-tuple-element.33.coeffs, f32[16,24,384]{2,1,0:T(8,128)S(1)} %get-tuple-element.34.start, f32[2,16,384]{2,1,0:T(8,128)S(1)} %get-tuple-element.36.forcing, f32[1,8,384]{2,1,0:T(8,128)S(1)} %collective-permute-done.4.far, ...), custom_call_target="tpu_custom_call" | custom-call | bytes 1048576 | tf_op jit(solution)/shard_map/run_forward/pallas_call | solution.py:45
  37.0 2.4 %all-to-all-done.1.gathered = f32[8,64,128]{2,1,0:T(8,128)S(1)} async-done(((f32[8,64,128]{2,1,0:T(8,128)}), f32[8,64,128]{2,1,0:T(8,128)S(1)}, u32[]{:S(2)}, u32[]{:S(2)}) %all-to-all-start.1) | async-done | bytes 262176 | tf_op jit(solution)/shard_map/all_to_all | solution.py:642
  39.4 1.1 %copy-done.1 = f32[1280,128]{1,0:T(8,128)S(1)} copy-done((f32[1280,128]{1,0:T(8,128)S(1)}, f32[1280,128]{1,0:T(8,128)}, u32[]{:S(2)}) %copy-start.1) | copy-done | bytes 655384
  40.5 3.5 %unweigh.1 = f32[2,1,256,128]{3,2,1,0:T(8,128)} custom-call(f32[8,64,128]{2,1,0:T(8,128)S(1)} %all-to-all-done.1.gathered, f32[1280,128]{1,0:T(8,128)S(1)} %copy-done.1, f32[8,512]{1,0:T(8,128)S(1)} %get-tuple-element.42.keys, f32[32,128,128]{2,1,0:T(8,128)} %weights.3), custom_call_target="tpu_custom_call" | custom-call | flops 4294967296 | bytes 1048576 | tf_op jit(solution)/shard_map/unweigh/pallas_call | solution.py:45
  (4 shorter events, 0.1 us)
Async XLA Ops:
  2.1 10.6 %collective-permute-start.1 = (f32[2,16,128]{2,1,0:T(8,128)S(1)}, f32[2,16,128]{2,1,0:T(8,128)S(1)}, u32[]{:S(2)}, u32[]{:S(2)}) collective-permute-start(f32[2,16,128]{2,1,0:T(8,128)S(1)} %get-tuple-element.25), channel_id=1, source_target_pairs={{1,2},{2,1},{3,4},{4,3},{5,6},{6,5},{7,0},{0,7},{9,10},{10,9},{11,... | collective-permute-start | bytes 49160 | tf_op jit(solution)/shard_map/ppermute | solution.py:71
  8.1 4.5 %collective-permute-start = (f32[2,16,128]{2,1,0:T(8,128)S(1)}, f32[2,16,128]{2,1,0:T(8,128)S(1)}, u32[]{:S(2)}, u32[]{:S(2)}) collective-permute-start(f32[2,16,128]{2,1,0:T(8,128)S(1)} %get-tuple-element.24.after), channel_id=1, source_target_pairs={{0,1},{1,0},{2,3},{3,2},{4,5},{5,4},{6,7},{7,6},{8,9},{9,8},{10,11... | collective-permute-start | bytes 49160 | tf_op jit(solution)/shard_map/ppermute | solution.py:72
  11.8 0.8 %copy-start = (f32[1280,128]{1,0:T(8,128)}, f32[1280,128]{1,0:T(8,128)S(1)}, u32[]{:S(2)}) copy-start(f32[1280,128]{1,0:T(8,128)S(1)} %get-tuple-element.41.found) | copy-start | bytes 1966084
  12.7 13.0 %all-to-all-start = ((f32[8,72,128]{2,1,0:T(8,128)}), f32[8,72,128]{2,1,0:T(8,128)S(1)}, u32[]{:S(2)}, u32[]{:S(2)}) async-start(f32[8,72,128]{2,1,0:T(8,128)} %get-tuple-element.35), calls=%async_computation | async-start | bytes 589824 | tf_op jit(solution)/shard_map/all_to_all | solution.py:624
  16.2 3.6 %collective-permute-start.2 = (f32[37,8,128]{2,1,0:T(8,128)S(1)}, f32[37,8,128]{2,1,0:T(8,128)S(1)}, u32[]{:S(2)}, u32[]{:S(2)}) collective-permute-start(f32[37,8,128]{2,1,0:T(8,128)S(1)} %get-tuple-element.31), channel_id=1, source_target_pairs={{8,16},{16,8},{9,17},{17,9},{10,18},{18,10},{11,19},{19,11},{12,20... | collective-permute-start | bytes 454664 | tf_op jit(solution)/shard_map/ppermute | solution.py:71
  16.8 3.9 %collective-permute-start.3 = (f32[37,8,128]{2,1,0:T(8,128)S(1)}, f32[37,8,128]{2,1,0:T(8,128)S(1)}, u32[]{:S(2)}, u32[]{:S(2)}) collective-permute-start(f32[37,8,128]{2,1,0:T(8,128)S(1)} %get-tuple-element.32), channel_id=1, source_target_pairs={{0,8},{8,0},{16,24},{24,16},{1,9},{9,1},{17,25},{25,17},{2,10},{10... | collective-permute-start | bytes 454664 | tf_op jit(solution)/shard_map/ppermute | solution.py:72
  25.7 13.7 %all-to-all-start.1 = ((f32[8,64,128]{2,1,0:T(8,128)}), f32[8,64,128]{2,1,0:T(8,128)S(1)}, u32[]{:S(2)}, u32[]{:S(2)}) async-start(f32[8,64,128]{2,1,0:T(8,128)} %get-tuple-element.40), calls=%async_computation.1 | async-start | bytes 524288 | tf_op jit(solution)/shard_map/all_to_all | solution.py:642
  29.4 6.0 %collective-permute-start.4 = (f32[1,8,384]{2,1,0:T(8,128)S(1)}, f32[1,8,384]{2,1,0:T(8,128)S(1)}, u32[]{:S(2)}, u32[]{:S(2)}) collective-permute-start(f32[1,8,384]{2,1,0:T(8,128)S(1)} %get-tuple-element.37), channel_id=1, source_target_pairs={{8,16},{16,8},{9,17},{17,9},{10,18},{18,10},{11,19},{19,11},{12,20... | collective-permute-start | bytes 36872 | tf_op jit(solution)/shard_map/ppermute | solution.py:71
  30.1 5.3 %collective-permute-start.5 = (f32[1,8,384]{2,1,0:T(8,128)S(1)}, f32[1,8,384]{2,1,0:T(8,128)S(1)}, u32[]{:S(2)}, u32[]{:S(2)}) collective-permute-start(f32[1,8,384]{2,1,0:T(8,128)S(1)} %get-tuple-element.38), channel_id=1, source_target_pairs={{0,8},{8,0},{16,24},{24,16},{1,9},{9,1},{17,25},{25,17},{2,10},{10... | collective-permute-start | bytes 36872 | tf_op jit(solution)/shard_map/ppermute | solution.py:72
  39.4 1.1 %copy-start.1 = (f32[1280,128]{1,0:T(8,128)S(1)}, f32[1280,128]{1,0:T(8,128)}, u32[]{:S(2)}) copy-start(f32[1280,128]{1,0:T(8,128)} %copy-done) | copy-start | bytes 1966084

commit v3 on v2

--- a/solution.py
+++ b/solution.py
@@ -12,7 +12,7 @@
 GROUP = 16
 f32 = jnp.float32
 bf16 = jnp.bfloat16
-VMEM_LIMIT = 32 * 1024 * 1024
+VMEM_LIMIT = 20 * 1024 * 1024
 
 
 def call(body, outs, scratch=(), flops=0, name=None, inputs=0, far=(), far_outs=(), aliases=None):
@@ -388,11 +388,11 @@
     return jnp.concatenate(out, axis=1)
 
 
-def find_slots(r, code, block_row, rank, capacity, blocks, column):
+def find_slots(r, code, block_row, rank, capacity, blocks, found):
     slots = block_row.shape[1]
     mine = rows((blocks, slots)) == block_row
     ranked = one_hot(rows((capacity, slots)) == rank.astype(jnp.int32) - r * capacity)
-    rest, found = code + 1.0, None
+    rest, codes = code + 1.0, None
     for base in (4096.0, 64.0, 1.0):
         digit = jnp.floor(rest * (1.0 / base))
         rest = rest - digit * base
@@ -402,25 +402,26 @@
             (((1,), (1,)), ((), ())),
             preferred_element_type=f32,
         )
-        found = part * base if found is None else found + part * base
-    found = found - 1.0
-    for w in range(blocks):
-        column[w * capacity : (w + 1) * capacity] = jnp.broadcast_to(found[:, w : w + 1], (capacity, BLOCK))
-
-
-def couple(blocks, part, table, size, capacity, rounds, prepare, column, gather_first, transposed, result, scratch):
-    vectors, products = scratch
+        codes = part * base if codes is None else codes + part * base
+    found[:, :blocks] = codes - 1.0
+
+
+def couple(blocks, part, table, size, capacity, rounds, prepare, found, gather_first, transposed, result, scratch):
+    column, vectors, products = scratch
     total_rows = column.shape[0]
     result[...] = jnp.zeros_like(result)
 
     def one_round(r, carry):
         prepare(r)
+        codes = found[...]
+        for w in range(blocks):
+            column[w * capacity : (w + 1) * capacity] = jnp.broadcast_to(codes[:, w : w + 1], (capacity, BLOCK))
         eye = rows((BLOCK, BLOCK)) == lanes((BLOCK, BLOCK))
         place_hot = []
         for at in range(0, total_rows, BLOCK):
-            found = column[at : at + BLOCK]
-            first = jnp.floor((found + 0.5) * (1.0 / size))
-            second = found - first * size
+            code = column[at : at + BLOCK]
+            first = jnp.floor((code + 0.5) * (1.0 / size))
+            second = code - first * size
             gather, put = (first, second) if gather_first else (second, first)
             width = table.shape[0]
             gather = jnp.concatenate([gather] * (width // BLOCK), axis=1)
@@ -467,7 +468,7 @@
 
 
 def weigh(atm_near, margins, weights, after, sums, found, keys, result, *scratch):
-    scratch, (held, arrived) = scratch[:2], scratch[2:]
+    scratch, (held, arrived) = scratch[:3], scratch[3:]
     fetch_weights(weights, held, arrived)
     lon_count = margins.shape[3]
     atm = atm_near.shape[2]
@@ -511,8 +512,8 @@
         sums[k, 4 * tile_lat :] = jnp.where((near < 2 * HALO) | (near >= BLOCK - 2 * HALO), upper, lower)
 
 
-def unweigh(gathered, found, keys, weights, gradient, result, column, *scratch):
-    scratch, (held, arrived) = scratch[:2], scratch[2:]
+def unweigh(gathered, found, keys, weights, gradient, result, codes, *scratch):
+    scratch, (held, arrived) = scratch[:3], scratch[3:]
     fetch_weights(weights, held, arrived)
     atm = gradient.shape[2]
     blocks = weights.shape[0]
@@ -532,11 +533,11 @@
     def prepare(r):
         @pl.when(r == 0)
         def _():
-            column[...] = found[...]
+            codes[...] = found[...]
 
         @pl.when(r > 0)
         def _():
-            find_slots(r, keys[0:1], keys[1:2].astype(jnp.int32), keys[2:3], capacity, blocks, column)
+            find_slots(r, keys[0:1], keys[1:2].astype(jnp.int32), keys[2:3], capacity, blocks, codes)
 
     couple(
         blocks,
@@ -546,7 +547,7 @@
         capacity,
         rounds,
         prepare,
-        column,
+        codes,
         True,
         True,
         result,
@@ -594,6 +595,7 @@
     def coupling_scratch(result_rows):
         return [
             pltpu.VMEM((result_rows, 2 * BLOCK), f32),
+            pltpu.VMEM((held_rows, BLOCK), f32),
             pltpu.VMEM((held_rows, 4 * BLOCK), f32),
             pltpu.VMEM((held_rows, 2 * BLOCK), f32),
             pltpu.VMEM((groups, GROUP, BLOCK, BLOCK), f32),
@@ -603,7 +605,7 @@
     coupling_flops = 4 * slots * blocks_of * 2 * BLOCK * BLOCK * 2
     sums, found, keys = call(
         weigh,
-        [(lon_count, sum_rows, BLOCK), (held_rows, BLOCK), (8, slots)],
+        [(lon_count, sum_rows, BLOCK), (places(slots, blocks_of), BLOCK), (8, slots)],
         coupling_scratch(ocean_blocks),
         coupling_flops,
         name="weigh",

time: 44.5 us -> 42.2 us (0.948)
  the two profiles are of different devices: /device:TPU:0 before, /device:TPU:1 now
where the time goes in v3:
time: 42.2 us; the launch traced here: 41.6 us
  starting transfers between devices  22.6 us (54%)
  Pallas kernels  13.4 us (32%)
  waiting for transfers between devices  4.86 us (12%)
  between operations  0.73 us (2%)
    pallas_call x8, Pallas kernels, run(): kernel(*(pltpu.with_memory_space_constraint(x, pltpu.HBM) if n in far els...  13.4 us
    ppermute x3, starting transfers between devices, swap(): far = lax.ppermute(far, axis, pairs[1])  13.3 us
    all_to_all x1, starting transfers between devices, on_device(): lax.all_to_all(blocks, 'lon', split_axis=0, concat_axis=0, tiled=True)  5.69 us
    all_to_all x1, starting transfers between devices, on_device(): lax.all_to_all(sums, 'lon', split_axis=0, concat_axis=0, tiled=True)  3.43 us
    ppermute x3, waiting for transfers between devices, swap(): far = lax.ppermute(far, axis, pairs[1])  3.24 us
    all_to_all x1, waiting for transfers between devices, on_device(): lax.all_to_all(blocks, 'lon', split_axis=0, concat_axis=0, tiled=True)  1.61 us
  transfers between devices with their start and end apart: 8, of which 3 were waited for; matrix products, arithmetic and copies ran while one was open for 0% of the time, Pallas kernels for 20%

profile of v3, /device:TPU:1, one launch (start us, length us, event | category | flops | bytes accessed | tf_op | source)
XLA Modules:
  0.0 41.6 jit_solution(339818652780279565)
XLA Ops:
  0.6 1.4 %pack_columns.1 = (f32[35,16,256]{2,1,0:T(8,128)S(1)}, f32[2,16,128]{2,1,0:T(8,128)S(1)}, f32[2,16,128]{2,1,0:T(8,128)S(1)}, f32[2,1,256,128]{3,2,1,0:T(8,128)S(1)}, s32[3,1,1,8,64]{4,3,2,1,0:T(8,128)S(1)}) custom-call(f32[2,4,16,256]{3,2,1,0:T(8,128)} %refs_0_.1, f32[2,4,16,256]{3,2,1,0:T(8,128)} %refs_1_.1, s32[4,16,256]{2,1,0:T(8,128)} %refs_2_.1, ...), custom_call_target="tpu_custom_call" | custom-call | bytes 1048576 | tf_op jit(solution)/shard_map/pack_columns/pallas_call | solution.py:45
  2.1 5.1 %collective-permute-start.1 = (f32[2,16,128]{2,1,0:T(8,128)S(1)}, f32[2,16,128]{2,1,0:T(8,128)S(1)}, u32[]{:S(2)}, u32[]{:S(2)}) collective-permute-start(f32[2,16,128]{2,1,0:T(8,128)S(1)} %get-tuple-element.25), channel_id=1, source_target_pairs={{1,2},{2,1},{3,4},{4,3},{5,6},{6,5},{7,0},{0,7},{9,10},{10,9},{11,... | collective-permute-start | bytes 49160 | tf_op jit(solution)/shard_map/ppermute | solution.py:71
  7.2 0.0 collective-permute-start
  7.2 3.7 %weigh.1 = (f32[8,72,128]{2,1,0:T(8,128)}, f32[40,128]{1,0:T(8,128)S(1)}, f32[8,512]{1,0:T(8,128)S(1)}) custom-call(f32[2,1,256,128]{3,2,1,0:T(8,128)S(1)} %get-tuple-element.26.atm_near, s32[3,1,1,8,64]{4,3,2,1,0:T(8,128)S(1)} %get-tuple-element.27.margins, f32[32,128,128]{2,1,0:T(8,128)} %weights.3, f32[2,16,128]{2,1,0:T(8,128)S(1)} %get-tuple-element.24.after), custom_call_target="tpu_custom_call" | custom-call | flops 4294967296 | bytes 1048576 | tf_op jit(solution)/shard_map/weigh/pallas_call | solution.py:45
  10.9 0.0 collective-permute-done.1.far_columns
  10.9 0.0 collective-permute-done.near_columns
  11.0 3.4 %all-to-all-start = ((f32[8,72,128]{2,1,0:T(8,128)}), f32[8,72,128]{2,1,0:T(8,128)S(1)}, u32[]{:S(2)}, u32[]{:S(2)}) async-start(f32[8,72,128]{2,1,0:T(8,128)} %get-tuple-element.35), calls=%async_computation | async-start | bytes 589824 | tf_op jit(solution)/shard_map/all_to_all | solution.py:626
  14.4 4.5 %collective-permute-start.2 = (f32[37,8,128]{2,1,0:T(8,128)S(1)}, f32[37,8,128]{2,1,0:T(8,128)S(1)}, u32[]{:S(2)}, u32[]{:S(2)}) collective-permute-start(f32[37,8,128]{2,1,0:T(8,128)S(1)} %get-tuple-element.31), channel_id=1, source_target_pairs={{8,16},{16,8},{9,17},{17,9},{10,18},{18,10},{11,19},{19,11},{12,20... | collective-permute-start | bytes 454664 | tf_op jit(solution)/shard_map/ppermute | solution.py:71
  19.0 0.1 collective-permute-start.3
  19.1 3.1 %collective-permute-done.2.far = f32[37,8,128]{2,1,0:T(8,128)S(1)} collective-permute-done((f32[37,8,128]{2,1,0:T(8,128)S(1)}, f32[37,8,128]{2,1,0:T(8,128)S(1)}, u32[]{:S(2)}, u32[]{:S(2)}) %collective-permute-start.2) | collective-permute-done | bytes 151584 | tf_op jit(solution)/shard_map/ppermute | solution.py:71
  22.1 0.0 collective-permute-done.3.near
  22.1 1.6 %run_adjoint.1 = (f32[8,64,128]{2,1,0:T(8,128)}, f32[6,4,24,384]{3,2,1,0:T(8,128)S(1)}, f32[16,24,384]{2,1,0:T(8,128)S(1)}, f32[2,3,4,24,384]{4,3,2,1,0:T(8,128)S(1)}) custom-call(f32[35,16,256]{2,1,0:T(8,128)S(1)} %get-tuple-element.23.fields, f32[2,16,128]{2,1,0:T(8,128)S(1)} %get-tuple-element.29.from_west, ...), custom_call_target="tpu_custom_call" | custom-call | bytes 1048576 | tf_op jit(solution)/shard_map/run_adjoint/pallas_call | solution.py:45
  23.8 0.0 all-to-all-done.received
  23.8 5.7 %all-to-all-start.1 = ((f32[8,64,128]{2,1,0:T(8,128)}), f32[8,64,128]{2,1,0:T(8,128)S(1)}, u32[]{:S(2)}, u32[]{:S(2)}) async-start(f32[8,64,128]{2,1,0:T(8,128)} %get-tuple-element.40), calls=%async_computation.1 | async-start | bytes 524288 | tf_op jit(solution)/shard_map/all_to_all | solution.py:644
  29.5 0.1 sum_forcing.1
  29.6 3.7 %collective-permute-start.4 = (f32[1,8,384]{2,1,0:T(8,128)S(1)}, f32[1,8,384]{2,1,0:T(8,128)S(1)}, u32[]{:S(2)}, u32[]{:S(2)}) collective-permute-start(f32[1,8,384]{2,1,0:T(8,128)S(1)} %get-tuple-element.37), channel_id=1, source_target_pairs={{8,16},{16,8},{9,17},{17,9},{10,18},{18,10},{11,19},{19,11},{12,20... | collective-permute-start | bytes 36872 | tf_op jit(solution)/shard_map/ppermute | solution.py:71
  33.3 0.1 collective-permute-start.5
  33.4 1.4 %finish_adjoint.1 = f32[2,4,16,256]{3,2,1,0:T(8,128)} custom-call(f32[6,4,24,384]{3,2,1,0:T(8,128)S(1)} %get-tuple-element.33.coeffs, f32[16,24,384]{2,1,0:T(8,128)S(1)} %get-tuple-element.34.start, f32[2,3,4,24,384]{4,3,2,1,0:T(8,128)S(1)} %get-tuple-element.39.states), custom_call_target="tpu_custom_call" | custom-call | bytes 1048576 | tf_op jit(solution)/shard_map/finish_adjoint/pallas_call | solution.py:45
  34.8 0.2 collective-permute-done.4.far
  34.9 0.0 collective-permute-done.5.near
  34.9 1.6 %run_forward.1 = f32[2,4,16,256]{3,2,1,0:T(8,128)} custom-call(f32[6,4,24,384]{3,2,1,0:T(8,128)S(1)} %get-tuple-element.33.coeffs, f32[16,24,384]{2,1,0:T(8,128)S(1)} %get-tuple-element.34.start, f32[2,16,384]{2,1,0:T(8,128)S(1)} %get-tuple-element.36.forcing, f32[1,8,384]{2,1,0:T(8,128)S(1)} %collective-permute-done.4.far, ...), custom_call_target="tpu_custom_call" | custom-call | bytes 1048576 | tf_op jit(solution)/shard_map/run_forward/pallas_call | solution.py:45
  36.5 1.6 %all-to-all-done.1.gathered = f32[8,64,128]{2,1,0:T(8,128)S(1)} async-done(((f32[8,64,128]{2,1,0:T(8,128)}), f32[8,64,128]{2,1,0:T(8,128)S(1)}, u32[]{:S(2)}, u32[]{:S(2)}) %all-to-all-start.1) | async-done | bytes 262176 | tf_op jit(solution)/shard_map/all_to_all | solution.py:644
  38.1 3.5 %unweigh.1 = f32[2,1,256,128]{3,2,1,0:T(8,128)} custom-call(f32[8,64,128]{2,1,0:T(8,128)S(1)} %all-to-all-done.1.gathered, f32[40,128]{1,0:T(8,128)S(1)} %get-tuple-element.41.found, f32[8,512]{1,0:T(8,128)S(1)} %get-tuple-element.42.keys, f32[32,128,128]{2,1,0:T(8,128)} %weights.3), custom_call_target="tpu_custom_call" | custom-call | flops 4294967296 | bytes 1048576 | tf_op jit(solution)/shard_map/unweigh/pallas_call | solution.py:45
  (1 shorter events, 0.0 us)
Async XLA Ops:
  2.1 8.8 %collective-permute-start.1 = (f32[2,16,128]{2,1,0:T(8,128)S(1)}, f32[2,16,128]{2,1,0:T(8,128)S(1)}, u32[]{:S(2)}, u32[]{:S(2)}) collective-permute-start(f32[2,16,128]{2,1,0:T(8,128)S(1)} %get-tuple-element.25), channel_id=1, source_target_pairs={{1,2},{2,1},{3,4},{4,3},{5,6},{6,5},{7,0},{0,7},{9,10},{10,9},{11,... | collective-permute-start | bytes 49160 | tf_op jit(solution)/shard_map/ppermute | solution.py:71
  7.2 3.7 %collective-permute-start = (f32[2,16,128]{2,1,0:T(8,128)S(1)}, f32[2,16,128]{2,1,0:T(8,128)S(1)}, u32[]{:S(2)}, u32[]{:S(2)}) collective-permute-start(f32[2,16,128]{2,1,0:T(8,128)S(1)} %get-tuple-element.24.after), channel_id=1, source_target_pairs={{0,1},{1,0},{2,3},{3,2},{4,5},{5,4},{6,7},{7,6},{8,9},{9,8},{10,11... | collective-permute-start | bytes 49160 | tf_op jit(solution)/shard_map/ppermute | solution.py:72
  11.0 12.8 %all-to-all-start = ((f32[8,72,128]{2,1,0:T(8,128)}), f32[8,72,128]{2,1,0:T(8,128)S(1)}, u32[]{:S(2)}, u32[]{:S(2)}) async-start(f32[8,72,128]{2,1,0:T(8,128)} %get-tuple-element.35), calls=%async_computation | async-start | bytes 589824 | tf_op jit(solution)/shard_map/all_to_all | solution.py:626
  14.4 7.7 %collective-permute-start.2 = (f32[37,8,128]{2,1,0:T(8,128)S(1)}, f32[37,8,128]{2,1,0:T(8,128)S(1)}, u32[]{:S(2)}, u32[]{:S(2)}) collective-permute-start(f32[37,8,128]{2,1,0:T(8,128)S(1)} %get-tuple-element.31), channel_id=1, source_target_pairs={{8,16},{16,8},{9,17},{17,9},{10,18},{18,10},{11,19},{19,11},{12,20... | collective-permute-start | bytes 454664 | tf_op jit(solution)/shard_map/ppermute | solution.py:71
  19.0 3.2 %collective-permute-start.3 = (f32[37,8,128]{2,1,0:T(8,128)S(1)}, f32[37,8,128]{2,1,0:T(8,128)S(1)}, u32[]{:S(2)}, u32[]{:S(2)}) collective-permute-start(f32[37,8,128]{2,1,0:T(8,128)S(1)} %get-tuple-element.32), channel_id=1, source_target_pairs={{0,8},{8,0},{16,24},{24,16},{1,9},{9,1},{17,25},{25,17},{2,10},{10... | collective-permute-start | bytes 454664 | tf_op jit(solution)/shard_map/ppermute | solution.py:72
  23.8 14.4 %all-to-all-start.1 = ((f32[8,64,128]{2,1,0:T(8,128)}), f32[8,64,128]{2,1,0:T(8,128)S(1)}, u32[]{:S(2)}, u32[]{:S(2)}) async-start(f32[8,64,128]{2,1,0:T(8,128)} %get-tuple-element.40), calls=%async_computation.1 | async-start | bytes 524288 | tf_op jit(solution)/shard_map/all_to_all | solution.py:644
  29.6 5.3 %collective-permute-start.4 = (f32[1,8,384]{2,1,0:T(8,128)S(1)}, f32[1,8,384]{2,1,0:T(8,128)S(1)}, u32[]{:S(2)}, u32[]{:S(2)}) collective-permute-start(f32[1,8,384]{2,1,0:T(8,128)S(1)} %get-tuple-element.37), channel_id=1, source_target_pairs={{8,16},{16,8},{9,17},{17,9},{10,18},{18,10},{11,19},{19,11},{12,20... | collective-permute-start | bytes 36872 | tf_op jit(solution)/shard_map/ppermute | solution.py:71
  33.3 1.7 %collective-permute-start.5 = (f32[1,8,384]{2,1,0:T(8,128)S(1)}, f32[1,8,384]{2,1,0:T(8,128)S(1)}, u32[]{:S(2)}, u32[]{:S(2)}) collective-permute-start(f32[1,8,384]{2,1,0:T(8,128)S(1)} %get-tuple-element.38), channel_id=1, source_target_pairs={{0,8},{8,0},{16,24},{24,16},{1,9},{9,1},{17,25},{25,17},{2,10},{10... | collective-permute-start | bytes 36872 | tf_op jit(solution)/shard_map/ppermute | solution.py:72

commit v4 on v3

--- a/solution.py
+++ b/solution.py
@@ -60,6 +60,16 @@
 def turn(x, shift, axis):
     shift %= x.shape[axis]
     return pltpu.roll(x, shift, axis) if shift else x
+
+
+def group_order(count):
+    middle = count // 2
+    return [middle] + [k for k in range(count) if k != middle]
+
+
+def exchange(x):
+    order = group_order(x.shape[0])
+    return lax.all_to_all(x, "lon", split_axis=0, concat_axis=0, tiled=True, axis_index_groups=[order])
 
 
 def swap(near, far, axis, wrap):
@@ -495,11 +505,11 @@
         at = (2 * k + h) * tile_lat
         return result[at : at + tile_lat, f * BLOCK : (f + 1) * BLOCK]
 
-    for k in range(lon_count):
+    for n, k in enumerate(group_order(lon_count)):
         edge = jnp.zeros((tile_lat, BLOCK), f32)
         for f in range(2):
             for h in range(2):
-                sums[k, (2 * f + h) * tile_lat : (2 * f + h + 1) * tile_lat] = block_sums(k, f, h)
+                sums[n, (2 * f + h) * tile_lat : (2 * f + h + 1) * tile_lat] = block_sums(k, f, h)
             at = f * HALO
             after = turn(block_sums((k + 1) % lon_count, f, 0), at, 1)
             before = turn(block_sums((k - 1) % lon_count, f, 1), -at, 1)
@@ -509,7 +519,7 @@
         upper, lower = edge[: tile_lat // 2], edge[tile_lat // 2 :]
         near = lane[: tile_lat // 2]
         lower = jnp.where(near < BLOCK // 2, turn(lower, 2 * HALO, 1), turn(lower, -2 * HALO, 1))
-        sums[k, 4 * tile_lat :] = jnp.where((near < 2 * HALO) | (near >= BLOCK - 2 * HALO), upper, lower)
+        sums[n, 4 * tile_lat :] = jnp.where((near < 2 * HALO) | (near >= BLOCK - 2 * HALO), upper, lower)
 
 
 def unweigh(gathered, found, keys, weights, gradient, result, codes, *scratch):
@@ -518,12 +528,14 @@
     atm = gradient.shape[2]
     blocks = weights.shape[0]
     lon_count, ocean_blocks = gathered.shape[0], gathered.shape[1] // 2
+    order = group_order(lon_count)
     capacity = places(keys.shape[1], blocks)
     rounds = jnp.max(keys[2:3]).astype(jnp.int32) // capacity + 1
     parts = [
         split(
             jnp.concatenate(
-                [gathered[k, f * ocean_blocks : (f + 1) * ocean_blocks] for k in range(lon_count)], axis=0
+                [gathered[order.index(k), f * ocean_blocks : (f + 1) * ocean_blocks] for k in range(lon_count)],
+                axis=0,
             )
         )
         for f in range(2)
@@ -623,7 +635,7 @@
         inputs=4,
         aliases={3: 4},
     )(fields, near_columns, far_columns, sums)
-    received = lax.all_to_all(sums, "lon", split_axis=0, concat_axis=0, tiled=True)
+    received = exchange(sums)
     near_rows, far_rows = swap(near, far, "lat", False)
 
     wide = (tile_lat + 8, tile_lon + BLOCK)
@@ -641,7 +653,7 @@
         inputs=5,
         far_outs=(0,),
     )(fields, from_west, from_east, far_rows, near_rows)
-    gathered = lax.all_to_all(blocks, "lon", split_axis=0, concat_axis=0, tiled=True)
+    gathered = exchange(blocks)
 
     message = (1, 8, tile_lon + BLOCK)
     forcing, near, far = call(

time: 42.2 us -> 42.2 us (level)
  the two profiles are of different devices: /device:TPU:1 before, /device:TPU:0 now
where the time goes in v4:
time: 42.2 us; the launch traced here: 41.8 us
  starting transfers between devices  24.6 us (58%)
  Pallas kernels  13.4 us (32%)
  waiting for transfers between devices  3.08 us (7%)
  between operations  0.69 us (2%)
    pallas_call x8, Pallas kernels, run(): kernel(*(pltpu.with_memory_space_constraint(x, pltpu.HBM) if n in far els...  13.4 us
    all_to_all x2, starting transfers between devices, exchange(): lax.all_to_all(x, 'lon', split_axis=0, concat_axis=0, tiled=True, axis_in...  10.4 us
    ppermute x3, starting transfers between devices, swap(): far = lax.ppermute(far, axis, pairs[1])  7.35 us
    ppermute x3, starting transfers between devices, swap(): return (lax.ppermute(near, axis, pairs[0]), far)  6.8 us
    all_to_all x2, waiting for transfers between devices, exchange(): lax.all_to_all(x, 'lon', split_axis=0, concat_axis=0, tiled=True, axis_in...  2.03 us
    ppermute x3, waiting for transfers between devices, swap(): return (lax.ppermute(near, axis, pairs[0]), far)  1.05 us
  transfers between devices with their start and end apart: 8, of which 3 were waited for; matrix products, arithmetic and copies ran while one was open for 0% of the time, Pallas kernels for 20%

profile of v4, /device:TPU:0, one launch (start us, length us, event | category | flops | bytes accessed | tf_op | source)
XLA Modules:
  0.0 41.8 jit_solution(4337032578896607486)
XLA Ops:
  0.6 1.4 %pack_columns.1 = (f32[35,16,256]{2,1,0:T(8,128)S(1)}, f32[2,16,128]{2,1,0:T(8,128)S(1)}, f32[2,16,128]{2,1,0:T(8,128)S(1)}, f32[2,1,256,128]{3,2,1,0:T(8,128)S(1)}, s32[3,1,1,8,64]{4,3,2,1,0:T(8,128)S(1)}) custom-call(f32[2,4,16,256]{3,2,1,0:T(8,128)} %refs_0_.1, f32[2,4,16,256]{3,2,1,0:T(8,128)} %refs_1_.1, s32[4,16,256]{2,1,0:T(8,128)} %refs_2_.1, ...), custom_call_target="tpu_custom_call" | custom-call | bytes 1048576 | tf_op jit(solution)/shard_map/pack_columns/pallas_call | solution.py:45
  2.1 6.0 %collective-permute-start.1 = (f32[2,16,128]{2,1,0:T(8,128)S(1)}, f32[2,16,128]{2,1,0:T(8,128)S(1)}, u32[]{:S(2)}, u32[]{:S(2)}) collective-permute-start(f32[2,16,128]{2,1,0:T(8,128)S(1)} %get-tuple-element.25), channel_id=1, source_target_pairs={{1,2},{2,1},{3,4},{4,3},{5,6},{6,5},{7,0},{0,7},{9,10},{10,9},{11,... | collective-permute-start | bytes 49160 | tf_op jit(solution)/shard_map/ppermute | solution.py:81
  8.1 0.0 collective-permute-start
  8.1 3.7 %weigh.1 = (f32[8,72,128]{2,1,0:T(8,128)}, f32[40,128]{1,0:T(8,128)S(1)}, f32[8,512]{1,0:T(8,128)S(1)}) custom-call(f32[2,1,256,128]{3,2,1,0:T(8,128)S(1)} %get-tuple-element.26.atm_near, s32[3,1,1,8,64]{4,3,2,1,0:T(8,128)S(1)} %get-tuple-element.27.margins, f32[32,128,128]{2,1,0:T(8,128)} %weights.3, f32[2,16,128]{2,1,0:T(8,128)S(1)} %get-tuple-element.24.after), custom_call_target="tpu_custom_call" | custom-call | flops 4294967296 | bytes 1048576 | tf_op jit(solution)/shard_map/weigh/pallas_call | solution.py:45
  11.8 0.0 collective-permute-done.1.far_columns
  11.8 0.0 collective-permute-done.near_columns
  11.9 5.6 %all-to-all-start = ((f32[8,72,128]{2,1,0:T(8,128)}), f32[8,72,128]{2,1,0:T(8,128)S(1)}, u32[]{:S(2)}, u32[]{:S(2)}) async-start(f32[8,72,128]{2,1,0:T(8,128)} %get-tuple-element.35), calls=%async_computation | async-start | bytes 589824 | tf_op jit(solution)/shard_map/all_to_all | solution.py:72
  17.6 0.7 %collective-permute-start.2 = (f32[37,8,128]{2,1,0:T(8,128)S(1)}, f32[37,8,128]{2,1,0:T(8,128)S(1)}, u32[]{:S(2)}, u32[]{:S(2)}) collective-permute-start(f32[37,8,128]{2,1,0:T(8,128)S(1)} %get-tuple-element.31), channel_id=1, source_target_pairs={{8,16},{16,8},{9,17},{17,9},{10,18},{18,10},{11,19},{19,11},{12,20... | collective-permute-start | bytes 454664 | tf_op jit(solution)/shard_map/ppermute | solution.py:81
  18.2 2.9 %collective-permute-start.3 = (f32[37,8,128]{2,1,0:T(8,128)S(1)}, f32[37,8,128]{2,1,0:T(8,128)S(1)}, u32[]{:S(2)}, u32[]{:S(2)}) collective-permute-start(f32[37,8,128]{2,1,0:T(8,128)S(1)} %get-tuple-element.32), channel_id=1, source_target_pairs={{0,8},{8,0},{16,24},{24,16},{1,9},{9,1},{17,25},{25,17},{2,10},{10... | collective-permute-start | bytes 454664 | tf_op jit(solution)/shard_map/ppermute | solution.py:82
  21.2 0.0 collective-permute-done.2.far
  21.2 1.0 %collective-permute-done.3.near = f32[37,8,128]{2,1,0:T(8,128)S(1)} collective-permute-done((f32[37,8,128]{2,1,0:T(8,128)S(1)}, f32[37,8,128]{2,1,0:T(8,128)S(1)}, u32[]{:S(2)}, u32[]{:S(2)}) %collective-permute-start.3) | collective-permute-done | bytes 151584 | tf_op jit(solution)/shard_map/ppermute | solution.py:82
  22.2 1.6 %run_adjoint.1 = (f32[8,64,128]{2,1,0:T(8,128)}, f32[6,4,24,384]{3,2,1,0:T(8,128)S(1)}, f32[16,24,384]{2,1,0:T(8,128)S(1)}, f32[2,3,4,24,384]{4,3,2,1,0:T(8,128)S(1)}) custom-call(f32[35,16,256]{2,1,0:T(8,128)S(1)} %get-tuple-element.23.fields, f32[2,16,128]{2,1,0:T(8,128)S(1)} %get-tuple-element.29.from_west, ...), custom_call_target="tpu_custom_call" | custom-call | bytes 1048576 | tf_op jit(solution)/shard_map/run_adjoint/pallas_call | solution.py:45
  23.8 1.3 %all-to-all-done.received = f32[8,72,128]{2,1,0:T(8,128)S(1)} async-done(((f32[8,72,128]{2,1,0:T(8,128)}), f32[8,72,128]{2,1,0:T(8,128)S(1)}, u32[]{:S(2)}, u32[]{:S(2)}) %all-to-all-start) | async-done | bytes 294944 | tf_op jit(solution)/shard_map/all_to_all | solution.py:72
  25.1 4.8 %all-to-all-start.1 = ((f32[8,64,128]{2,1,0:T(8,128)}), f32[8,64,128]{2,1,0:T(8,128)S(1)}, u32[]{:S(2)}, u32[]{:S(2)}) async-start(f32[8,64,128]{2,1,0:T(8,128)} %get-tuple-element.40), calls=%async_computation.1 | async-start | bytes 524288 | tf_op jit(solution)/shard_map/all_to_all | solution.py:72
  29.9 0.1 sum_forcing.1
  30.0 0.7 %collective-permute-start.4 = (f32[1,8,384]{2,1,0:T(8,128)S(1)}, f32[1,8,384]{2,1,0:T(8,128)S(1)}, u32[]{:S(2)}, u32[]{:S(2)}) collective-permute-start(f32[1,8,384]{2,1,0:T(8,128)S(1)} %get-tuple-element.37), channel_id=1, source_target_pairs={{8,16},{16,8},{9,17},{17,9},{10,18},{18,10},{11,19},{19,11},{12,20... | collective-permute-start | bytes 36872 | tf_op jit(solution)/shard_map/ppermute | solution.py:81
  30.7 3.9 %collective-permute-start.5 = (f32[1,8,384]{2,1,0:T(8,128)S(1)}, f32[1,8,384]{2,1,0:T(8,128)S(1)}, u32[]{:S(2)}, u32[]{:S(2)}) collective-permute-start(f32[1,8,384]{2,1,0:T(8,128)S(1)} %get-tuple-element.38), channel_id=1, source_target_pairs={{0,8},{8,0},{16,24},{24,16},{1,9},{9,1},{17,25},{25,17},{2,10},{10... | collective-permute-start | bytes 36872 | tf_op jit(solution)/shard_map/ppermute | solution.py:82
  34.5 1.4 %finish_adjoint.1 = f32[2,4,16,256]{3,2,1,0:T(8,128)} custom-call(f32[6,4,24,384]{3,2,1,0:T(8,128)S(1)} %get-tuple-element.33.coeffs, f32[16,24,384]{2,1,0:T(8,128)S(1)} %get-tuple-element.34.start, f32[2,3,4,24,384]{4,3,2,1,0:T(8,128)S(1)} %get-tuple-element.39.states), custom_call_target="tpu_custom_call" | custom-call | bytes 1048576 | tf_op jit(solution)/shard_map/finish_adjoint/pallas_call | solution.py:45
  36.0 0.0 collective-permute-done.4.far
  36.0 0.0 collective-permute-done.5.near
  36.0 1.6 %run_forward.1 = f32[2,4,16,256]{3,2,1,0:T(8,128)} custom-call(f32[6,4,24,384]{3,2,1,0:T(8,128)S(1)} %get-tuple-element.33.coeffs, f32[16,24,384]{2,1,0:T(8,128)S(1)} %get-tuple-element.34.start, f32[2,16,384]{2,1,0:T(8,128)S(1)} %get-tuple-element.36.forcing, f32[1,8,384]{2,1,0:T(8,128)S(1)} %collective-permute-done.4.far, ...), custom_call_target="tpu_custom_call" | custom-call | bytes 1048576 | tf_op jit(solution)/shard_map/run_forward/pallas_call | solution.py:45
  37.5 0.7 %all-to-all-done.1.gathered = f32[8,64,128]{2,1,0:T(8,128)S(1)} async-done(((f32[8,64,128]{2,1,0:T(8,128)}), f32[8,64,128]{2,1,0:T(8,128)S(1)}, u32[]{:S(2)}, u32[]{:S(2)}) %all-to-all-start.1) | async-done | bytes 262176 | tf_op jit(solution)/shard_map/all_to_all | solution.py:72
  38.3 3.5 %unweigh.1 = f32[2,1,256,128]{3,2,1,0:T(8,128)} custom-call(f32[8,64,128]{2,1,0:T(8,128)S(1)} %all-to-all-done.1.gathered, f32[40,128]{1,0:T(8,128)S(1)} %get-tuple-element.41.found, f32[8,512]{1,0:T(8,128)S(1)} %get-tuple-element.42.keys, f32[32,128,128]{2,1,0:T(8,128)} %weights.3), custom_call_target="tpu_custom_call" | custom-call | flops 4294967296 | bytes 1048576 | tf_op jit(solution)/shard_map/unweigh/pallas_call | solution.py:45
  (1 shorter events, 0.0 us)
Async XLA Ops:
  2.1 9.7 %collective-permute-start.1 = (f32[2,16,128]{2,1,0:T(8,128)S(1)}, f32[2,16,128]{2,1,0:T(8,128)S(1)}, u32[]{:S(2)}, u32[]{:S(2)}) collective-permute-start(f32[2,16,128]{2,1,0:T(8,128)S(1)} %get-tuple-element.25), channel_id=1, source_target_pairs={{1,2},{2,1},{3,4},{4,3},{5,6},{6,5},{7,0},{0,7},{9,10},{10,9},{11,... | collective-permute-start | bytes 49160 | tf_op jit(solution)/shard_map/ppermute | solution.py:81
  8.1 3.7 %collective-permute-start = (f32[2,16,128]{2,1,0:T(8,128)S(1)}, f32[2,16,128]{2,1,0:T(8,128)S(1)}, u32[]{:S(2)}, u32[]{:S(2)}) collective-permute-start(f32[2,16,128]{2,1,0:T(8,128)S(1)} %get-tuple-element.24.after), channel_id=1, source_target_pairs={{0,1},{1,0},{2,3},{3,2},{4,5},{5,4},{6,7},{7,6},{8,9},{9,8},{10,11... | collective-permute-start | bytes 49160 | tf_op jit(solution)/shard_map/ppermute | solution.py:82
  11.9 13.2 %all-to-all-start = ((f32[8,72,128]{2,1,0:T(8,128)}), f32[8,72,128]{2,1,0:T(8,128)S(1)}, u32[]{:S(2)}, u32[]{:S(2)}) async-start(f32[8,72,128]{2,1,0:T(8,128)} %get-tuple-element.35), calls=%async_computation | async-start | bytes 589824 | tf_op jit(solution)/shard_map/all_to_all | solution.py:72
  17.6 3.6 %collective-permute-start.2 = (f32[37,8,128]{2,1,0:T(8,128)S(1)}, f32[37,8,128]{2,1,0:T(8,128)S(1)}, u32[]{:S(2)}, u32[]{:S(2)}) collective-permute-start(f32[37,8,128]{2,1,0:T(8,128)S(1)} %get-tuple-element.31), channel_id=1, source_target_pairs={{8,16},{16,8},{9,17},{17,9},{10,18},{18,10},{11,19},{19,11},{12,20... | collective-permute-start | bytes 454664 | tf_op jit(solution)/shard_map/ppermute | solution.py:81
  18.2 4.0 %collective-permute-start.3 = (f32[37,8,128]{2,1,0:T(8,128)S(1)}, f32[37,8,128]{2,1,0:T(8,128)S(1)}, u32[]{:S(2)}, u32[]{:S(2)}) collective-permute-start(f32[37,8,128]{2,1,0:T(8,128)S(1)} %get-tuple-element.32), channel_id=1, source_target_pairs={{0,8},{8,0},{16,24},{24,16},{1,9},{9,1},{17,25},{25,17},{2,10},{10... | collective-permute-start | bytes 454664 | tf_op jit(solution)/shard_map/ppermute | solution.py:82
  25.1 13.2 %all-to-all-start.1 = ((f32[8,64,128]{2,1,0:T(8,128)}), f32[8,64,128]{2,1,0:T(8,128)S(1)}, u32[]{:S(2)}, u32[]{:S(2)}) async-start(f32[8,64,128]{2,1,0:T(8,128)} %get-tuple-element.40), calls=%async_computation.1 | async-start | bytes 524288 | tf_op jit(solution)/shard_map/all_to_all | solution.py:72
  30.0 5.9 %collective-permute-start.4 = (f32[1,8,384]{2,1,0:T(8,128)S(1)}, f32[1,8,384]{2,1,0:T(8,128)S(1)}, u32[]{:S(2)}, u32[]{:S(2)}) collective-permute-start(f32[1,8,384]{2,1,0:T(8,128)S(1)} %get-tuple-element.37), channel_id=1, source_target_pairs={{8,16},{16,8},{9,17},{17,9},{10,18},{18,10},{11,19},{19,11},{12,20... | collective-permute-start | bytes 36872 | tf_op jit(solution)/shard_map/ppermute | solution.py:81
  30.7 5.3 %collective-permute-start.5 = (f32[1,8,384]{2,1,0:T(8,128)S(1)}, f32[1,8,384]{2,1,0:T(8,128)S(1)}, u32[]{:S(2)}, u32[]{:S(2)}) collective-permute-start(f32[1,8,384]{2,1,0:T(8,128)S(1)} %get-tuple-element.38), channel_id=1, source_target_pairs={{0,8},{8,0},{16,24},{24,16},{1,9},{9,1},{17,25},{25,17},{2,10},{10... | collective-permute-start | bytes 36872 | tf_op jit(solution)/shard_map/ppermute | solution.py:82

commit v5 on v4

--- a/solution.py
+++ b/solution.py
@@ -63,8 +63,8 @@
 
 
 def group_order(count):
-    middle = count // 2
-    return [middle] + [k for k in range(count) if k != middle]
+    half = count // 2
+    return [k for n in range(half) for k in (half + n, n)]
 
 
 def exchange(x):

time: 42.2 us -> 41.5 us (0.983)
  the two profiles are of different devices: /device:TPU:0 before, /device:TPU:1 now
where the time goes in v5:
time: 41.5 us; the launch traced here: 40.7 us
  starting transfers between devices  23.6 us (57%)
  Pallas kernels  13.4 us (32%)
  waiting for transfers between devices  2.97 us (7%)
  between operations  0.73 us (2%)
    ppermute x3, starting transfers between devices, swap(): far = lax.ppermute(far, axis, pairs[1])  13.9 us
    pallas_call x8, Pallas kernels, run(): kernel(*(pltpu.with_memory_space_constraint(x, pltpu.HBM) if n in far els...  13.4 us
    all_to_all x2, starting transfers between devices, exchange(): lax.all_to_all(x, 'lon', split_axis=0, concat_axis=0, tiled=True, axis_in...  9.58 us
    ppermute x3, waiting for transfers between devices, swap(): far = lax.ppermute(far, axis, pairs[1])  2.96 us
  transfers between devices with their start and end apart: 8, of which 2 were waited for; matrix products, arithmetic and copies ran while one was open for 0% of the time, Pallas kernels for 21%

profile of v5, /device:TPU:1, one launch (start us, length us, event | category | flops | bytes accessed | tf_op | source)
XLA Modules:
  0.0 40.7 jit_solution(10508978914146058632)
XLA Ops:
  0.6 1.4 %pack_columns.1 = (f32[35,16,256]{2,1,0:T(8,128)S(1)}, f32[2,16,128]{2,1,0:T(8,128)S(1)}, f32[2,16,128]{2,1,0:T(8,128)S(1)}, f32[2,1,256,128]{3,2,1,0:T(8,128)S(1)}, s32[3,1,1,8,64]{4,3,2,1,0:T(8,128)S(1)}) custom-call(f32[2,4,16,256]{3,2,1,0:T(8,128)} %refs_0_.1, f32[2,4,16,256]{3,2,1,0:T(8,128)} %refs_1_.1, s32[4,16,256]{2,1,0:T(8,128)} %refs_2_.1, ...), custom_call_target="tpu_custom_call" | custom-call | bytes 1048576 | tf_op jit(solution)/shard_map/pack_columns/pallas_call | solution.py:45
  2.1 5.1 %collective-permute-start.1 = (f32[2,16,128]{2,1,0:T(8,128)S(1)}, f32[2,16,128]{2,1,0:T(8,128)S(1)}, u32[]{:S(2)}, u32[]{:S(2)}) collective-permute-start(f32[2,16,128]{2,1,0:T(8,128)S(1)} %get-tuple-element.25), channel_id=1, source_target_pairs={{1,2},{2,1},{3,4},{4,3},{5,6},{6,5},{7,0},{0,7},{9,10},{10,9},{11,... | collective-permute-start | bytes 49160 | tf_op jit(solution)/shard_map/ppermute | solution.py:81
  7.2 0.0 collective-permute-start
  7.2 3.7 %weigh.1 = (f32[8,72,128]{2,1,0:T(8,128)}, f32[40,128]{1,0:T(8,128)S(1)}, f32[8,512]{1,0:T(8,128)S(1)}) custom-call(f32[2,1,256,128]{3,2,1,0:T(8,128)S(1)} %get-tuple-element.26.atm_near, s32[3,1,1,8,64]{4,3,2,1,0:T(8,128)S(1)} %get-tuple-element.27.margins, f32[32,128,128]{2,1,0:T(8,128)} %weights.3, f32[2,16,128]{2,1,0:T(8,128)S(1)} %get-tuple-element.24.after), custom_call_target="tpu_custom_call" | custom-call | flops 4294967296 | bytes 1048576 | tf_op jit(solution)/shard_map/weigh/pallas_call | solution.py:45
  10.9 0.0 collective-permute-done.1.far_columns
  10.9 0.0 collective-permute-done.near_columns
  11.0 4.8 %all-to-all-start = ((f32[8,72,128]{2,1,0:T(8,128)}), f32[8,72,128]{2,1,0:T(8,128)S(1)}, u32[]{:S(2)}, u32[]{:S(2)}) async-start(f32[8,72,128]{2,1,0:T(8,128)} %get-tuple-element.35), calls=%async_computation | async-start | bytes 589824 | tf_op jit(solution)/shard_map/all_to_all | solution.py:72
  15.8 4.8 %collective-permute-start.2 = (f32[37,8,128]{2,1,0:T(8,128)S(1)}, f32[37,8,128]{2,1,0:T(8,128)S(1)}, u32[]{:S(2)}, u32[]{:S(2)}) collective-permute-start(f32[37,8,128]{2,1,0:T(8,128)S(1)} %get-tuple-element.31), channel_id=1, source_target_pairs={{8,16},{16,8},{9,17},{17,9},{10,18},{18,10},{11,19},{19,11},{12,20... | collective-permute-start | bytes 454664 | tf_op jit(solution)/shard_map/ppermute | solution.py:81
  20.6 0.1 collective-permute-start.3
  20.7 2.9 %collective-permute-done.2.far = f32[37,8,128]{2,1,0:T(8,128)S(1)} collective-permute-done((f32[37,8,128]{2,1,0:T(8,128)S(1)}, f32[37,8,128]{2,1,0:T(8,128)S(1)}, u32[]{:S(2)}, u32[]{:S(2)}) %collective-permute-start.2) | collective-permute-done | bytes 151584 | tf_op jit(solution)/shard_map/ppermute | solution.py:81
  23.6 0.0 collective-permute-done.3.near
  23.6 1.6 %run_adjoint.1 = (f32[8,64,128]{2,1,0:T(8,128)}, f32[6,4,24,384]{3,2,1,0:T(8,128)S(1)}, f32[16,24,384]{2,1,0:T(8,128)S(1)}, f32[2,3,4,24,384]{4,3,2,1,0:T(8,128)S(1)}) custom-call(f32[35,16,256]{2,1,0:T(8,128)S(1)} %get-tuple-element.23.fields, f32[2,16,128]{2,1,0:T(8,128)S(1)} %get-tuple-element.29.from_west, ...), custom_call_target="tpu_custom_call" | custom-call | bytes 1048576 | tf_op jit(solution)/shard_map/run_adjoint/pallas_call | solution.py:45
  25.2 0.0 all-to-all-done.received
  25.2 4.8 %all-to-all-start.1 = ((f32[8,64,128]{2,1,0:T(8,128)}), f32[8,64,128]{2,1,0:T(8,128)S(1)}, u32[]{:S(2)}, u32[]{:S(2)}) async-start(f32[8,64,128]{2,1,0:T(8,128)} %get-tuple-element.40), calls=%async_computation.1 | async-start | bytes 524288 | tf_op jit(solution)/shard_map/all_to_all | solution.py:72
  30.0 0.1 sum_forcing.1
  30.1 3.9 %collective-permute-start.4 = (f32[1,8,384]{2,1,0:T(8,128)S(1)}, f32[1,8,384]{2,1,0:T(8,128)S(1)}, u32[]{:S(2)}, u32[]{:S(2)}) collective-permute-start(f32[1,8,384]{2,1,0:T(8,128)S(1)} %get-tuple-element.37), channel_id=1, source_target_pairs={{8,16},{16,8},{9,17},{17,9},{10,18},{18,10},{11,19},{19,11},{12,20... | collective-permute-start | bytes 36872 | tf_op jit(solution)/shard_map/ppermute | solution.py:81
  34.0 0.1 collective-permute-start.5
  34.1 1.4 %finish_adjoint.1 = f32[2,4,16,256]{3,2,1,0:T(8,128)} custom-call(f32[6,4,24,384]{3,2,1,0:T(8,128)S(1)} %get-tuple-element.33.coeffs, f32[16,24,384]{2,1,0:T(8,128)S(1)} %get-tuple-element.34.start, f32[2,3,4,24,384]{4,3,2,1,0:T(8,128)S(1)} %get-tuple-element.39.states), custom_call_target="tpu_custom_call" | custom-call | bytes 1048576 | tf_op jit(solution)/shard_map/finish_adjoint/pallas_call | solution.py:45
  35.5 0.1 collective-permute-done.4.far
  35.6 0.0 collective-permute-done.5.near
  35.6 1.6 %run_forward.1 = f32[2,4,16,256]{3,2,1,0:T(8,128)} custom-call(f32[6,4,24,384]{3,2,1,0:T(8,128)S(1)} %get-tuple-element.33.coeffs, f32[16,24,384]{2,1,0:T(8,128)S(1)} %get-tuple-element.34.start, f32[2,16,384]{2,1,0:T(8,128)S(1)} %get-tuple-element.36.forcing, f32[1,8,384]{2,1,0:T(8,128)S(1)} %collective-permute-done.4.far, ...), custom_call_target="tpu_custom_call" | custom-call | bytes 1048576 | tf_op jit(solution)/shard_map/run_forward/pallas_call | solution.py:45
  37.2 0.0 all-to-all-done.1.gathered
  37.2 3.5 %unweigh.1 = f32[2,1,256,128]{3,2,1,0:T(8,128)} custom-call(f32[8,64,128]{2,1,0:T(8,128)S(1)} %all-to-all-done.1.gathered, f32[40,128]{1,0:T(8,128)S(1)} %get-tuple-element.41.found, f32[8,512]{1,0:T(8,128)S(1)} %get-tuple-element.42.keys, f32[32,128,128]{2,1,0:T(8,128)} %weights.3), custom_call_target="tpu_custom_call" | custom-call | flops 4294967296 | bytes 1048576 | tf_op jit(solution)/shard_map/unweigh/pallas_call | solution.py:45
  (1 shorter events, 0.0 us)
Async XLA Ops:
  2.1 8.8 %collective-permute-start.1 = (f32[2,16,128]{2,1,0:T(8,128)S(1)}, f32[2,16,128]{2,1,0:T(8,128)S(1)}, u32[]{:S(2)}, u32[]{:S(2)}) collective-permute-start(f32[2,16,128]{2,1,0:T(8,128)S(1)} %get-tuple-element.25), channel_id=1, source_target_pairs={{1,2},{2,1},{3,4},{4,3},{5,6},{6,5},{7,0},{0,7},{9,10},{10,9},{11,... | collective-permute-start | bytes 49160 | tf_op jit(solution)/shard_map/ppermute | solution.py:81
  7.2 3.7 %collective-permute-start = (f32[2,16,128]{2,1,0:T(8,128)S(1)}, f32[2,16,128]{2,1,0:T(8,128)S(1)}, u32[]{:S(2)}, u32[]{:S(2)}) collective-permute-start(f32[2,16,128]{2,1,0:T(8,128)S(1)} %get-tuple-element.24.after), channel_id=1, source_target_pairs={{0,1},{1,0},{2,3},{3,2},{4,5},{5,4},{6,7},{7,6},{8,9},{9,8},{10,11... | collective-permute-start | bytes 49160 | tf_op jit(solution)/shard_map/ppermute | solution.py:82
  11.0 14.2 %all-to-all-start = ((f32[8,72,128]{2,1,0:T(8,128)}), f32[8,72,128]{2,1,0:T(8,128)S(1)}, u32[]{:S(2)}, u32[]{:S(2)}) async-start(f32[8,72,128]{2,1,0:T(8,128)} %get-tuple-element.35), calls=%async_computation | async-start | bytes 589824 | tf_op jit(solution)/shard_map/all_to_all | solution.py:72
  15.8 7.8 %collective-permute-start.2 = (f32[37,8,128]{2,1,0:T(8,128)S(1)}, f32[37,8,128]{2,1,0:T(8,128)S(1)}, u32[]{:S(2)}, u32[]{:S(2)}) collective-permute-start(f32[37,8,128]{2,1,0:T(8,128)S(1)} %get-tuple-element.31), channel_id=1, source_target_pairs={{8,16},{16,8},{9,17},{17,9},{10,18},{18,10},{11,19},{19,11},{12,20... | collective-permute-start | bytes 454664 | tf_op jit(solution)/shard_map/ppermute | solution.py:81
  20.6 2.9 %collective-permute-start.3 = (f32[37,8,128]{2,1,0:T(8,128)S(1)}, f32[37,8,128]{2,1,0:T(8,128)S(1)}, u32[]{:S(2)}, u32[]{:S(2)}) collective-permute-start(f32[37,8,128]{2,1,0:T(8,128)S(1)} %get-tuple-element.32), channel_id=1, source_target_pairs={{0,8},{8,0},{16,24},{24,16},{1,9},{9,1},{17,25},{25,17},{2,10},{10... | collective-permute-start | bytes 454664 | tf_op jit(solution)/shard_map/ppermute | solution.py:82
  25.2 12.0 %all-to-all-start.1 = ((f32[8,64,128]{2,1,0:T(8,128)}), f32[8,64,128]{2,1,0:T(8,128)S(1)}, u32[]{:S(2)}, u32[]{:S(2)}) async-start(f32[8,64,128]{2,1,0:T(8,128)} %get-tuple-element.40), calls=%async_computation.1 | async-start | bytes 524288 | tf_op jit(solution)/shard_map/all_to_all | solution.py:72
  30.1 5.5 %collective-permute-start.4 = (f32[1,8,384]{2,1,0:T(8,128)S(1)}, f32[1,8,384]{2,1,0:T(8,128)S(1)}, u32[]{:S(2)}, u32[]{:S(2)}) collective-permute-start(f32[1,8,384]{2,1,0:T(8,128)S(1)} %get-tuple-element.37), channel_id=1, source_target_pairs={{8,16},{16,8},{9,17},{17,9},{10,18},{18,10},{11,19},{19,11},{12,20... | collective-permute-start | bytes 36872 | tf_op jit(solution)/shard_map/ppermute | solution.py:81
  34.0 1.6 %collective-permute-start.5 = (f32[1,8,384]{2,1,0:T(8,128)S(1)}, f32[1,8,384]{2,1,0:T(8,128)S(1)}, u32[]{:S(2)}, u32[]{:S(2)}) collective-permute-start(f32[1,8,384]{2,1,0:T(8,128)S(1)} %get-tuple-element.38), channel_id=1, source_target_pairs={{0,8},{8,0},{16,24},{24,16},{1,9},{9,1},{17,25},{25,17},{2,10},{10... | collective-permute-start | bytes 36872 | tf_op jit(solution)/shard_map/ppermute | solution.py:82

commit v6 on v5

--- a/solution.py
+++ b/solution.py
@@ -623,7 +623,7 @@
         name="weigh",
         inputs=4,
         far=(2,),
-    )(atm_near, margins_near, weights, near)
+    )(atm_near, margins_near, weights, far)
 
     sources = count * halves + 2 * parts
     message = (-(-sources // 2), 8, BLOCK)

time: 41.5 us -> 40.9 us (0.986)
  starting transfers between devices: 23.6 us -> 23.1 us
    ppermute x3, starting transfers between devices: 0.14 us -> 2.25 us  [swap(): return (lax.ppermute(near, axis, pairs[0]), far)]
    all_to_all x2, starting transfers between devices: 9.58 us -> 8.21 us  [exchange(): lax.all_to_all(x, 'lon', split_axis=0, concat_axis=0, tiled=True, axis_in...]
    ppermute x3, starting transfers between devices: 13.9 us -> 12.7 us  [swap(): far = lax.ppermute(far, axis, pairs[1])]
where the time goes in v6:
time: 40.9 us; the launch traced here: 40.2 us
  starting transfers between devices  23.1 us (56%)
  Pallas kernels  13.4 us (33%)
  waiting for transfers between devices  2.96 us (7%)
  between operations  0.73 us (2%)
    pallas_call x8, Pallas kernels, run(): kernel(*(pltpu.with_memory_space_constraint(x, pltpu.HBM) if n in far els...  13.4 us
    ppermute x3, starting transfers between devices, swap(): far = lax.ppermute(far, axis, pairs[1])  12.7 us
    all_to_all x2, starting transfers between devices, exchange(): lax.all_to_all(x, 'lon', split_axis=0, concat_axis=0, tiled=True, axis_in...  8.21 us
    ppermute x3, waiting for transfers between devices, swap(): far = lax.ppermute(far, axis, pairs[1])  2.95 us
    ppermute x3, starting transfers between devices, swap(): return (lax.ppermute(near, axis, pairs[0]), far)  2.25 us
  transfers between devices with their start and end apart: 8, of which 2 were waited for; matrix products, arithmetic and copies ran while one was open for 0% of the time, Pallas kernels for 21%

profile of v6, /device:TPU:1, one launch (start us, length us, event | category | flops | bytes accessed | tf_op | source)
XLA Modules:
  0.0 40.2 jit_solution(8145677595080055700)
XLA Ops:
  0.6 1.4 %pack_columns.1 = (f32[35,16,256]{2,1,0:T(8,128)S(1)}, f32[2,16,128]{2,1,0:T(8,128)S(1)}, f32[2,16,128]{2,1,0:T(8,128)S(1)}, f32[2,1,256,128]{3,2,1,0:T(8,128)S(1)}, s32[3,1,1,8,64]{4,3,2,1,0:T(8,128)S(1)}) custom-call(f32[2,4,16,256]{3,2,1,0:T(8,128)} %refs_0_.1, f32[2,4,16,256]{3,2,1,0:T(8,128)} %refs_1_.1, s32[4,16,256]{2,1,0:T(8,128)} %refs_2_.1, ...), custom_call_target="tpu_custom_call" | custom-call | bytes 1048576 | tf_op jit(solution)/shard_map/pack_columns/pallas_call | solution.py:45
  2.1 2.1 %collective-permute-start = (f32[2,16,128]{2,1,0:T(8,128)S(1)}, f32[2,16,128]{2,1,0:T(8,128)S(1)}, u32[]{:S(2)}, u32[]{:S(2)}) collective-permute-start(f32[2,16,128]{2,1,0:T(8,128)S(1)} %get-tuple-element.24), channel_id=1, source_target_pairs={{0,1},{1,0},{2,3},{3,2},{4,5},{5,4},{6,7},{7,6},{8,9},{9,8},{10,11... | collective-permute-start | bytes 49160 | tf_op jit(solution)/shard_map/ppermute | solution.py:82
  4.2 3.3 %collective-permute-start.1 = (f32[2,16,128]{2,1,0:T(8,128)S(1)}, f32[2,16,128]{2,1,0:T(8,128)S(1)}, u32[]{:S(2)}, u32[]{:S(2)}) collective-permute-start(f32[2,16,128]{2,1,0:T(8,128)S(1)} %get-tuple-element.25.after), channel_id=1, source_target_pairs={{1,2},{2,1},{3,4},{4,3},{5,6},{6,5},{7,0},{0,7},{9,10},{10,9},{11,... | collective-permute-start | bytes 49160 | tf_op jit(solution)/shard_map/ppermute | solution.py:81
  7.5 3.7 %weigh.1 = (f32[8,72,128]{2,1,0:T(8,128)}, f32[40,128]{1,0:T(8,128)S(1)}, f32[8,512]{1,0:T(8,128)S(1)}) custom-call(f32[2,1,256,128]{3,2,1,0:T(8,128)S(1)} %get-tuple-element.26.atm_near, s32[3,1,1,8,64]{4,3,2,1,0:T(8,128)S(1)} %get-tuple-element.27.margins, f32[32,128,128]{2,1,0:T(8,128)} %weights.3, f32[2,16,128]{2,1,0:T(8,128)S(1)} %get-tuple-element.25.after), custom_call_target="tpu_custom_call" | custom-call | flops 4294967296 | bytes 1048576 | tf_op jit(solution)/shard_map/weigh/pallas_call | solution.py:45
  11.2 0.0 collective-permute-done.near_columns
  11.2 0.0 collective-permute-done.1.far_columns
  11.2 3.6 %all-to-all-start = ((f32[8,72,128]{2,1,0:T(8,128)}), f32[8,72,128]{2,1,0:T(8,128)S(1)}, u32[]{:S(2)}, u32[]{:S(2)}) async-start(f32[8,72,128]{2,1,0:T(8,128)} %get-tuple-element.35), calls=%async_computation | async-start | bytes 589824 | tf_op jit(solution)/shard_map/all_to_all | solution.py:72
  14.9 5.2 %collective-permute-start.2 = (f32[37,8,128]{2,1,0:T(8,128)S(1)}, f32[37,8,128]{2,1,0:T(8,128)S(1)}, u32[]{:S(2)}, u32[]{:S(2)}) collective-permute-start(f32[37,8,128]{2,1,0:T(8,128)S(1)} %get-tuple-element.31), channel_id=1, source_target_pairs={{8,16},{16,8},{9,17},{17,9},{10,18},{18,10},{11,19},{19,11},{12,20... | collective-permute-start | bytes 454664 | tf_op jit(solution)/shard_map/ppermute | solution.py:81
  20.1 0.1 collective-permute-start.3
  20.2 2.8 %collective-permute-done.2.far = f32[37,8,128]{2,1,0:T(8,128)S(1)} collective-permute-done((f32[37,8,128]{2,1,0:T(8,128)S(1)}, f32[37,8,128]{2,1,0:T(8,128)S(1)}, u32[]{:S(2)}, u32[]{:S(2)}) %collective-permute-start.2) | collective-permute-done | bytes 151584 | tf_op jit(solution)/shard_map/ppermute | solution.py:81
  22.9 0.0 collective-permute-done.3.near
  22.9 1.6 %run_adjoint.1 = (f32[8,64,128]{2,1,0:T(8,128)}, f32[6,4,24,384]{3,2,1,0:T(8,128)S(1)}, f32[16,24,384]{2,1,0:T(8,128)S(1)}, f32[2,3,4,24,384]{4,3,2,1,0:T(8,128)S(1)}) custom-call(f32[35,16,256]{2,1,0:T(8,128)S(1)} %get-tuple-element.23.fields, f32[2,16,128]{2,1,0:T(8,128)S(1)} %get-tuple-element.29.from_west, ...), custom_call_target="tpu_custom_call" | custom-call | bytes 1048576 | tf_op jit(solution)/shard_map/run_adjoint/pallas_call | solution.py:45
  24.6 0.0 all-to-all-done.received
  24.6 4.6 %all-to-all-start.1 = ((f32[8,64,128]{2,1,0:T(8,128)}), f32[8,64,128]{2,1,0:T(8,128)S(1)}, u32[]{:S(2)}, u32[]{:S(2)}) async-start(f32[8,64,128]{2,1,0:T(8,128)} %get-tuple-element.40), calls=%async_computation.1 | async-start | bytes 524288 | tf_op jit(solution)/shard_map/all_to_all | solution.py:72
  29.1 0.1 sum_forcing.1
  29.3 4.2 %collective-permute-start.4 = (f32[1,8,384]{2,1,0:T(8,128)S(1)}, f32[1,8,384]{2,1,0:T(8,128)S(1)}, u32[]{:S(2)}, u32[]{:S(2)}) collective-permute-start(f32[1,8,384]{2,1,0:T(8,128)S(1)} %get-tuple-element.37), channel_id=1, source_target_pairs={{8,16},{16,8},{9,17},{17,9},{10,18},{18,10},{11,19},{19,11},{12,20... | collective-permute-start | bytes 36872 | tf_op jit(solution)/shard_map/ppermute | solution.py:81
  33.5 0.1 collective-permute-start.5
  33.5 1.4 %finish_adjoint.1 = f32[2,4,16,256]{3,2,1,0:T(8,128)} custom-call(f32[6,4,24,384]{3,2,1,0:T(8,128)S(1)} %get-tuple-element.33.coeffs, f32[16,24,384]{2,1,0:T(8,128)S(1)} %get-tuple-element.34.start, f32[2,3,4,24,384]{4,3,2,1,0:T(8,128)S(1)} %get-tuple-element.39.states), custom_call_target="tpu_custom_call" | custom-call | bytes 1048576 | tf_op jit(solution)/shard_map/finish_adjoint/pallas_call | solution.py:45
  35.0 0.2 collective-permute-done.4.far
  35.1 0.0 collective-permute-done.5.near
  35.1 1.6 %run_forward.1 = f32[2,4,16,256]{3,2,1,0:T(8,128)} custom-call(f32[6,4,24,384]{3,2,1,0:T(8,128)S(1)} %get-tuple-element.33.coeffs, f32[16,24,384]{2,1,0:T(8,128)S(1)} %get-tuple-element.34.start, f32[2,16,384]{2,1,0:T(8,128)S(1)} %get-tuple-element.36.forcing, f32[1,8,384]{2,1,0:T(8,128)S(1)} %collective-permute-done.4.far, ...), custom_call_target="tpu_custom_call" | custom-call | bytes 1048576 | tf_op jit(solution)/shard_map/run_forward/pallas_call | solution.py:45
  36.7 0.0 all-to-all-done.1.gathered
  36.7 3.5 %unweigh.1 = f32[2,1,256,128]{3,2,1,0:T(8,128)} custom-call(f32[8,64,128]{2,1,0:T(8,128)S(1)} %all-to-all-done.1.gathered, f32[40,128]{1,0:T(8,128)S(1)} %get-tuple-element.41.found, f32[8,512]{1,0:T(8,128)S(1)} %get-tuple-element.42.keys, f32[32,128,128]{2,1,0:T(8,128)} %weights.3), custom_call_target="tpu_custom_call" | custom-call | flops 4294967296 | bytes 1048576 | tf_op jit(solution)/shard_map/unweigh/pallas_call | solution.py:45
  (1 shorter events, 0.0 us)
Async XLA Ops:
  2.1 9.1 %collective-permute-start = (f32[2,16,128]{2,1,0:T(8,128)S(1)}, f32[2,16,128]{2,1,0:T(8,128)S(1)}, u32[]{:S(2)}, u32[]{:S(2)}) collective-permute-start(f32[2,16,128]{2,1,0:T(8,128)S(1)} %get-tuple-element.24), channel_id=1, source_target_pairs={{0,1},{1,0},{2,3},{3,2},{4,5},{5,4},{6,7},{7,6},{8,9},{9,8},{10,11... | collective-permute-start | bytes 49160 | tf_op jit(solution)/shard_map/ppermute | solution.py:82
  4.2 7.0 %collective-permute-start.1 = (f32[2,16,128]{2,1,0:T(8,128)S(1)}, f32[2,16,128]{2,1,0:T(8,128)S(1)}, u32[]{:S(2)}, u32[]{:S(2)}) collective-permute-start(f32[2,16,128]{2,1,0:T(8,128)S(1)} %get-tuple-element.25.after), channel_id=1, source_target_pairs={{1,2},{2,1},{3,4},{4,3},{5,6},{6,5},{7,0},{0,7},{9,10},{10,9},{11,... | collective-permute-start | bytes 49160 | tf_op jit(solution)/shard_map/ppermute | solution.py:81
  11.2 13.3 %all-to-all-start = ((f32[8,72,128]{2,1,0:T(8,128)}), f32[8,72,128]{2,1,0:T(8,128)S(1)}, u32[]{:S(2)}, u32[]{:S(2)}) async-start(f32[8,72,128]{2,1,0:T(8,128)} %get-tuple-element.35), calls=%async_computation | async-start | bytes 589824 | tf_op jit(solution)/shard_map/all_to_all | solution.py:72
  14.9 8.0 %collective-permute-start.2 = (f32[37,8,128]{2,1,0:T(8,128)S(1)}, f32[37,8,128]{2,1,0:T(8,128)S(1)}, u32[]{:S(2)}, u32[]{:S(2)}) collective-permute-start(f32[37,8,128]{2,1,0:T(8,128)S(1)} %get-tuple-element.31), channel_id=1, source_target_pairs={{8,16},{16,8},{9,17},{17,9},{10,18},{18,10},{11,19},{19,11},{12,20... | collective-permute-start | bytes 454664 | tf_op jit(solution)/shard_map/ppermute | solution.py:81
  20.1 2.9 %collective-permute-start.3 = (f32[37,8,128]{2,1,0:T(8,128)S(1)}, f32[37,8,128]{2,1,0:T(8,128)S(1)}, u32[]{:S(2)}, u32[]{:S(2)}) collective-permute-start(f32[37,8,128]{2,1,0:T(8,128)S(1)} %get-tuple-element.32), channel_id=1, source_target_pairs={{0,8},{8,0},{16,24},{24,16},{1,9},{9,1},{17,25},{25,17},{2,10},{10... | collective-permute-start | bytes 454664 | tf_op jit(solution)/shard_map/ppermute | solution.py:82
  24.6 12.1 %all-to-all-start.1 = ((f32[8,64,128]{2,1,0:T(8,128)}), f32[8,64,128]{2,1,0:T(8,128)S(1)}, u32[]{:S(2)}, u32[]{:S(2)}) async-start(f32[8,64,128]{2,1,0:T(8,128)} %get-tuple-element.40), calls=%async_computation.1 | async-start | bytes 524288 | tf_op jit(solution)/shard_map/all_to_all | solution.py:72
  29.3 5.8 %collective-permute-start.4 = (f32[1,8,384]{2,1,0:T(8,128)S(1)}, f32[1,8,384]{2,1,0:T(8,128)S(1)}, u32[]{:S(2)}, u32[]{:S(2)}) collective-permute-start(f32[1,8,384]{2,1,0:T(8,128)S(1)} %get-tuple-element.37), channel_id=1, source_target_pairs={{8,16},{16,8},{9,17},{17,9},{10,18},{18,10},{11,19},{19,11},{12,20... | collective-permute-start | bytes 36872 | tf_op jit(solution)/shard_map/ppermute | solution.py:81
  33.5 1.7 %collective-permute-start.5 = (f32[1,8,384]{2,1,0:T(8,128)S(1)}, f32[1,8,384]{2,1,0:T(8,128)S(1)}, u32[]{:S(2)}, u32[]{:S(2)}) collective-permute-start(f32[1,8,384]{2,1,0:T(8,128)S(1)} %get-tuple-element.38), channel_id=1, source_target_pairs={{0,8},{8,0},{16,24},{24,16},{1,9},{9,1},{17,25},{25,17},{2,10},{10... | collective-permute-start | bytes 36872 | tf_op jit(solution)/shard_map/ppermute | solution.py:82

commit v7 on v6

--- a/solution.py
+++ b/solution.py
@@ -378,6 +378,10 @@
     return 8 * (-(-2 * slots // (8 * blocks)) + 1)
 
 
+def round_chunks(slots, blocks):
+    return -(-(slots + 7 * blocks) // BLOCK)
+
+
 def as_row(ids):
     return jnp.concatenate([ids[k : k + 1, :] for k in range(ids.shape[0])], axis=1)
 
@@ -395,55 +399,64 @@
         here = jnp.where(mine[:, at : at + BLOCK], run[:, :BLOCK] + before, 0.0)
         out.append(jnp.sum(here, axis=0, keepdims=True))
         before = before + run[:, BLOCK:]
-    return jnp.concatenate(out, axis=1)
-
-
-def find_slots(r, code, block_row, rank, capacity, blocks, found):
-    slots = block_row.shape[1]
-    mine = rows((blocks, slots)) == block_row
-    ranked = one_hot(rows((capacity, slots)) == rank.astype(jnp.int32) - r * capacity)
-    rest, codes = code + 1.0, None
-    for base in (4096.0, 64.0, 1.0):
-        digit = jnp.floor(rest * (1.0 / base))
-        rest = rest - digit * base
-        part = lax.dot_general(
-            ranked,
-            jnp.where(mine, digit, 0.0).astype(bf16),
-            (((1,), (1,)), ((), ())),
-            preferred_element_type=f32,
-        )
-        codes = part * base if codes is None else codes + part * base
-    found[:, :blocks] = codes - 1.0
-
-
-def couple(blocks, part, table, size, capacity, rounds, prepare, found, gather_first, transposed, result, scratch):
-    column, vectors, products = scratch
-    total_rows = column.shape[0]
+    return jnp.concatenate(out, axis=1), before
+
+
+def find_slots(r, keys, counts, capacity, columns, lines, starts):
+    slots = keys.shape[1]
+    blocks = counts.shape[0]
+    atm_row, ocean_row, block_row, rank = (keys[n : n + 1] for n in range(4))
+    count = jnp.clip(counts - r * capacity, 0.0, capacity)
+    tiles = jnp.floor((count + 7.0) * 0.125) * 8.0
+    shape = (blocks, blocks)
+    first = jnp.dot(one_hot(lanes(shape) < rows(shape)), tiles.astype(bf16), preferred_element_type=f32)
+    starts[...] = first.astype(jnp.int32)
+    mine = rows((blocks, slots)).astype(f32) == block_row
+    own = jnp.where(mine, jnp.concatenate([first] * (slots // BLOCK), axis=1), 0.0)
+    place = rank - r * capacity
+    here = (place >= 0.0) & (place < capacity)
+    place = jnp.where(here, jnp.sum(own, axis=0, keepdims=True) + place, -1.0)
+    run = jnp.floor(place * (1.0 / BLOCK))
+    low = one_hot(rows((BLOCK, slots)).astype(f32) == place - run * BLOCK)
+    size = lines.shape[1]
+    in_run = rows((size, slots)).astype(f32) == run
+    ocean_high = jnp.floor(ocean_row * (1.0 / BLOCK))
+    digits = [atm_row, ocean_high, ocean_row - ocean_high * BLOCK]
+    digits = [jnp.where(in_run, digit, 0.0).astype(bf16) for digit in digits]
+    across = (((1,), (1,)), ((), ()))
+    down = [lax.dot_general(low, digit, across, preferred_element_type=f32) for digit in digits]
+    along = [lax.dot_general(digit, low, across, preferred_element_type=f32) for digit in digits]
+    columns[0, :, :size], columns[1, :, :size] = down[0], down[1] * BLOCK + down[2] - 1.0
+    ocean = along[1] * BLOCK + along[2] - 1.0
+    lines[0], lines[1] = jnp.where(ocean < 0.0, -1.0, along[0]), ocean
+
+
+def couple(part, table, capacity, rounds, prepare, columns, lines, starts, transposed, result, scratch):
+    vectors, products, starts_near, moved = scratch
+    blocks = starts.shape[0]
+    total_rows = vectors.shape[0] - capacity
+    width = table.shape[0]
     result[...] = jnp.zeros_like(result)
+    products[...] = jnp.zeros_like(products)
 
     def one_round(r, carry):
         prepare(r)
-        codes = found[...]
-        for w in range(blocks):
-            column[w * capacity : (w + 1) * capacity] = jnp.broadcast_to(codes[:, w : w + 1], (capacity, BLOCK))
-        eye = rows((BLOCK, BLOCK)) == lanes((BLOCK, BLOCK))
+        move = pltpu.make_async_copy(starts, starts_near, moved)
+        move.start()
         place_hot = []
-        for at in range(0, total_rows, BLOCK):
-            code = column[at : at + BLOCK]
-            first = jnp.floor((code + 0.5) * (1.0 / size))
-            second = code - first * size
-            gather, put = (first, second) if gather_first else (second, first)
-            width = table.shape[0]
+        for n in range(total_rows // BLOCK):
+            gather = jnp.broadcast_to(columns[int(transposed), :, n : n + 1], (BLOCK, BLOCK))
             gather = jnp.concatenate([gather] * (width // BLOCK), axis=1)
             hot = one_hot(gather == lanes((BLOCK, width)).astype(f32))
-            vectors[at : at + BLOCK] = jnp.dot(hot, table, preferred_element_type=f32)
-            put = jnp.sum(jnp.where(eye, put, 0.0), axis=0, keepdims=True)
+            vectors[n * BLOCK : (n + 1) * BLOCK] = jnp.dot(hot, table, preferred_element_type=f32)
+            put = lines[1 - int(transposed), n : n + 1]
             place_hot.append(one_hot(rows((result.shape[0], BLOCK)).astype(f32) == put))
+        move.wait()
 
         def group(g, carry):
             for u in range(GROUP):
-                at = pl.multiple_of((g * GROUP + u) * capacity, 8)
-                own = vectors[pl.ds(at, capacity)]
+                at = pl.ds(pl.multiple_of(starts_near[g * GROUP + u, 0], 8), capacity)
+                own = vectors[at]
                 left = jnp.concatenate([own[:, n * BLOCK : (n + 1) * BLOCK] for n in range(4)], axis=0)
                 high, low = part(r, g, u)
                 right = jnp.concatenate([high, low], axis=1 if transposed else 0)
@@ -452,7 +465,7 @@
                 for f in range(2):
                     high_part = product[f * capacity : (f + 1) * capacity]
                     low_part = product[(f + 2) * capacity : (f + 3) * capacity, :BLOCK]
-                    products[pl.ds(at, capacity), f * BLOCK : (f + 1) * BLOCK] = (
+                    products[at, f * BLOCK : (f + 1) * BLOCK] = (
                         high_part[:, BLOCK:] + low_part
                     ) + high_part[:, :BLOCK]
             return carry
@@ -460,7 +473,7 @@
         lax.fori_loop(0, blocks // GROUP, group, 0)
         summed = jnp.dot(
             jnp.concatenate(place_hot, axis=1),
-            jnp.concatenate(split(products[...]), axis=1),
+            jnp.concatenate(split(products[:total_rows]), axis=1),
             preferred_element_type=f32,
         )
         result[...] += summed[:, : 2 * BLOCK] + summed[:, 2 * BLOCK :]
@@ -469,36 +482,37 @@
     lax.fori_loop(0, rounds, one_round, 0)
 
 
-def slot_keys(ids, tile_lat, atm):
+def slot_keys(ids, tile_lat, keys):
     lon_count, cap = ids.shape[3:]
     ocean, atm_ids, block_ids = (ids[n, 0, 0] for n in range(3))
     order = (ocean & 1) * tile_lat + (ocean >> 1) + rows((lon_count, cap)) * (2 * tile_lat)
-    order = jnp.where(ocean >= 0, order, lon_count * 2 * tile_lat)
-    return as_row((order * atm + atm_ids).astype(f32)), as_row(block_ids)
-
-
-def weigh(atm_near, margins, weights, after, sums, found, keys, result, *scratch):
-    scratch, (held, arrived) = scratch[:3], scratch[3:]
+    order = jnp.where(ocean >= 0, order, lon_count * 2 * tile_lat) + 1
+    for n, part in enumerate((atm_ids, order, block_ids)):
+        keys[n : n + 1] = as_row(part.astype(f32))
+
+
+def weigh(
+    atm_near, margins, weights, after, sums, keys, counts, columns, lines, starts, result, *scratch
+):
+    scratch, (held, arrived) = scratch[:4], scratch[4:]
     fetch_weights(weights, held, arrived)
     lon_count = margins.shape[3]
-    atm = atm_near.shape[2]
     blocks = weights.shape[0]
     tile_lat = 2 * sums.shape[1] // 9
-    code, block_row = slot_keys(margins, tile_lat, atm)
-    rank = rank_slots(block_row, blocks)
-    keys[0:1] = code
-    keys[1:2] = block_row.astype(f32)
-    keys[2:3] = rank
-    capacity = places(code.shape[1], blocks)
+    slot_keys(margins, tile_lat, keys)
+    rank, count = rank_slots(keys[2:3].astype(jnp.int32), blocks)
+    keys[3:4] = rank
+    counts[...] = count
+    capacity = places(keys.shape[1], blocks)
     rounds = jnp.max(rank).astype(jnp.int32) // capacity + 1
     parts = [split(atm_near[f, 0]) for f in range(2)]
     table = jnp.concatenate([parts[f][n] for n in range(2) for f in range(2)], axis=1)
+    part = held_part(weights, held, arrived)
 
     def prepare(r):
-        find_slots(rounds - 1 - r, code, block_row, rank, capacity, blocks, found)
-
-    part = held_part(weights, held, arrived)
-    couple(blocks, part, table, atm, capacity, rounds, prepare, found, False, False, result, scratch)
+        find_slots((rounds - 1 - r).astype(f32), keys, counts[...], capacity, columns, lines, starts)
+
+    couple(part, table, capacity, rounds, prepare, columns, lines, starts, False, result, scratch)
     lane = lanes((tile_lat, BLOCK))
 
     def block_sums(k, f, h):
@@ -522,15 +536,16 @@
         sums[n, 4 * tile_lat :] = jnp.where((near < 2 * HALO) | (near >= BLOCK - 2 * HALO), upper, lower)
 
 
-def unweigh(gathered, found, keys, weights, gradient, result, codes, *scratch):
-    scratch, (held, arrived) = scratch[:3], scratch[3:]
+def unweigh(
+    gathered, keys, counts, columns_in, lines_in, starts_in, weights, gradient, result, columns, lines, starts, *scratch
+):
+    scratch, (held, arrived) = scratch[:4], scratch[4:]
     fetch_weights(weights, held, arrived)
-    atm = gradient.shape[2]
     blocks = weights.shape[0]
     lon_count, ocean_blocks = gathered.shape[0], gathered.shape[1] // 2
     order = group_order(lon_count)
     capacity = places(keys.shape[1], blocks)
-    rounds = jnp.max(keys[2:3]).astype(jnp.int32) // capacity + 1
+    rounds = jnp.max(keys[3:4]).astype(jnp.int32) // capacity + 1
     parts = [
         split(
             jnp.concatenate(
@@ -545,26 +560,16 @@
     def prepare(r):
         @pl.when(r == 0)
         def _():
-            codes[...] = found[...]
+            columns[...] = columns_in[...]
+            lines[...] = lines_in[...]
+            starts[...] = starts_in[...]
 
         @pl.when(r > 0)
         def _():
-            find_slots(r, keys[0:1], keys[1:2].astype(jnp.int32), keys[2:3], capacity, blocks, codes)
-
-    couple(
-        blocks,
-        held_part(weights, held, arrived),
-        table,
-        atm,
-        capacity,
-        rounds,
-        prepare,
-        codes,
-        True,
-        True,
-        result,
-        scratch,
-    )
+            find_slots(r.astype(f32), keys, counts[...], capacity, columns, lines, starts)
+
+    part = held_part(weights, held, arrived)
+    couple(part, table, capacity, rounds, prepare, columns, lines, starts, True, result, scratch)
     for f in range(2):
         gradient[f, 0] = result[:, f * BLOCK : (f + 1) * BLOCK]
 
@@ -602,22 +607,29 @@
     groups = blocks_of // GROUP
     sum_rows = 2 * halves * tile_lat + tile_lat // 2
     ocean_blocks = lon_count * halves * tile_lat
-    held_rows = -(-places(slots, blocks_of) * blocks_of // BLOCK) * BLOCK
+    chunks = round_chunks(slots, blocks_of)
+    held_rows = chunks * BLOCK + places(slots, blocks_of)
 
     def coupling_scratch(result_rows):
         return [
             pltpu.VMEM((result_rows, 2 * BLOCK), f32),
-            pltpu.VMEM((held_rows, BLOCK), f32),
             pltpu.VMEM((held_rows, 4 * BLOCK), f32),
             pltpu.VMEM((held_rows, 2 * BLOCK), f32),
+            pltpu.SMEM((blocks_of, BLOCK), jnp.int32),
+            pltpu.SemaphoreType.DMA,
             pltpu.VMEM((groups, GROUP, BLOCK, BLOCK), f32),
             pltpu.SemaphoreType.DMA((groups,)),
         ]
 
     coupling_flops = 4 * slots * blocks_of * 2 * BLOCK * BLOCK * 2
-    sums, found, keys = call(
+    found = [
+        jax.ShapeDtypeStruct((2, BLOCK, BLOCK), f32),
+        jax.ShapeDtypeStruct((2, -(-chunks // 8) * 8, BLOCK), f32),
+        jax.ShapeDtypeStruct((blocks_of, BLOCK), jnp.int32),
+    ]
+    sums, *slot_data = call(
         weigh,
-        [(lon_count, sum_rows, BLOCK), (places(slots, blocks_of), BLOCK), (8, slots)],
+        [(lon_count, sum_rows, BLOCK), (8, slots), (blocks_of, BLOCK), *found],
         coupling_scratch(ocean_blocks),
         coupling_flops,
         name="weigh",
@@ -678,12 +690,12 @@
     (gradient,) = call(
         unweigh,
         [atm_state.shape],
-        [coupling_scratch(atm)[0], in_vmem(found), *coupling_scratch(atm)[1:]],
+        [coupling_scratch(atm)[0], *map(in_vmem, found), *coupling_scratch(atm)[1:]],
         coupling_flops,
         name="unweigh",
-        inputs=4,
-        far=(3,),
-    )(gathered, found, keys, weights)
+        inputs=7,
+        far=(6,),
+    )(gathered, *slot_data, weights)
     return (final, adjoint, gradient)
 
 

time: 40.9 us -> 40.8 us (level)
  no operation moved by 1% of the time
where the time goes in v7:
time: 40.8 us; the launch traced here: 40.1 us
  starting transfers between devices  23.1 us (57%)
  Pallas kernels  13.3 us (33%)
  waiting for transfers between devices  2.96 us (7%)
  between operations  0.73 us (2%)
    pallas_call x8, Pallas kernels, run(): kernel(*(pltpu.with_memory_space_constraint(x, pltpu.HBM) if n in far els...  13.3 us
    ppermute x3, starting transfers between devices, swap(): far = lax.ppermute(far, axis, pairs[1])  12.6 us
    all_to_all x2, starting transfers between devices, exchange(): lax.all_to_all(x, 'lon', split_axis=0, concat_axis=0, tiled=True, axis_in...  8.21 us
    ppermute x3, waiting for transfers between devices, swap(): far = lax.ppermute(far, axis, pairs[1])  2.95 us
    ppermute x3, starting transfers between devices, swap(): return (lax.ppermute(near, axis, pairs[0]), far)  2.25 us
  transfers between devices with their start and end apart: 8, of which 2 were waited for; matrix products, arithmetic and copies ran while one was open for 0% of the time, Pallas kernels for 21%

profile of v7, /device:TPU:1, one launch (start us, length us, event | category | flops | bytes accessed | tf_op | source)
XLA Modules:
  0.0 40.1 jit_solution(9464294443533231555)
XLA Ops:
  0.6 1.4 %pack_columns.1 = (f32[35,16,256]{2,1,0:T(8,128)S(1)}, f32[2,16,128]{2,1,0:T(8,128)S(1)}, f32[2,16,128]{2,1,0:T(8,128)S(1)}, f32[2,1,256,128]{3,2,1,0:T(8,128)S(1)}, s32[3,1,1,8,64]{4,3,2,1,0:T(8,128)S(1)}) custom-call(f32[2,4,16,256]{3,2,1,0:T(8,128)} %refs_0_.1, f32[2,4,16,256]{3,2,1,0:T(8,128)} %refs_1_.1, s32[4,16,256]{2,1,0:T(8,128)} %refs_2_.1, ...), custom_call_target="tpu_custom_call" | custom-call | bytes 1048576 | tf_op jit(solution)/shard_map/pack_columns/pallas_call | solution.py:45
  2.1 2.1 %collective-permute-start = (f32[2,16,128]{2,1,0:T(8,128)S(1)}, f32[2,16,128]{2,1,0:T(8,128)S(1)}, u32[]{:S(2)}, u32[]{:S(2)}) collective-permute-start(f32[2,16,128]{2,1,0:T(8,128)S(1)} %get-tuple-element.27), channel_id=1, source_target_pairs={{0,1},{1,0},{2,3},{3,2},{4,5},{5,4},{6,7},{7,6},{8,9},{9,8},{10,11... | collective-permute-start | bytes 49160 | tf_op jit(solution)/shard_map/ppermute | solution.py:82
  4.2 3.3 %collective-permute-start.1 = (f32[2,16,128]{2,1,0:T(8,128)S(1)}, f32[2,16,128]{2,1,0:T(8,128)S(1)}, u32[]{:S(2)}, u32[]{:S(2)}) collective-permute-start(f32[2,16,128]{2,1,0:T(8,128)S(1)} %get-tuple-element.28.after), channel_id=1, source_target_pairs={{1,2},{2,1},{3,4},{4,3},{5,6},{6,5},{7,0},{0,7},{9,10},{10,9},{11,... | collective-permute-start | bytes 49160 | tf_op jit(solution)/shard_map/ppermute | solution.py:81
  7.5 3.7 %weigh.1 = (f32[8,72,128]{2,1,0:T(8,128)}, f32[8,512]{1,0:T(8,128)S(1)}, f32[32,128]{1,0:T(8,128)S(1)}, f32[2,128,128]{2,1,0:T(8,128)S(1)}, f32[2,8,128]{2,1,0:T(8,128)S(1)}, /*index=5*/s32[32,128]{1,0:T(8,128)S(1)}) custom-call(f32[2,1,256,128]{3,2,1,0:T(8,128)S(1)} %get-tuple-element.29.atm_near, s32[3,1,1,8,64]{4,3,2,1,0:T(8,128)S(1)} %get-tuple-element.30.margins, ...), custom_call_target="tpu_custom_call" | custom-call | flops 4294967296 | bytes 1048576 | tf_op jit(solution)/shard_map/weigh/pallas_call | solution.py:45
  11.2 0.0 collective-permute-done.near_columns
  11.2 0.0 collective-permute-done.1.far_columns
  11.2 3.6 %all-to-all-start = ((f32[8,72,128]{2,1,0:T(8,128)}), f32[8,72,128]{2,1,0:T(8,128)S(1)}, u32[]{:S(2)}, u32[]{:S(2)}) async-start(f32[8,72,128]{2,1,0:T(8,128)} %get-tuple-element.38), calls=%async_computation | async-start | bytes 589824 | tf_op jit(solution)/shard_map/all_to_all | solution.py:72
  14.9 5.2 %collective-permute-start.2 = (f32[37,8,128]{2,1,0:T(8,128)S(1)}, f32[37,8,128]{2,1,0:T(8,128)S(1)}, u32[]{:S(2)}, u32[]{:S(2)}) collective-permute-start(f32[37,8,128]{2,1,0:T(8,128)S(1)} %get-tuple-element.34), channel_id=1, source_target_pairs={{8,16},{16,8},{9,17},{17,9},{10,18},{18,10},{11,19},{19,11},{12,20... | collective-permute-start | bytes 454664 | tf_op jit(solution)/shard_map/ppermute | solution.py:81
  20.1 0.1 collective-permute-start.3
  20.2 2.8 %collective-permute-done.2.far = f32[37,8,128]{2,1,0:T(8,128)S(1)} collective-permute-done((f32[37,8,128]{2,1,0:T(8,128)S(1)}, f32[37,8,128]{2,1,0:T(8,128)S(1)}, u32[]{:S(2)}, u32[]{:S(2)}) %collective-permute-start.2) | collective-permute-done | bytes 151584 | tf_op jit(solution)/shard_map/ppermute | solution.py:81
  22.9 0.0 collective-permute-done.3.near
  22.9 1.6 %run_adjoint.1 = (f32[8,64,128]{2,1,0:T(8,128)}, f32[6,4,24,384]{3,2,1,0:T(8,128)S(1)}, f32[16,24,384]{2,1,0:T(8,128)S(1)}, f32[2,3,4,24,384]{4,3,2,1,0:T(8,128)S(1)}) custom-call(f32[35,16,256]{2,1,0:T(8,128)S(1)} %get-tuple-element.26.fields, f32[2,16,128]{2,1,0:T(8,128)S(1)} %get-tuple-element.32.from_west, ...), custom_call_target="tpu_custom_call" | custom-call | bytes 1048576 | tf_op jit(solution)/shard_map/run_adjoint/pallas_call | solution.py:45
  24.6 0.0 all-to-all-done.received
  24.6 4.6 %all-to-all-start.1 = ((f32[8,64,128]{2,1,0:T(8,128)}), f32[8,64,128]{2,1,0:T(8,128)S(1)}, u32[]{:S(2)}, u32[]{:S(2)}) async-start(f32[8,64,128]{2,1,0:T(8,128)} %get-tuple-element.43), calls=%async_computation.1 | async-start | bytes 524288 | tf_op jit(solution)/shard_map/all_to_all | solution.py:72
  29.1 0.1 sum_forcing.1
  29.3 4.2 %collective-permute-start.4 = (f32[1,8,384]{2,1,0:T(8,128)S(1)}, f32[1,8,384]{2,1,0:T(8,128)S(1)}, u32[]{:S(2)}, u32[]{:S(2)}) collective-permute-start(f32[1,8,384]{2,1,0:T(8,128)S(1)} %get-tuple-element.40), channel_id=1, source_target_pairs={{8,16},{16,8},{9,17},{17,9},{10,18},{18,10},{11,19},{19,11},{12,20... | collective-permute-start | bytes 36872 | tf_op jit(solution)/shard_map/ppermute | solution.py:81
  33.5 0.1 collective-permute-start.5
  33.5 1.4 %finish_adjoint.1 = f32[2,4,16,256]{3,2,1,0:T(8,128)} custom-call(f32[6,4,24,384]{3,2,1,0:T(8,128)S(1)} %get-tuple-element.36.coeffs, f32[16,24,384]{2,1,0:T(8,128)S(1)} %get-tuple-element.37.start, f32[2,3,4,24,384]{4,3,2,1,0:T(8,128)S(1)} %get-tuple-element.42.states), custom_call_target="tpu_custom_call" | custom-call | bytes 1048576 | tf_op jit(solution)/shard_map/finish_adjoint/pallas_call | solution.py:45
  35.0 0.2 collective-permute-done.4.far
  35.1 0.0 collective-permute-done.5.near
  35.1 1.6 %run_forward.1 = f32[2,4,16,256]{3,2,1,0:T(8,128)} custom-call(f32[6,4,24,384]{3,2,1,0:T(8,128)S(1)} %get-tuple-element.36.coeffs, f32[16,24,384]{2,1,0:T(8,128)S(1)} %get-tuple-element.37.start, f32[2,16,384]{2,1,0:T(8,128)S(1)} %get-tuple-element.39.forcing, f32[1,8,384]{2,1,0:T(8,128)S(1)} %collective-permute-done.4.far, ...), custom_call_target="tpu_custom_call" | custom-call | bytes 1048576 | tf_op jit(solution)/shard_map/run_forward/pallas_call | solution.py:45
  36.7 0.0 all-to-all-done.1.gathered
  36.7 3.4 %unweigh.1 = f32[2,1,256,128]{3,2,1,0:T(8,128)} custom-call(f32[8,64,128]{2,1,0:T(8,128)S(1)} %all-to-all-done.1.gathered, f32[8,512]{1,0:T(8,128)S(1)} %get-tuple-element.44.keys, f32[32,128]{1,0:T(8,128)S(1)} %get-tuple-element.45.counts, f32[2,128,128]{2,1,0:T(8,128)S(1)} %get-tuple-element.46.columns_in, f32[2,8,128]{2,1,0:T(8,128)S(1)} %get-tuple-element.47.lines_in, ...), custom_call_target="tpu_custom_call" | custom-call | flops 4294967296 | bytes 1048576 | tf_op jit(solution)/shard_map/unweigh/pallas_call | solution.py:45
  (1 shorter events, 0.0 us)
Async XLA Ops:
  2.1 9.1 %collective-permute-start = (f32[2,16,128]{2,1,0:T(8,128)S(1)}, f32[2,16,128]{2,1,0:T(8,128)S(1)}, u32[]{:S(2)}, u32[]{:S(2)}) collective-permute-start(f32[2,16,128]{2,1,0:T(8,128)S(1)} %get-tuple-element.27), channel_id=1, source_target_pairs={{0,1},{1,0},{2,3},{3,2},{4,5},{5,4},{6,7},{7,6},{8,9},{9,8},{10,11... | collective-permute-start | bytes 49160 | tf_op jit(solution)/shard_map/ppermute | solution.py:82
  4.2 7.0 %collective-permute-start.1 = (f32[2,16,128]{2,1,0:T(8,128)S(1)}, f32[2,16,128]{2,1,0:T(8,128)S(1)}, u32[]{:S(2)}, u32[]{:S(2)}) collective-permute-start(f32[2,16,128]{2,1,0:T(8,128)S(1)} %get-tuple-element.28.after), channel_id=1, source_target_pairs={{1,2},{2,1},{3,4},{4,3},{5,6},{6,5},{7,0},{0,7},{9,10},{10,9},{11,... | collective-permute-start | bytes 49160 | tf_op jit(solution)/shard_map/ppermute | solution.py:81
  11.2 13.3 %all-to-all-start = ((f32[8,72,128]{2,1,0:T(8,128)}), f32[8,72,128]{2,1,0:T(8,128)S(1)}, u32[]{:S(2)}, u32[]{:S(2)}) async-start(f32[8,72,128]{2,1,0:T(8,128)} %get-tuple-element.38), calls=%async_computation | async-start | bytes 589824 | tf_op jit(solution)/shard_map/all_to_all | solution.py:72
  14.9 8.0 %collective-permute-start.2 = (f32[37,8,128]{2,1,0:T(8,128)S(1)}, f32[37,8,128]{2,1,0:T(8,128)S(1)}, u32[]{:S(2)}, u32[]{:S(2)}) collective-permute-start(f32[37,8,128]{2,1,0:T(8,128)S(1)} %get-tuple-element.34), channel_id=1, source_target_pairs={{8,16},{16,8},{9,17},{17,9},{10,18},{18,10},{11,19},{19,11},{12,20... | collective-permute-start | bytes 454664 | tf_op jit(solution)/shard_map/ppermute | solution.py:81
  20.1 2.9 %collective-permute-start.3 = (f32[37,8,128]{2,1,0:T(8,128)S(1)}, f32[37,8,128]{2,1,0:T(8,128)S(1)}, u32[]{:S(2)}, u32[]{:S(2)}) collective-permute-start(f32[37,8,128]{2,1,0:T(8,128)S(1)} %get-tuple-element.35), channel_id=1, source_target_pairs={{0,8},{8,0},{16,24},{24,16},{1,9},{9,1},{17,25},{25,17},{2,10},{10... | collective-permute-start | bytes 454664 | tf_op jit(solution)/shard_map/ppermute | solution.py:82
  24.6 12.1 %all-to-all-start.1 = ((f32[8,64,128]{2,1,0:T(8,128)}), f32[8,64,128]{2,1,0:T(8,128)S(1)}, u32[]{:S(2)}, u32[]{:S(2)}) async-start(f32[8,64,128]{2,1,0:T(8,128)} %get-tuple-element.43), calls=%async_computation.1 | async-start | bytes 524288 | tf_op jit(solution)/shard_map/all_to_all | solution.py:72
  29.3 5.8 %collective-permute-start.4 = (f32[1,8,384]{2,1,0:T(8,128)S(1)}, f32[1,8,384]{2,1,0:T(8,128)S(1)}, u32[]{:S(2)}, u32[]{:S(2)}) collective-permute-start(f32[1,8,384]{2,1,0:T(8,128)S(1)} %get-tuple-element.40), channel_id=1, source_target_pairs={{8,16},{16,8},{9,17},{17,9},{10,18},{18,10},{11,19},{19,11},{12,20... | collective-permute-start | bytes 36872 | tf_op jit(solution)/shard_map/ppermute | solution.py:81
  33.5 1.7 %collective-permute-start.5 = (f32[1,8,384]{2,1,0:T(8,128)S(1)}, f32[1,8,384]{2,1,0:T(8,128)S(1)}, u32[]{:S(2)}, u32[]{:S(2)}) collective-permute-start(f32[1,8,384]{2,1,0:T(8,128)S(1)} %get-tuple-element.41), channel_id=1, source_target_pairs={{0,8},{8,0},{16,24},{24,16},{1,9},{9,1},{17,25},{25,17},{2,10},{10... | collective-permute-start | bytes 36872 | tf_op jit(solution)/shard_map/ppermute | solution.py:82

commit v8 on v7

--- a/solution.py
+++ b/solution.py
@@ -454,20 +454,32 @@
         move.wait()
 
         def group(g, carry):
-            for u in range(GROUP):
-                at = pl.ds(pl.multiple_of(starts_near[g * GROUP + u, 0], 8), capacity)
-                own = vectors[at]
-                left = jnp.concatenate([own[:, n * BLOCK : (n + 1) * BLOCK] for n in range(4)], axis=0)
-                high, low = part(r, g, u)
-                right = jnp.concatenate([high, low], axis=1 if transposed else 0)
+            for u in range(0, GROUP, 2):
+                pair = [
+                    pl.ds(pl.multiple_of(starts_near[g * GROUP + u + n, 0], 8), capacity) for n in range(2)
+                ]
+                left, right = [], []
+                for n, at in enumerate(pair):
+                    own = vectors[at]
+                    own = jnp.concatenate([own[:, m * BLOCK : (m + 1) * BLOCK] for m in range(4)], axis=0)
+                    own, none = own.astype(bf16), jnp.zeros((4 * capacity, BLOCK), bf16)
+                    left.append(jnp.concatenate([none, own] if n else [own, none], axis=1))
+                    right.append(jnp.concatenate(part(r, g, u + n), axis=1 if transposed else 0))
                 contract = (((1,), (0 if transposed else 1,)), ((), ()))
-                product = lax.dot_general(left.astype(bf16), right, contract, preferred_element_type=f32)
-                for f in range(2):
-                    high_part = product[f * capacity : (f + 1) * capacity]
-                    low_part = product[(f + 2) * capacity : (f + 3) * capacity, :BLOCK]
-                    products[at, f * BLOCK : (f + 1) * BLOCK] = (
-                        high_part[:, BLOCK:] + low_part
-                    ) + high_part[:, :BLOCK]
+                product = lax.dot_general(
+                    jnp.concatenate(left, axis=0),
+                    jnp.concatenate(right, axis=0 if transposed else 1),
+                    contract,
+                    preferred_element_type=f32,
+                )
+                for n, at in enumerate(pair):
+                    own = product[4 * n * capacity : 4 * (n + 1) * capacity]
+                    for f in range(2):
+                        high_part = own[f * capacity : (f + 1) * capacity]
+                        low_part = own[(f + 2) * capacity : (f + 3) * capacity, :BLOCK]
+                        products[at, f * BLOCK : (f + 1) * BLOCK] = (
+                            high_part[:, BLOCK:] + low_part
+                        ) + high_part[:, :BLOCK]
             return carry
 
         lax.fori_loop(0, blocks // GROUP, group, 0)

time: 40.8 us -> 40.8 us (level)
  no operation moved by 1% of the time
where the time goes in v8:
time: 40.8 us; the launch traced here: 40.1 us
  starting transfers between devices  23 us (56%)
  Pallas kernels  13.4 us (33%)
  waiting for transfers between devices  2.96 us (7%)
  between operations  0.73 us (2%)
    pallas_call x8, Pallas kernels, run(): kernel(*(pltpu.with_memory_space_constraint(x, pltpu.HBM) if n in far els...  13.4 us
    ppermute x3, starting transfers between devices, swap(): far = lax.ppermute(far, axis, pairs[1])  12.5 us
    all_to_all x2, starting transfers between devices, exchange(): lax.all_to_all(x, 'lon', split_axis=0, concat_axis=0, tiled=True, axis_in...  8.28 us
    ppermute x3, waiting for transfers between devices, swap(): far = lax.ppermute(far, axis, pairs[1])  2.95 us
    ppermute x3, starting transfers between devices, swap(): return (lax.ppermute(near, axis, pairs[0]), far)  2.25 us
  transfers between devices with their start and end apart: 8, of which 2 were waited for; matrix products, arithmetic and copies ran while one was open for 0% of the time, Pallas kernels for 21%

profile of v8, /device:TPU:1, one launch (start us, length us, event | category | flops | bytes accessed | tf_op | source)
XLA Modules:
  0.0 40.1 jit_solution(4458493971008010915)
XLA Ops:
  0.6 1.4 %pack_columns.1 = (f32[35,16,256]{2,1,0:T(8,128)S(1)}, f32[2,16,128]{2,1,0:T(8,128)S(1)}, f32[2,16,128]{2,1,0:T(8,128)S(1)}, f32[2,1,256,128]{3,2,1,0:T(8,128)S(1)}, s32[3,1,1,8,64]{4,3,2,1,0:T(8,128)S(1)}) custom-call(f32[2,4,16,256]{3,2,1,0:T(8,128)} %refs_0_.1, f32[2,4,16,256]{3,2,1,0:T(8,128)} %refs_1_.1, s32[4,16,256]{2,1,0:T(8,128)} %refs_2_.1, ...), custom_call_target="tpu_custom_call" | custom-call | bytes 1048576 | tf_op jit(solution)/shard_map/pack_columns/pallas_call | solution.py:45
  2.1 2.1 %collective-permute-start = (f32[2,16,128]{2,1,0:T(8,128)S(1)}, f32[2,16,128]{2,1,0:T(8,128)S(1)}, u32[]{:S(2)}, u32[]{:S(2)}) collective-permute-start(f32[2,16,128]{2,1,0:T(8,128)S(1)} %get-tuple-element.27), channel_id=1, source_target_pairs={{0,1},{1,0},{2,3},{3,2},{4,5},{5,4},{6,7},{7,6},{8,9},{9,8},{10,11... | collective-permute-start | bytes 49160 | tf_op jit(solution)/shard_map/ppermute | solution.py:82
  4.2 3.3 %collective-permute-start.1 = (f32[2,16,128]{2,1,0:T(8,128)S(1)}, f32[2,16,128]{2,1,0:T(8,128)S(1)}, u32[]{:S(2)}, u32[]{:S(2)}) collective-permute-start(f32[2,16,128]{2,1,0:T(8,128)S(1)} %get-tuple-element.28.after), channel_id=1, source_target_pairs={{1,2},{2,1},{3,4},{4,3},{5,6},{6,5},{7,0},{0,7},{9,10},{10,9},{11,... | collective-permute-start | bytes 49160 | tf_op jit(solution)/shard_map/ppermute | solution.py:81
  7.5 3.8 %weigh.1 = (f32[8,72,128]{2,1,0:T(8,128)}, f32[8,512]{1,0:T(8,128)S(1)}, f32[32,128]{1,0:T(8,128)S(1)}, f32[2,128,128]{2,1,0:T(8,128)S(1)}, f32[2,8,128]{2,1,0:T(8,128)S(1)}, /*index=5*/s32[32,128]{1,0:T(8,128)S(1)}) custom-call(f32[2,1,256,128]{3,2,1,0:T(8,128)S(1)} %get-tuple-element.29.atm_near, s32[3,1,1,8,64]{4,3,2,1,0:T(8,128)S(1)} %get-tuple-element.30.margins, ...), custom_call_target="tpu_custom_call" | custom-call | flops 4294967296 | bytes 1048576 | tf_op jit(solution)/shard_map/weigh/pallas_call | solution.py:45
  11.2 0.0 collective-permute-done.near_columns
  11.2 0.0 collective-permute-done.1.far_columns
  11.3 3.6 %all-to-all-start = ((f32[8,72,128]{2,1,0:T(8,128)}), f32[8,72,128]{2,1,0:T(8,128)S(1)}, u32[]{:S(2)}, u32[]{:S(2)}) async-start(f32[8,72,128]{2,1,0:T(8,128)} %get-tuple-element.38), calls=%async_computation | async-start | bytes 589824 | tf_op jit(solution)/shard_map/all_to_all | solution.py:72
  15.0 5.1 %collective-permute-start.2 = (f32[37,8,128]{2,1,0:T(8,128)S(1)}, f32[37,8,128]{2,1,0:T(8,128)S(1)}, u32[]{:S(2)}, u32[]{:S(2)}) collective-permute-start(f32[37,8,128]{2,1,0:T(8,128)S(1)} %get-tuple-element.34), channel_id=1, source_target_pairs={{8,16},{16,8},{9,17},{17,9},{10,18},{18,10},{11,19},{19,11},{12,20... | collective-permute-start | bytes 454664 | tf_op jit(solution)/shard_map/ppermute | solution.py:81
  20.1 0.1 collective-permute-start.3
  20.2 2.8 %collective-permute-done.2.far = f32[37,8,128]{2,1,0:T(8,128)S(1)} collective-permute-done((f32[37,8,128]{2,1,0:T(8,128)S(1)}, f32[37,8,128]{2,1,0:T(8,128)S(1)}, u32[]{:S(2)}, u32[]{:S(2)}) %collective-permute-start.2) | collective-permute-done | bytes 151584 | tf_op jit(solution)/shard_map/ppermute | solution.py:81
  22.9 0.0 collective-permute-done.3.near
  22.9 1.6 %run_adjoint.1 = (f32[8,64,128]{2,1,0:T(8,128)}, f32[6,4,24,384]{3,2,1,0:T(8,128)S(1)}, f32[16,24,384]{2,1,0:T(8,128)S(1)}, f32[2,3,4,24,384]{4,3,2,1,0:T(8,128)S(1)}) custom-call(f32[35,16,256]{2,1,0:T(8,128)S(1)} %get-tuple-element.26.fields, f32[2,16,128]{2,1,0:T(8,128)S(1)} %get-tuple-element.32.from_west, ...), custom_call_target="tpu_custom_call" | custom-call | bytes 1048576 | tf_op jit(solution)/shard_map/run_adjoint/pallas_call | solution.py:45
  24.6 0.0 all-to-all-done.received
  24.6 4.6 %all-to-all-start.1 = ((f32[8,64,128]{2,1,0:T(8,128)}), f32[8,64,128]{2,1,0:T(8,128)S(1)}, u32[]{:S(2)}, u32[]{:S(2)}) async-start(f32[8,64,128]{2,1,0:T(8,128)} %get-tuple-element.43), calls=%async_computation.1 | async-start | bytes 524288 | tf_op jit(solution)/shard_map/all_to_all | solution.py:72
  29.2 0.1 sum_forcing.1
  29.3 4.1 %collective-permute-start.4 = (f32[1,8,384]{2,1,0:T(8,128)S(1)}, f32[1,8,384]{2,1,0:T(8,128)S(1)}, u32[]{:S(2)}, u32[]{:S(2)}) collective-permute-start(f32[1,8,384]{2,1,0:T(8,128)S(1)} %get-tuple-element.40), channel_id=1, source_target_pairs={{8,16},{16,8},{9,17},{17,9},{10,18},{18,10},{11,19},{19,11},{12,20... | collective-permute-start | bytes 36872 | tf_op jit(solution)/shard_map/ppermute | solution.py:81
  33.5 0.1 collective-permute-start.5
  33.5 1.4 %finish_adjoint.1 = f32[2,4,16,256]{3,2,1,0:T(8,128)} custom-call(f32[6,4,24,384]{3,2,1,0:T(8,128)S(1)} %get-tuple-element.36.coeffs, f32[16,24,384]{2,1,0:T(8,128)S(1)} %get-tuple-element.37.start, f32[2,3,4,24,384]{4,3,2,1,0:T(8,128)S(1)} %get-tuple-element.42.states), custom_call_target="tpu_custom_call" | custom-call | bytes 1048576 | tf_op jit(solution)/shard_map/finish_adjoint/pallas_call | solution.py:45
  35.0 0.2 collective-permute-done.4.far
  35.1 0.0 collective-permute-done.5.near
  35.1 1.6 %run_forward.1 = f32[2,4,16,256]{3,2,1,0:T(8,128)} custom-call(f32[6,4,24,384]{3,2,1,0:T(8,128)S(1)} %get-tuple-element.36.coeffs, f32[16,24,384]{2,1,0:T(8,128)S(1)} %get-tuple-element.37.start, f32[2,16,384]{2,1,0:T(8,128)S(1)} %get-tuple-element.39.forcing, f32[1,8,384]{2,1,0:T(8,128)S(1)} %collective-permute-done.4.far, ...), custom_call_target="tpu_custom_call" | custom-call | bytes 1048576 | tf_op jit(solution)/shard_map/run_forward/pallas_call | solution.py:45
  36.7 0.0 all-to-all-done.1.gathered
  36.7 3.4 %unweigh.1 = f32[2,1,256,128]{3,2,1,0:T(8,128)} custom-call(f32[8,64,128]{2,1,0:T(8,128)S(1)} %all-to-all-done.1.gathered, f32[8,512]{1,0:T(8,128)S(1)} %get-tuple-element.44.keys, f32[32,128]{1,0:T(8,128)S(1)} %get-tuple-element.45.counts, f32[2,128,128]{2,1,0:T(8,128)S(1)} %get-tuple-element.46.columns_in, f32[2,8,128]{2,1,0:T(8,128)S(1)} %get-tuple-element.47.lines_in, ...), custom_call_target="tpu_custom_call" | custom-call | flops 4294967296 | bytes 1048576 | tf_op jit(solution)/shard_map/unweigh/pallas_call | solution.py:45
  (1 shorter events, 0.0 us)
Async XLA Ops:
  2.1 9.2 %collective-permute-start = (f32[2,16,128]{2,1,0:T(8,128)S(1)}, f32[2,16,128]{2,1,0:T(8,128)S(1)}, u32[]{:S(2)}, u32[]{:S(2)}) collective-permute-start(f32[2,16,128]{2,1,0:T(8,128)S(1)} %get-tuple-element.27), channel_id=1, source_target_pairs={{0,1},{1,0},{2,3},{3,2},{4,5},{5,4},{6,7},{7,6},{8,9},{9,8},{10,11... | collective-permute-start | bytes 49160 | tf_op jit(solution)/shard_map/ppermute | solution.py:82
  4.2 7.1 %collective-permute-start.1 = (f32[2,16,128]{2,1,0:T(8,128)S(1)}, f32[2,16,128]{2,1,0:T(8,128)S(1)}, u32[]{:S(2)}, u32[]{:S(2)}) collective-permute-start(f32[2,16,128]{2,1,0:T(8,128)S(1)} %get-tuple-element.28.after), channel_id=1, source_target_pairs={{1,2},{2,1},{3,4},{4,3},{5,6},{6,5},{7,0},{0,7},{9,10},{10,9},{11,... | collective-permute-start | bytes 49160 | tf_op jit(solution)/shard_map/ppermute | solution.py:81
  11.3 13.2 %all-to-all-start = ((f32[8,72,128]{2,1,0:T(8,128)}), f32[8,72,128]{2,1,0:T(8,128)S(1)}, u32[]{:S(2)}, u32[]{:S(2)}) async-start(f32[8,72,128]{2,1,0:T(8,128)} %get-tuple-element.38), calls=%async_computation | async-start | bytes 589824 | tf_op jit(solution)/shard_map/all_to_all | solution.py:72
  15.0 8.0 %collective-permute-start.2 = (f32[37,8,128]{2,1,0:T(8,128)S(1)}, f32[37,8,128]{2,1,0:T(8,128)S(1)}, u32[]{:S(2)}, u32[]{:S(2)}) collective-permute-start(f32[37,8,128]{2,1,0:T(8,128)S(1)} %get-tuple-element.34), channel_id=1, source_target_pairs={{8,16},{16,8},{9,17},{17,9},{10,18},{18,10},{11,19},{19,11},{12,20... | collective-permute-start | bytes 454664 | tf_op jit(solution)/shard_map/ppermute | solution.py:81
  20.1 2.9 %collective-permute-start.3 = (f32[37,8,128]{2,1,0:T(8,128)S(1)}, f32[37,8,128]{2,1,0:T(8,128)S(1)}, u32[]{:S(2)}, u32[]{:S(2)}) collective-permute-start(f32[37,8,128]{2,1,0:T(8,128)S(1)} %get-tuple-element.35), channel_id=1, source_target_pairs={{0,8},{8,0},{16,24},{24,16},{1,9},{9,1},{17,25},{25,17},{2,10},{10... | collective-permute-start | bytes 454664 | tf_op jit(solution)/shard_map/ppermute | solution.py:82
  24.6 12.1 %all-to-all-start.1 = ((f32[8,64,128]{2,1,0:T(8,128)}), f32[8,64,128]{2,1,0:T(8,128)S(1)}, u32[]{:S(2)}, u32[]{:S(2)}) async-start(f32[8,64,128]{2,1,0:T(8,128)} %get-tuple-element.43), calls=%async_computation.1 | async-start | bytes 524288 | tf_op jit(solution)/shard_map/all_to_all | solution.py:72
  29.3 5.8 %collective-permute-start.4 = (f32[1,8,384]{2,1,0:T(8,128)S(1)}, f32[1,8,384]{2,1,0:T(8,128)S(1)}, u32[]{:S(2)}, u32[]{:S(2)}) collective-permute-start(f32[1,8,384]{2,1,0:T(8,128)S(1)} %get-tuple-element.40), channel_id=1, source_target_pairs={{8,16},{16,8},{9,17},{17,9},{10,18},{18,10},{11,19},{19,11},{12,20... | collective-permute-start | bytes 36872 | tf_op jit(solution)/shard_map/ppermute | solution.py:81
  33.5 1.7 %collective-permute-start.5 = (f32[1,8,384]{2,1,0:T(8,128)S(1)}, f32[1,8,384]{2,1,0:T(8,128)S(1)}, u32[]{:S(2)}, u32[]{:S(2)}) collective-permute-start(f32[1,8,384]{2,1,0:T(8,128)S(1)} %get-tuple-element.41), channel_id=1, source_target_pairs={{0,8},{8,0},{16,24},{24,16},{1,9},{9,1},{17,25},{25,17},{2,10},{10... | collective-permute-start | bytes 36872 | tf_op jit(solution)/shard_map/ppermute | solution.py:82

commit v9 on v7

--- a/solution.py
+++ b/solution.py
@@ -10,6 +10,7 @@
 HALO = STEPS
 PER_LANES = BLOCK // HALO
 GROUP = 16
+FETCH = 4
 f32 = jnp.float32
 bf16 = jnp.bfloat16
 VMEM_LIMIT = 20 * 1024 * 1024
@@ -347,14 +348,14 @@
     return high, (x - high.astype(f32)).astype(bf16)
 
 
-def weight_copies(weights, held, arrived):
-    for g in range(held.shape[0]):
-        yield pltpu.make_async_copy(weights.at[pl.ds(g * GROUP, GROUP)], held.at[g], arrived.at[g])
+def weight_copy(weights, held, arrived, n):
+    own = pl.ds(n * FETCH, FETCH)
+    return pltpu.make_async_copy(weights.at[own], held.at[own], arrived.at[n])
 
 
 def fetch_weights(weights, held, arrived):
-    for copy in weight_copies(weights, held, arrived):
-        copy.start()
+    for n in range(held.shape[0] // FETCH):
+        weight_copy(weights, held, arrived, n).start()
 
 
 def held_part(weights, held, arrived):
@@ -363,9 +364,10 @@
 
             @pl.when(r == 0)
             def _():
-                pltpu.make_async_copy(weights.at[pl.ds(g * GROUP, GROUP)], held.at[g], arrived.at[g]).wait()
-
-        return split(held[g, u])
+                for n in range(GROUP // FETCH):
+                    weight_copy(weights, held, arrived, g * (GROUP // FETCH) + n).wait()
+
+        return split(held[g * GROUP + u])
 
     return part
 
@@ -432,7 +434,7 @@
 
 
 def couple(part, table, capacity, rounds, prepare, columns, lines, starts, transposed, result, scratch):
-    vectors, products, starts_near, moved = scratch
+    vectors, products, starts_near = scratch
     blocks = starts.shape[0]
     total_rows = vectors.shape[0] - capacity
     width = table.shape[0]
@@ -441,8 +443,9 @@
 
     def one_round(r, carry):
         prepare(r)
-        move = pltpu.make_async_copy(starts, starts_near, moved)
-        move.start()
+        first_rows = starts[...]
+        for w in range(blocks):
+            starts_near[w] = first_rows[w, 0]
         place_hot = []
         for n in range(total_rows // BLOCK):
             gather = jnp.broadcast_to(columns[int(transposed), :, n : n + 1], (BLOCK, BLOCK))
@@ -451,11 +454,10 @@
             vectors[n * BLOCK : (n + 1) * BLOCK] = jnp.dot(hot, table, preferred_element_type=f32)
             put = lines[1 - int(transposed), n : n + 1]
             place_hot.append(one_hot(rows((result.shape[0], BLOCK)).astype(f32) == put))
-        move.wait()
 
         def group(g, carry):
             for u in range(GROUP):
-                at = pl.ds(pl.multiple_of(starts_near[g * GROUP + u, 0], 8), capacity)
+                at = pl.ds(pl.multiple_of(starts_near[g * GROUP + u], 8), capacity)
                 own = vectors[at]
                 left = jnp.concatenate([own[:, n * BLOCK : (n + 1) * BLOCK] for n in range(4)], axis=0)
                 high, low = part(r, g, u)
@@ -494,7 +496,7 @@
 def weigh(
     atm_near, margins, weights, after, sums, keys, counts, columns, lines, starts, result, *scratch
 ):
-    scratch, (held, arrived) = scratch[:4], scratch[4:]
+    scratch, (held, arrived) = scratch[:3], scratch[3:]
     fetch_weights(weights, held, arrived)
     lon_count = margins.shape[3]
     blocks = weights.shape[0]
@@ -539,7 +541,7 @@
 def unweigh(
     gathered, keys, counts, columns_in, lines_in, starts_in, weights, gradient, result, columns, lines, starts, *scratch
 ):
-    scratch, (held, arrived) = scratch[:4], scratch[4:]
+    scratch, (held, arrived) = scratch[:3], scratch[3:]
     fetch_weights(weights, held, arrived)
     blocks = weights.shape[0]
     lon_count, ocean_blocks = gathered.shape[0], gathered.shape[1] // 2
@@ -604,7 +606,6 @@
     near_columns, far_columns = swap(near, far, "lon", True)
 
     blocks_of, atm = weights.shape[0], atm_state.shape[2]
-    groups = blocks_of // GROUP
     sum_rows = 2 * halves * tile_lat + tile_lat // 2
     ocean_blocks = lon_count * halves * tile_lat
     chunks = round_chunks(slots, blocks_of)
@@ -615,10 +616,9 @@
             pltpu.VMEM((result_rows, 2 * BLOCK), f32),
             pltpu.VMEM((held_rows, 4 * BLOCK), f32),
             pltpu.VMEM((held_rows, 2 * BLOCK), f32),
-            pltpu.SMEM((blocks_of, BLOCK), jnp.int32),
-            pltpu.SemaphoreType.DMA,
-            pltpu.VMEM((groups, GROUP, BLOCK, BLOCK), f32),
-            pltpu.SemaphoreType.DMA((groups,)),
+            pltpu.SMEM((blocks_of,), jnp.int32),
+            pltpu.VMEM(weights.shape, f32),
+            pltpu.SemaphoreType.DMA((blocks_of // FETCH,)),
         ]
 
     coupling_flops = 4 * slots * blocks_of * 2 * BLOCK * BLOCK * 2

time: 40.8 us -> 40.8 us (level)
  no operation moved by 1% of the time
where the time goes in v9:
time: 40.8 us; the launch traced here: 40.1 us
  starting transfers between devices  23.1 us (57%)
  Pallas kernels  13.4 us (33%)
  waiting for transfers between devices  2.96 us (7%)
  between operations  0.73 us (2%)
    pallas_call x8, Pallas kernels, run(): kernel(*(pltpu.with_memory_space_constraint(x, pltpu.HBM) if n in far els...  13.4 us
    ppermute x3, starting transfers between devices, swap(): far = lax.ppermute(far, axis, pairs[1])  12.6 us
    all_to_all x2, starting transfers between devices, exchange(): lax.all_to_all(x, 'lon', split_axis=0, concat_axis=0, tiled=True, axis_in...  8.24 us
    ppermute x3, waiting for transfers between devices, swap(): far = lax.ppermute(far, axis, pairs[1])  2.95 us
    ppermute x3, starting transfers between devices, swap(): return (lax.ppermute(near, axis, pairs[0]), far)  2.25 us
  transfers between devices with their start and end apart: 8, of which 2 were waited for; matrix products, arithmetic and copies ran while one was open for 0% of the time, Pallas kernels for 21%

profile of v9, /device:TPU:1, one launch (start us, length us, event | category | flops | bytes accessed | tf_op | source)
XLA Modules:
  0.0 40.1 jit_solution(5209826924845218001)
XLA Ops:
  0.6 1.4 %pack_columns.1 = (f32[35,16,256]{2,1,0:T(8,128)S(1)}, f32[2,16,128]{2,1,0:T(8,128)S(1)}, f32[2,16,128]{2,1,0:T(8,128)S(1)}, f32[2,1,256,128]{3,2,1,0:T(8,128)S(1)}, s32[3,1,1,8,64]{4,3,2,1,0:T(8,128)S(1)}) custom-call(f32[2,4,16,256]{3,2,1,0:T(8,128)} %refs_0_.1, f32[2,4,16,256]{3,2,1,0:T(8,128)} %refs_1_.1, s32[4,16,256]{2,1,0:T(8,128)} %refs_2_.1, ...), custom_call_target="tpu_custom_call" | custom-call | bytes 1048576 | tf_op jit(solution)/shard_map/pack_columns/pallas_call | solution.py:46
  2.1 2.1 %collective-permute-start = (f32[2,16,128]{2,1,0:T(8,128)S(1)}, f32[2,16,128]{2,1,0:T(8,128)S(1)}, u32[]{:S(2)}, u32[]{:S(2)}) collective-permute-start(f32[2,16,128]{2,1,0:T(8,128)S(1)} %get-tuple-element.27), channel_id=1, source_target_pairs={{0,1},{1,0},{2,3},{3,2},{4,5},{5,4},{6,7},{7,6},{8,9},{9,8},{10,11... | collective-permute-start | bytes 49160 | tf_op jit(solution)/shard_map/ppermute | solution.py:83
  4.2 3.3 %collective-permute-start.1 = (f32[2,16,128]{2,1,0:T(8,128)S(1)}, f32[2,16,128]{2,1,0:T(8,128)S(1)}, u32[]{:S(2)}, u32[]{:S(2)}) collective-permute-start(f32[2,16,128]{2,1,0:T(8,128)S(1)} %get-tuple-element.28.after), channel_id=1, source_target_pairs={{1,2},{2,1},{3,4},{4,3},{5,6},{6,5},{7,0},{0,7},{9,10},{10,9},{11,... | collective-permute-start | bytes 49160 | tf_op jit(solution)/shard_map/ppermute | solution.py:82
  7.5 3.7 %weigh.1 = (f32[8,72,128]{2,1,0:T(8,128)}, f32[8,512]{1,0:T(8,128)S(1)}, f32[32,128]{1,0:T(8,128)S(1)}, f32[2,128,128]{2,1,0:T(8,128)S(1)}, f32[2,8,128]{2,1,0:T(8,128)S(1)}, /*index=5*/s32[32,128]{1,0:T(8,128)S(1)}) custom-call(f32[2,1,256,128]{3,2,1,0:T(8,128)S(1)} %get-tuple-element.29.atm_near, s32[3,1,1,8,64]{4,3,2,1,0:T(8,128)S(1)} %get-tuple-element.30.margins, ...), custom_call_target="tpu_custom_call" | custom-call | flops 4294967296 | bytes 1048576 | tf_op jit(solution)/shard_map/weigh/pallas_call | solution.py:46
  11.2 0.0 collective-permute-done.near_columns
  11.2 0.0 collective-permute-done.1.far_columns
  11.3 3.6 %all-to-all-start = ((f32[8,72,128]{2,1,0:T(8,128)}), f32[8,72,128]{2,1,0:T(8,128)S(1)}, u32[]{:S(2)}, u32[]{:S(2)}) async-start(f32[8,72,128]{2,1,0:T(8,128)} %get-tuple-element.38), calls=%async_computation | async-start | bytes 589824 | tf_op jit(solution)/shard_map/all_to_all | solution.py:73
  14.9 5.1 %collective-permute-start.2 = (f32[37,8,128]{2,1,0:T(8,128)S(1)}, f32[37,8,128]{2,1,0:T(8,128)S(1)}, u32[]{:S(2)}, u32[]{:S(2)}) collective-permute-start(f32[37,8,128]{2,1,0:T(8,128)S(1)} %get-tuple-element.34), channel_id=1, source_target_pairs={{8,16},{16,8},{9,17},{17,9},{10,18},{18,10},{11,19},{19,11},{12,20... | collective-permute-start | bytes 454664 | tf_op jit(solution)/shard_map/ppermute | solution.py:82
  20.1 0.1 collective-permute-start.3
  20.2 2.8 %collective-permute-done.2.far = f32[37,8,128]{2,1,0:T(8,128)S(1)} collective-permute-done((f32[37,8,128]{2,1,0:T(8,128)S(1)}, f32[37,8,128]{2,1,0:T(8,128)S(1)}, u32[]{:S(2)}, u32[]{:S(2)}) %collective-permute-start.2) | collective-permute-done | bytes 151584 | tf_op jit(solution)/shard_map/ppermute | solution.py:82
  22.9 0.0 collective-permute-done.3.near
  22.9 1.6 %run_adjoint.1 = (f32[8,64,128]{2,1,0:T(8,128)}, f32[6,4,24,384]{3,2,1,0:T(8,128)S(1)}, f32[16,24,384]{2,1,0:T(8,128)S(1)}, f32[2,3,4,24,384]{4,3,2,1,0:T(8,128)S(1)}) custom-call(f32[35,16,256]{2,1,0:T(8,128)S(1)} %get-tuple-element.26.fields, f32[2,16,128]{2,1,0:T(8,128)S(1)} %get-tuple-element.32.from_west, ...), custom_call_target="tpu_custom_call" | custom-call | bytes 1048576 | tf_op jit(solution)/shard_map/run_adjoint/pallas_call | solution.py:46
  24.6 0.0 all-to-all-done.received
  24.6 4.6 %all-to-all-start.1 = ((f32[8,64,128]{2,1,0:T(8,128)}), f32[8,64,128]{2,1,0:T(8,128)S(1)}, u32[]{:S(2)}, u32[]{:S(2)}) async-start(f32[8,64,128]{2,1,0:T(8,128)} %get-tuple-element.43), calls=%async_computation.1 | async-start | bytes 524288 | tf_op jit(solution)/shard_map/all_to_all | solution.py:73
  29.2 0.1 sum_forcing.1
  29.3 4.2 %collective-permute-start.4 = (f32[1,8,384]{2,1,0:T(8,128)S(1)}, f32[1,8,384]{2,1,0:T(8,128)S(1)}, u32[]{:S(2)}, u32[]{:S(2)}) collective-permute-start(f32[1,8,384]{2,1,0:T(8,128)S(1)} %get-tuple-element.40), channel_id=1, source_target_pairs={{8,16},{16,8},{9,17},{17,9},{10,18},{18,10},{11,19},{19,11},{12,20... | collective-permute-start | bytes 36872 | tf_op jit(solution)/shard_map/ppermute | solution.py:82
  33.5 0.1 collective-permute-start.5
  33.5 1.4 %finish_adjoint.1 = f32[2,4,16,256]{3,2,1,0:T(8,128)} custom-call(f32[6,4,24,384]{3,2,1,0:T(8,128)S(1)} %get-tuple-element.36.coeffs, f32[16,24,384]{2,1,0:T(8,128)S(1)} %get-tuple-element.37.start, f32[2,3,4,24,384]{4,3,2,1,0:T(8,128)S(1)} %get-tuple-element.42.states), custom_call_target="tpu_custom_call" | custom-call | bytes 1048576 | tf_op jit(solution)/shard_map/finish_adjoint/pallas_call | solution.py:46
  35.0 0.2 collective-permute-done.4.far
  35.1 0.0 collective-permute-done.5.near
  35.1 1.6 %run_forward.1 = f32[2,4,16,256]{3,2,1,0:T(8,128)} custom-call(f32[6,4,24,384]{3,2,1,0:T(8,128)S(1)} %get-tuple-element.36.coeffs, f32[16,24,384]{2,1,0:T(8,128)S(1)} %get-tuple-element.37.start, f32[2,16,384]{2,1,0:T(8,128)S(1)} %get-tuple-element.39.forcing, f32[1,8,384]{2,1,0:T(8,128)S(1)} %collective-permute-done.4.far, ...), custom_call_target="tpu_custom_call" | custom-call | bytes 1048576 | tf_op jit(solution)/shard_map/run_forward/pallas_call | solution.py:46
  36.7 0.0 all-to-all-done.1.gathered
  36.7 3.4 %unweigh.1 = f32[2,1,256,128]{3,2,1,0:T(8,128)} custom-call(f32[8,64,128]{2,1,0:T(8,128)S(1)} %all-to-all-done.1.gathered, f32[8,512]{1,0:T(8,128)S(1)} %get-tuple-element.44.keys, f32[32,128]{1,0:T(8,128)S(1)} %get-tuple-element.45.counts, f32[2,128,128]{2,1,0:T(8,128)S(1)} %get-tuple-element.46.columns_in, f32[2,8,128]{2,1,0:T(8,128)S(1)} %get-tuple-element.47.lines_in, ...), custom_call_target="tpu_custom_call" | custom-call | flops 4294967296 | bytes 1048576 | tf_op jit(solution)/shard_map/unweigh/pallas_call | solution.py:46
  (1 shorter events, 0.0 us)
Async XLA Ops:
  2.1 9.1 %collective-permute-start = (f32[2,16,128]{2,1,0:T(8,128)S(1)}, f32[2,16,128]{2,1,0:T(8,128)S(1)}, u32[]{:S(2)}, u32[]{:S(2)}) collective-permute-start(f32[2,16,128]{2,1,0:T(8,128)S(1)} %get-tuple-element.27), channel_id=1, source_target_pairs={{0,1},{1,0},{2,3},{3,2},{4,5},{5,4},{6,7},{7,6},{8,9},{9,8},{10,11... | collective-permute-start | bytes 49160 | tf_op jit(solution)/shard_map/ppermute | solution.py:83
  4.2 7.0 %collective-permute-start.1 = (f32[2,16,128]{2,1,0:T(8,128)S(1)}, f32[2,16,128]{2,1,0:T(8,128)S(1)}, u32[]{:S(2)}, u32[]{:S(2)}) collective-permute-start(f32[2,16,128]{2,1,0:T(8,128)S(1)} %get-tuple-element.28.after), channel_id=1, source_target_pairs={{1,2},{2,1},{3,4},{4,3},{5,6},{6,5},{7,0},{0,7},{9,10},{10,9},{11,... | collective-permute-start | bytes 49160 | tf_op jit(solution)/shard_map/ppermute | solution.py:82
  11.3 13.3 %all-to-all-start = ((f32[8,72,128]{2,1,0:T(8,128)}), f32[8,72,128]{2,1,0:T(8,128)S(1)}, u32[]{:S(2)}, u32[]{:S(2)}) async-start(f32[8,72,128]{2,1,0:T(8,128)} %get-tuple-element.38), calls=%async_computation | async-start | bytes 589824 | tf_op jit(solution)/shard_map/all_to_all | solution.py:73
  14.9 8.0 %collective-permute-start.2 = (f32[37,8,128]{2,1,0:T(8,128)S(1)}, f32[37,8,128]{2,1,0:T(8,128)S(1)}, u32[]{:S(2)}, u32[]{:S(2)}) collective-permute-start(f32[37,8,128]{2,1,0:T(8,128)S(1)} %get-tuple-element.34), channel_id=1, source_target_pairs={{8,16},{16,8},{9,17},{17,9},{10,18},{18,10},{11,19},{19,11},{12,20... | collective-permute-start | bytes 454664 | tf_op jit(solution)/shard_map/ppermute | solution.py:82
  20.1 2.9 %collective-permute-start.3 = (f32[37,8,128]{2,1,0:T(8,128)S(1)}, f32[37,8,128]{2,1,0:T(8,128)S(1)}, u32[]{:S(2)}, u32[]{:S(2)}) collective-permute-start(f32[37,8,128]{2,1,0:T(8,128)S(1)} %get-tuple-element.35), channel_id=1, source_target_pairs={{0,8},{8,0},{16,24},{24,16},{1,9},{9,1},{17,25},{25,17},{2,10},{10... | collective-permute-start | bytes 454664 | tf_op jit(solution)/shard_map/ppermute | solution.py:83
  24.6 12.1 %all-to-all-start.1 = ((f32[8,64,128]{2,1,0:T(8,128)}), f32[8,64,128]{2,1,0:T(8,128)S(1)}, u32[]{:S(2)}, u32[]{:S(2)}) async-start(f32[8,64,128]{2,1,0:T(8,128)} %get-tuple-element.43), calls=%async_computation.1 | async-start | bytes 524288 | tf_op jit(solution)/shard_map/all_to_all | solution.py:73
  29.3 5.8 %collective-permute-start.4 = (f32[1,8,384]{2,1,0:T(8,128)S(1)}, f32[1,8,384]{2,1,0:T(8,128)S(1)}, u32[]{:S(2)}, u32[]{:S(2)}) collective-permute-start(f32[1,8,384]{2,1,0:T(8,128)S(1)} %get-tuple-element.40), channel_id=1, source_target_pairs={{8,16},{16,8},{9,17},{17,9},{10,18},{18,10},{11,19},{19,11},{12,20... | collective-permute-start | bytes 36872 | tf_op jit(solution)/shard_map/ppermute | solution.py:82
  33.5 1.7 %collective-permute-start.5 = (f32[1,8,384]{2,1,0:T(8,128)S(1)}, f32[1,8,384]{2,1,0:T(8,128)S(1)}, u32[]{:S(2)}, u32[]{:S(2)}) collective-permute-start(f32[1,8,384]{2,1,0:T(8,128)S(1)} %get-tuple-element.41), channel_id=1, source_target_pairs={{0,8},{8,0},{16,24},{24,16},{1,9},{9,1},{17,25},{25,17},{2,10},{10... | collective-permute-start | bytes 36872 | tf_op jit(solution)/shard_map/ppermute | solution.py:83

commit v10 on v9

--- a/solution.py
+++ b/solution.py
@@ -459,17 +459,14 @@
             for u in range(GROUP):
                 at = pl.ds(pl.multiple_of(starts_near[g * GROUP + u], 8), capacity)
                 own = vectors[at]
-                left = jnp.concatenate([own[:, n * BLOCK : (n + 1) * BLOCK] for n in range(4)], axis=0)
-                high, low = part(r, g, u)
-                right = jnp.concatenate([high, low], axis=1 if transposed else 0)
+                left = jnp.concatenate([own[:, : 2 * BLOCK], own[:, 2 * BLOCK :]], axis=0)
+                both = jnp.concatenate(part(r, g, u), axis=1 if transposed else 0)
+                right = jnp.concatenate([both, both], axis=0 if transposed else 1)
                 contract = (((1,), (0 if transposed else 1,)), ((), ()))
                 product = lax.dot_general(left.astype(bf16), right, contract, preferred_element_type=f32)
                 for f in range(2):
-                    high_part = product[f * capacity : (f + 1) * capacity]
-                    low_part = product[(f + 2) * capacity : (f + 3) * capacity, :BLOCK]
-                    products[at, f * BLOCK : (f + 1) * BLOCK] = (
-                        high_part[:, BLOCK:] + low_part
-                    ) + high_part[:, :BLOCK]
+                    field = product[f * capacity : (f + 1) * capacity]
+                    products[at, f * BLOCK : (f + 1) * BLOCK] = field[:, :BLOCK] + field[:, BLOCK:]
             return carry
 
         lax.fori_loop(0, blocks // GROUP, group, 0)
@@ -508,7 +505,7 @@
     capacity = places(keys.shape[1], blocks)
     rounds = jnp.max(rank).astype(jnp.int32) // capacity + 1
     parts = [split(atm_near[f, 0]) for f in range(2)]
-    table = jnp.concatenate([parts[f][n] for n in range(2) for f in range(2)], axis=1)
+    table = jnp.concatenate([parts[f][n] for f in range(2) for n in range(2)], axis=1)
     part = held_part(weights, held, arrived)
 
     def prepare(r):
@@ -557,7 +554,7 @@
         )
         for f in range(2)
     ]
-    table = jnp.concatenate([parts[f][n] for n in range(2) for f in range(2)], axis=1)
+    table = jnp.concatenate([parts[f][n] for f in range(2) for n in range(2)], axis=1)
 
     def prepare(r):
         @pl.when(r == 0)

time: 40.8 us -> 40.9 us (level)
    ppermute x3, starting transfers between devices: 12.6 us -> 12 us  [swap(): far = lax.ppermute(far, axis, pairs[1])]
    pallas_call x8, Pallas kernels: 13.4 us -> 13.8 us  [run(): kernel(*(pltpu.with_memory_space_constraint(x, pltpu.HBM) if n in far els...]
  transfers between devices with their start and end apart: 8 -> 8, of which waited for: 2 -> 2; matrix products, arithmetic and copies ran while one was open for 0% -> 0% of each run, Pallas kernels for 21% -> 22%
where the time goes in v10:
time: 40.9 us; the launch traced here: 40.2 us
  starting transfers between devices  22.7 us (56%)
  Pallas kernels  13.8 us (34%)
  waiting for transfers between devices  2.99 us (7%)
  between operations  0.73 us (2%)
    pallas_call x8, Pallas kernels, run(): kernel(*(pltpu.with_memory_space_constraint(x, pltpu.HBM) if n in far els...  13.8 us
    ppermute x3, starting transfers between devices, swap(): far = lax.ppermute(far, axis, pairs[1])  12 us
    all_to_all x2, starting transfers between devices, exchange(): lax.all_to_all(x, 'lon', split_axis=0, concat_axis=0, tiled=True, axis_in...  8.4 us
    ppermute x3, waiting for transfers between devices, swap(): far = lax.ppermute(far, axis, pairs[1])  2.98 us
    ppermute x3, starting transfers between devices, swap(): return (lax.ppermute(near, axis, pairs[0]), far)  2.25 us
  transfers between devices with their start and end apart: 8, of which 2 were waited for; matrix products, arithmetic and copies ran while one was open for 0% of the time, Pallas kernels for 22%

profile of v10, /device:TPU:1, one launch (start us, length us, event | category | flops | bytes accessed | tf_op | source)
XLA Modules:
  0.0 40.2 jit_solution(924439356781912322)
XLA Ops:
  0.6 1.4 %pack_columns.1 = (f32[35,16,256]{2,1,0:T(8,128)S(1)}, f32[2,16,128]{2,1,0:T(8,128)S(1)}, f32[2,16,128]{2,1,0:T(8,128)S(1)}, f32[2,1,256,128]{3,2,1,0:T(8,128)S(1)}, s32[3,1,1,8,64]{4,3,2,1,0:T(8,128)S(1)}) custom-call(f32[2,4,16,256]{3,2,1,0:T(8,128)} %refs_0_.1, f32[2,4,16,256]{3,2,1,0:T(8,128)} %refs_1_.1, s32[4,16,256]{2,1,0:T(8,128)} %refs_2_.1, ...), custom_call_target="tpu_custom_call" | custom-call | bytes 1048576 | tf_op jit(solution)/shard_map/pack_columns/pallas_call | solution.py:46
  2.1 2.1 %collective-permute-start = (f32[2,16,128]{2,1,0:T(8,128)S(1)}, f32[2,16,128]{2,1,0:T(8,128)S(1)}, u32[]{:S(2)}, u32[]{:S(2)}) collective-permute-start(f32[2,16,128]{2,1,0:T(8,128)S(1)} %get-tuple-element.27), channel_id=1, source_target_pairs={{0,1},{1,0},{2,3},{3,2},{4,5},{5,4},{6,7},{7,6},{8,9},{9,8},{10,11... | collective-permute-start | bytes 49160 | tf_op jit(solution)/shard_map/ppermute | solution.py:83
  4.2 3.3 %collective-permute-start.1 = (f32[2,16,128]{2,1,0:T(8,128)S(1)}, f32[2,16,128]{2,1,0:T(8,128)S(1)}, u32[]{:S(2)}, u32[]{:S(2)}) collective-permute-start(f32[2,16,128]{2,1,0:T(8,128)S(1)} %get-tuple-element.28.after), channel_id=1, source_target_pairs={{1,2},{2,1},{3,4},{4,3},{5,6},{6,5},{7,0},{0,7},{9,10},{10,9},{11,... | collective-permute-start | bytes 49160 | tf_op jit(solution)/shard_map/ppermute | solution.py:82
  7.5 4.2 %weigh.1 = (f32[8,72,128]{2,1,0:T(8,128)}, f32[8,512]{1,0:T(8,128)S(1)}, f32[32,128]{1,0:T(8,128)S(1)}, f32[2,128,128]{2,1,0:T(8,128)S(1)}, f32[2,8,128]{2,1,0:T(8,128)S(1)}, /*index=5*/s32[32,128]{1,0:T(8,128)S(1)}) custom-call(f32[2,1,256,128]{3,2,1,0:T(8,128)S(1)} %get-tuple-element.29.atm_near, s32[3,1,1,8,64]{4,3,2,1,0:T(8,128)S(1)} %get-tuple-element.30.margins, ...), custom_call_target="tpu_custom_call" | custom-call | flops 4294967296 | bytes 1048576 | tf_op jit(solution)/shard_map/weigh/pallas_call | solution.py:46
  11.7 0.0 collective-permute-done.near_columns
  11.7 0.0 collective-permute-done.1.far_columns
  11.8 3.6 %all-to-all-start = ((f32[8,72,128]{2,1,0:T(8,128)}), f32[8,72,128]{2,1,0:T(8,128)S(1)}, u32[]{:S(2)}, u32[]{:S(2)}) async-start(f32[8,72,128]{2,1,0:T(8,128)} %get-tuple-element.38), calls=%async_computation | async-start | bytes 589824 | tf_op jit(solution)/shard_map/all_to_all | solution.py:73
  15.4 4.8 %collective-permute-start.2 = (f32[37,8,128]{2,1,0:T(8,128)S(1)}, f32[37,8,128]{2,1,0:T(8,128)S(1)}, u32[]{:S(2)}, u32[]{:S(2)}) collective-permute-start(f32[37,8,128]{2,1,0:T(8,128)S(1)} %get-tuple-element.34), channel_id=1, source_target_pairs={{8,16},{16,8},{9,17},{17,9},{10,18},{18,10},{11,19},{19,11},{12,20... | collective-permute-start | bytes 454664 | tf_op jit(solution)/shard_map/ppermute | solution.py:82
  20.2 0.1 collective-permute-start.3
  20.3 2.9 %collective-permute-done.2.far = f32[37,8,128]{2,1,0:T(8,128)S(1)} collective-permute-done((f32[37,8,128]{2,1,0:T(8,128)S(1)}, f32[37,8,128]{2,1,0:T(8,128)S(1)}, u32[]{:S(2)}, u32[]{:S(2)}) %collective-permute-start.2) | collective-permute-done | bytes 151584 | tf_op jit(solution)/shard_map/ppermute | solution.py:82
  23.2 0.0 collective-permute-done.3.near
  23.2 1.6 %run_adjoint.1 = (f32[8,64,128]{2,1,0:T(8,128)}, f32[6,4,24,384]{3,2,1,0:T(8,128)S(1)}, f32[16,24,384]{2,1,0:T(8,128)S(1)}, f32[2,3,4,24,384]{4,3,2,1,0:T(8,128)S(1)}) custom-call(f32[35,16,256]{2,1,0:T(8,128)S(1)} %get-tuple-element.26.fields, f32[2,16,128]{2,1,0:T(8,128)S(1)} %get-tuple-element.32.from_west, ...), custom_call_target="tpu_custom_call" | custom-call | bytes 1048576 | tf_op jit(solution)/shard_map/run_adjoint/pallas_call | solution.py:46
  24.8 0.0 all-to-all-done.received
  24.8 4.8 %all-to-all-start.1 = ((f32[8,64,128]{2,1,0:T(8,128)}), f32[8,64,128]{2,1,0:T(8,128)S(1)}, u32[]{:S(2)}, u32[]{:S(2)}) async-start(f32[8,64,128]{2,1,0:T(8,128)} %get-tuple-element.43), calls=%async_computation.1 | async-start | bytes 524288 | tf_op jit(solution)/shard_map/all_to_all | solution.py:73
  29.6 0.1 sum_forcing.1
  29.7 3.9 %collective-permute-start.4 = (f32[1,8,384]{2,1,0:T(8,128)S(1)}, f32[1,8,384]{2,1,0:T(8,128)S(1)}, u32[]{:S(2)}, u32[]{:S(2)}) collective-permute-start(f32[1,8,384]{2,1,0:T(8,128)S(1)} %get-tuple-element.40), channel_id=1, source_target_pairs={{8,16},{16,8},{9,17},{17,9},{10,18},{18,10},{11,19},{19,11},{12,20... | collective-permute-start | bytes 36872 | tf_op jit(solution)/shard_map/ppermute | solution.py:82
  33.6 0.1 collective-permute-start.5
  33.7 1.4 %finish_adjoint.1 = f32[2,4,16,256]{3,2,1,0:T(8,128)} custom-call(f32[6,4,24,384]{3,2,1,0:T(8,128)S(1)} %get-tuple-element.36.coeffs, f32[16,24,384]{2,1,0:T(8,128)S(1)} %get-tuple-element.37.start, f32[2,3,4,24,384]{4,3,2,1,0:T(8,128)S(1)} %get-tuple-element.42.states), custom_call_target="tpu_custom_call" | custom-call | bytes 1048576 | tf_op jit(solution)/shard_map/finish_adjoint/pallas_call | solution.py:46
  35.1 0.1 collective-permute-done.4.far
  35.2 0.0 collective-permute-done.5.near
  35.2 1.6 %run_forward.1 = f32[2,4,16,256]{3,2,1,0:T(8,128)} custom-call(f32[6,4,24,384]{3,2,1,0:T(8,128)S(1)} %get-tuple-element.36.coeffs, f32[16,24,384]{2,1,0:T(8,128)S(1)} %get-tuple-element.37.start, f32[2,16,384]{2,1,0:T(8,128)S(1)} %get-tuple-element.39.forcing, f32[1,8,384]{2,1,0:T(8,128)S(1)} %collective-permute-done.4.far, ...), custom_call_target="tpu_custom_call" | custom-call | bytes 1048576 | tf_op jit(solution)/shard_map/run_forward/pallas_call | solution.py:46
  36.8 0.0 all-to-all-done.1.gathered
  36.8 3.4 %unweigh.1 = f32[2,1,256,128]{3,2,1,0:T(8,128)} custom-call(f32[8,64,128]{2,1,0:T(8,128)S(1)} %all-to-all-done.1.gathered, f32[8,512]{1,0:T(8,128)S(1)} %get-tuple-element.44.keys, f32[32,128]{1,0:T(8,128)S(1)} %get-tuple-element.45.counts, f32[2,128,128]{2,1,0:T(8,128)S(1)} %get-tuple-element.46.columns_in, f32[2,8,128]{2,1,0:T(8,128)S(1)} %get-tuple-element.47.lines_in, ...), custom_call_target="tpu_custom_call" | custom-call | flops 4294967296 | bytes 1048576 | tf_op jit(solution)/shard_map/unweigh/pallas_call | solution.py:46
  (1 shorter events, 0.0 us)
Async XLA Ops:
  2.1 9.6 %collective-permute-start = (f32[2,16,128]{2,1,0:T(8,128)S(1)}, f32[2,16,128]{2,1,0:T(8,128)S(1)}, u32[]{:S(2)}, u32[]{:S(2)}) collective-permute-start(f32[2,16,128]{2,1,0:T(8,128)S(1)} %get-tuple-element.27), channel_id=1, source_target_pairs={{0,1},{1,0},{2,3},{3,2},{4,5},{5,4},{6,7},{7,6},{8,9},{9,8},{10,11... | collective-permute-start | bytes 49160 | tf_op jit(solution)/shard_map/ppermute | solution.py:83
  4.2 7.5 %collective-permute-start.1 = (f32[2,16,128]{2,1,0:T(8,128)S(1)}, f32[2,16,128]{2,1,0:T(8,128)S(1)}, u32[]{:S(2)}, u32[]{:S(2)}) collective-permute-start(f32[2,16,128]{2,1,0:T(8,128)S(1)} %get-tuple-element.28.after), channel_id=1, source_target_pairs={{1,2},{2,1},{3,4},{4,3},{5,6},{6,5},{7,0},{0,7},{9,10},{10,9},{11,... | collective-permute-start | bytes 49160 | tf_op jit(solution)/shard_map/ppermute | solution.py:82
  11.8 13.1 %all-to-all-start = ((f32[8,72,128]{2,1,0:T(8,128)}), f32[8,72,128]{2,1,0:T(8,128)S(1)}, u32[]{:S(2)}, u32[]{:S(2)}) async-start(f32[8,72,128]{2,1,0:T(8,128)} %get-tuple-element.38), calls=%async_computation | async-start | bytes 589824 | tf_op jit(solution)/shard_map/all_to_all | solution.py:73
  15.4 7.8 %collective-permute-start.2 = (f32[37,8,128]{2,1,0:T(8,128)S(1)}, f32[37,8,128]{2,1,0:T(8,128)S(1)}, u32[]{:S(2)}, u32[]{:S(2)}) collective-permute-start(f32[37,8,128]{2,1,0:T(8,128)S(1)} %get-tuple-element.34), channel_id=1, source_target_pairs={{8,16},{16,8},{9,17},{17,9},{10,18},{18,10},{11,19},{19,11},{12,20... | collective-permute-start | bytes 454664 | tf_op jit(solution)/shard_map/ppermute | solution.py:82
  20.2 3.0 %collective-permute-start.3 = (f32[37,8,128]{2,1,0:T(8,128)S(1)}, f32[37,8,128]{2,1,0:T(8,128)S(1)}, u32[]{:S(2)}, u32[]{:S(2)}) collective-permute-start(f32[37,8,128]{2,1,0:T(8,128)S(1)} %get-tuple-element.35), channel_id=1, source_target_pairs={{0,8},{8,0},{16,24},{24,16},{1,9},{9,1},{17,25},{25,17},{2,10},{10... | collective-permute-start | bytes 454664 | tf_op jit(solution)/shard_map/ppermute | solution.py:83
  24.8 12.0 %all-to-all-start.1 = ((f32[8,64,128]{2,1,0:T(8,128)}), f32[8,64,128]{2,1,0:T(8,128)S(1)}, u32[]{:S(2)}, u32[]{:S(2)}) async-start(f32[8,64,128]{2,1,0:T(8,128)} %get-tuple-element.43), calls=%async_computation.1 | async-start | bytes 524288 | tf_op jit(solution)/shard_map/all_to_all | solution.py:73
  29.7 5.5 %collective-permute-start.4 = (f32[1,8,384]{2,1,0:T(8,128)S(1)}, f32[1,8,384]{2,1,0:T(8,128)S(1)}, u32[]{:S(2)}, u32[]{:S(2)}) collective-permute-start(f32[1,8,384]{2,1,0:T(8,128)S(1)} %get-tuple-element.40), channel_id=1, source_target_pairs={{8,16},{16,8},{9,17},{17,9},{10,18},{18,10},{11,19},{19,11},{12,20... | collective-permute-start | bytes 36872 | tf_op jit(solution)/shard_map/ppermute | solution.py:82
  33.6 1.6 %collective-permute-start.5 = (f32[1,8,384]{2,1,0:T(8,128)S(1)}, f32[1,8,384]{2,1,0:T(8,128)S(1)}, u32[]{:S(2)}, u32[]{:S(2)}) collective-permute-start(f32[1,8,384]{2,1,0:T(8,128)S(1)} %get-tuple-element.41), channel_id=1, source_target_pairs={{0,8},{8,0},{16,24},{24,16},{1,9},{9,1},{17,25},{25,17},{2,10},{10... | collective-permute-start | bytes 36872 | tf_op jit(solution)/shard_map/ppermute | solution.py:83

commit v11 on v9

--- a/solution.py
+++ b/solution.py
@@ -64,8 +64,8 @@
 
 
 def group_order(count):
-    half = count // 2
-    return [k for n in range(half) for k in (half + n, n)]
+    half, quarter = count // 2, count // 4
+    return [k for n in range(half) for k in ((n + quarter) % half, half + (n + quarter) % half)]
 
 
 def exchange(x):
@@ -315,7 +315,7 @@
     near[0], far[0] = sort_swap("lat", to_north, to_south)
 
 
-def run_forward(coeffs, start, forcing, far, near, final, state):
+def run_forward(coeffs, start, forcing, near, far, final, state):
     levels = coeffs.shape[1]
     tile_lat, tile_lon = final.shape[2:]
     for f in range(2):
@@ -685,7 +685,7 @@
         [pltpu.VMEM((2, levels, *wide), f32)],
         name="run_forward",
         inputs=5,
-    )(coeffs, start, forcing, far_rows, near_rows)
+    )(coeffs, start, forcing, near_rows, far_rows)
 
     (gradient,) = call(
         unweigh,

time: 40.8 us -> 41 us (level)
  waiting for transfers between devices: 2.96 us -> 3.79 us
    all_to_all x2, starting transfers between devices: 8.24 us -> 7.64 us  [exchange(): lax.all_to_all(x, 'lon', split_axis=0, concat_axis=0, tiled=True, axis_in...]
    all_to_all x2, waiting for transfers between devices: 0.01 us -> 0.47 us  [exchange(): lax.all_to_all(x, 'lon', split_axis=0, concat_axis=0, tiled=True, axis_in...]
  transfers between devices with their start and end apart: 8 -> 8, of which waited for: 2 -> 3; matrix products, arithmetic and copies ran while one was open for 0% -> 0% of each run, Pallas kernels for 21% -> 21%
where the time goes in v11:
time: 41 us; the launch traced here: 40.6 us
  starting transfers between devices  22.7 us (55%)
  Pallas kernels  13.4 us (33%)
  waiting for transfers between devices  3.79 us (9%)
  between operations  0.73 us (2%)
    pallas_call x8, Pallas kernels, run(): kernel(*(pltpu.with_memory_space_constraint(x, pltpu.HBM) if n in far els...  13.4 us
    ppermute x3, starting transfers between devices, swap(): far = lax.ppermute(far, axis, pairs[1])  12.9 us
    all_to_all x2, starting transfers between devices, exchange(): lax.all_to_all(x, 'lon', split_axis=0, concat_axis=0, tiled=True, axis_in...  7.64 us
    ppermute x3, waiting for transfers between devices, swap(): far = lax.ppermute(far, axis, pairs[1])  3.32 us
    ppermute x3, starting transfers between devices, swap(): return (lax.ppermute(near, axis, pairs[0]), far)  2.18 us
  transfers between devices with their start and end apart: 8, of which 3 were waited for; matrix products, arithmetic and copies ran while one was open for 0% of the time, Pallas kernels for 21%

profile of v11, /device:TPU:1, one launch (start us, length us, event | category | flops | bytes accessed | tf_op | source)
XLA Modules:
  0.0 40.6 jit_solution(4750091471086388162)
XLA Ops:
  0.6 1.4 %pack_columns.1 = (f32[35,16,256]{2,1,0:T(8,128)S(1)}, f32[2,16,128]{2,1,0:T(8,128)S(1)}, f32[2,16,128]{2,1,0:T(8,128)S(1)}, f32[2,1,256,128]{3,2,1,0:T(8,128)S(1)}, s32[3,1,1,8,64]{4,3,2,1,0:T(8,128)S(1)}) custom-call(f32[2,4,16,256]{3,2,1,0:T(8,128)} %refs_0_.1, f32[2,4,16,256]{3,2,1,0:T(8,128)} %refs_1_.1, s32[4,16,256]{2,1,0:T(8,128)} %refs_2_.1, ...), custom_call_target="tpu_custom_call" | custom-call | bytes 1048576 | tf_op jit(solution)/shard_map/pack_columns/pallas_call | solution.py:46
  2.1 2.1 %collective-permute-start = (f32[2,16,128]{2,1,0:T(8,128)S(1)}, f32[2,16,128]{2,1,0:T(8,128)S(1)}, u32[]{:S(2)}, u32[]{:S(2)}) collective-permute-start(f32[2,16,128]{2,1,0:T(8,128)S(1)} %get-tuple-element.27), channel_id=1, source_target_pairs={{0,1},{1,0},{2,3},{3,2},{4,5},{5,4},{6,7},{7,6},{8,9},{9,8},{10,11... | collective-permute-start | bytes 49160 | tf_op jit(solution)/shard_map/ppermute | solution.py:83
  4.2 3.3 %collective-permute-start.1 = (f32[2,16,128]{2,1,0:T(8,128)S(1)}, f32[2,16,128]{2,1,0:T(8,128)S(1)}, u32[]{:S(2)}, u32[]{:S(2)}) collective-permute-start(f32[2,16,128]{2,1,0:T(8,128)S(1)} %get-tuple-element.28.after), channel_id=1, source_target_pairs={{1,2},{2,1},{3,4},{4,3},{5,6},{6,5},{7,0},{0,7},{9,10},{10,9},{11,... | collective-permute-start | bytes 49160 | tf_op jit(solution)/shard_map/ppermute | solution.py:82
  7.5 3.7 %weigh.1 = (f32[8,72,128]{2,1,0:T(8,128)}, f32[8,512]{1,0:T(8,128)S(1)}, f32[32,128]{1,0:T(8,128)S(1)}, f32[2,128,128]{2,1,0:T(8,128)S(1)}, f32[2,8,128]{2,1,0:T(8,128)S(1)}, /*index=5*/s32[32,128]{1,0:T(8,128)S(1)}) custom-call(f32[2,1,256,128]{3,2,1,0:T(8,128)S(1)} %get-tuple-element.29.atm_near, s32[3,1,1,8,64]{4,3,2,1,0:T(8,128)S(1)} %get-tuple-element.30.margins, ...), custom_call_target="tpu_custom_call" | custom-call | flops 4294967296 | bytes 1048576 | tf_op jit(solution)/shard_map/weigh/pallas_call | solution.py:46
  11.2 0.0 collective-permute-done.near_columns
  11.2 0.0 collective-permute-done.1.far_columns
  11.3 3.4 %all-to-all-start = ((f32[8,72,128]{2,1,0:T(8,128)}), f32[8,72,128]{2,1,0:T(8,128)S(1)}, u32[]{:S(2)}, u32[]{:S(2)}) async-start(f32[8,72,128]{2,1,0:T(8,128)} %get-tuple-element.38), calls=%async_computation | async-start | bytes 589824 | tf_op jit(solution)/shard_map/all_to_all | solution.py:73
  14.7 5.4 %collective-permute-start.2 = (f32[37,8,128]{2,1,0:T(8,128)S(1)}, f32[37,8,128]{2,1,0:T(8,128)S(1)}, u32[]{:S(2)}, u32[]{:S(2)}) collective-permute-start(f32[37,8,128]{2,1,0:T(8,128)S(1)} %get-tuple-element.34), channel_id=1, source_target_pairs={{8,16},{16,8},{9,17},{17,9},{10,18},{18,10},{11,19},{19,11},{12,20... | collective-permute-start | bytes 454664 | tf_op jit(solution)/shard_map/ppermute | solution.py:82
  20.1 0.1 collective-permute-start.3
  20.2 3.1 %collective-permute-done.2.far = f32[37,8,128]{2,1,0:T(8,128)S(1)} collective-permute-done((f32[37,8,128]{2,1,0:T(8,128)S(1)}, f32[37,8,128]{2,1,0:T(8,128)S(1)}, u32[]{:S(2)}, u32[]{:S(2)}) %collective-permute-start.2) | collective-permute-done | bytes 151584 | tf_op jit(solution)/shard_map/ppermute | solution.py:82
  23.2 0.0 collective-permute-done.3.near
  23.2 1.6 %run_adjoint.1 = (f32[8,64,128]{2,1,0:T(8,128)}, f32[6,4,24,384]{3,2,1,0:T(8,128)S(1)}, f32[16,24,384]{2,1,0:T(8,128)S(1)}, f32[2,3,4,24,384]{4,3,2,1,0:T(8,128)S(1)}) custom-call(f32[35,16,256]{2,1,0:T(8,128)S(1)} %get-tuple-element.26.fields, f32[2,16,128]{2,1,0:T(8,128)S(1)} %get-tuple-element.32.from_west, ...), custom_call_target="tpu_custom_call" | custom-call | bytes 1048576 | tf_op jit(solution)/shard_map/run_adjoint/pallas_call | solution.py:46
  24.9 0.0 all-to-all-done.received
  24.9 4.3 %all-to-all-start.1 = ((f32[8,64,128]{2,1,0:T(8,128)}), f32[8,64,128]{2,1,0:T(8,128)S(1)}, u32[]{:S(2)}, u32[]{:S(2)}) async-start(f32[8,64,128]{2,1,0:T(8,128)} %get-tuple-element.43), calls=%async_computation.1 | async-start | bytes 524288 | tf_op jit(solution)/shard_map/all_to_all | solution.py:73
  29.1 0.1 sum_forcing.1
  29.3 0.0 collective-permute-start.4
  29.3 4.2 %collective-permute-start.5 = (f32[1,8,384]{2,1,0:T(8,128)S(1)}, f32[1,8,384]{2,1,0:T(8,128)S(1)}, u32[]{:S(2)}, u32[]{:S(2)}) collective-permute-start(f32[1,8,384]{2,1,0:T(8,128)S(1)} %get-tuple-element.41), channel_id=1, source_target_pairs={{8,16},{16,8},{9,17},{17,9},{10,18},{18,10},{11,19},{19,11},{12,20... | collective-permute-start | bytes 36872 | tf_op jit(solution)/shard_map/ppermute | solution.py:82
  33.5 1.4 %finish_adjoint.1 = f32[2,4,16,256]{3,2,1,0:T(8,128)} custom-call(f32[6,4,24,384]{3,2,1,0:T(8,128)S(1)} %get-tuple-element.36.coeffs, f32[16,24,384]{2,1,0:T(8,128)S(1)} %get-tuple-element.37.start, f32[2,3,4,24,384]{4,3,2,1,0:T(8,128)S(1)} %get-tuple-element.42.states), custom_call_target="tpu_custom_call" | custom-call | bytes 1048576 | tf_op jit(solution)/shard_map/finish_adjoint/pallas_call | solution.py:46
  34.9 0.0 collective-permute-done.4.near
  34.9 0.2 collective-permute-done.5.far
  35.1 1.6 %run_forward.1 = f32[2,4,16,256]{3,2,1,0:T(8,128)} custom-call(f32[6,4,24,384]{3,2,1,0:T(8,128)S(1)} %get-tuple-element.36.coeffs, f32[16,24,384]{2,1,0:T(8,128)S(1)} %get-tuple-element.37.start, f32[2,16,384]{2,1,0:T(8,128)S(1)} %get-tuple-element.39.forcing, f32[1,8,384]{2,1,0:T(8,128)S(1)} %collective-permute-done.4.near, ...), custom_call_target="tpu_custom_call" | custom-call | bytes 1048576 | tf_op jit(solution)/shard_map/run_forward/pallas_call | solution.py:46
  36.7 0.5 %all-to-all-done.1.gathered = f32[8,64,128]{2,1,0:T(8,128)S(1)} async-done(((f32[8,64,128]{2,1,0:T(8,128)}), f32[8,64,128]{2,1,0:T(8,128)S(1)}, u32[]{:S(2)}, u32[]{:S(2)}) %all-to-all-start.1) | async-done | bytes 262176 | tf_op jit(solution)/shard_map/all_to_all | solution.py:73
  37.2 3.4 %unweigh.1 = f32[2,1,256,128]{3,2,1,0:T(8,128)} custom-call(f32[8,64,128]{2,1,0:T(8,128)S(1)} %all-to-all-done.1.gathered, f32[8,512]{1,0:T(8,128)S(1)} %get-tuple-element.44.keys, f32[32,128]{1,0:T(8,128)S(1)} %get-tuple-element.45.counts, f32[2,128,128]{2,1,0:T(8,128)S(1)} %get-tuple-element.46.columns_in, f32[2,8,128]{2,1,0:T(8,128)S(1)} %get-tuple-element.47.lines_in, ...), custom_call_target="tpu_custom_call" | custom-call | flops 4294967296 | bytes 1048576 | tf_op jit(solution)/shard_map/unweigh/pallas_call | solution.py:46
  (1 shorter events, 0.0 us)
Async XLA Ops:
  2.1 9.1 %collective-permute-start = (f32[2,16,128]{2,1,0:T(8,128)S(1)}, f32[2,16,128]{2,1,0:T(8,128)S(1)}, u32[]{:S(2)}, u32[]{:S(2)}) collective-permute-start(f32[2,16,128]{2,1,0:T(8,128)S(1)} %get-tuple-element.27), channel_id=1, source_target_pairs={{0,1},{1,0},{2,3},{3,2},{4,5},{5,4},{6,7},{7,6},{8,9},{9,8},{10,11... | collective-permute-start | bytes 49160 | tf_op jit(solution)/shard_map/ppermute | solution.py:83
  4.2 7.0 %collective-permute-start.1 = (f32[2,16,128]{2,1,0:T(8,128)S(1)}, f32[2,16,128]{2,1,0:T(8,128)S(1)}, u32[]{:S(2)}, u32[]{:S(2)}) collective-permute-start(f32[2,16,128]{2,1,0:T(8,128)S(1)} %get-tuple-element.28.after), channel_id=1, source_target_pairs={{1,2},{2,1},{3,4},{4,3},{5,6},{6,5},{7,0},{0,7},{9,10},{10,9},{11,... | collective-permute-start | bytes 49160 | tf_op jit(solution)/shard_map/ppermute | solution.py:82
  11.3 13.6 %all-to-all-start = ((f32[8,72,128]{2,1,0:T(8,128)}), f32[8,72,128]{2,1,0:T(8,128)S(1)}, u32[]{:S(2)}, u32[]{:S(2)}) async-start(f32[8,72,128]{2,1,0:T(8,128)} %get-tuple-element.38), calls=%async_computation | async-start | bytes 589824 | tf_op jit(solution)/shard_map/all_to_all | solution.py:73
  14.7 8.6 %collective-permute-start.2 = (f32[37,8,128]{2,1,0:T(8,128)S(1)}, f32[37,8,128]{2,1,0:T(8,128)S(1)}, u32[]{:S(2)}, u32[]{:S(2)}) collective-permute-start(f32[37,8,128]{2,1,0:T(8,128)S(1)} %get-tuple-element.34), channel_id=1, source_target_pairs={{8,16},{16,8},{9,17},{17,9},{10,18},{18,10},{11,19},{19,11},{12,20... | collective-permute-start | bytes 454664 | tf_op jit(solution)/shard_map/ppermute | solution.py:82
  20.1 3.2 %collective-permute-start.3 = (f32[37,8,128]{2,1,0:T(8,128)S(1)}, f32[37,8,128]{2,1,0:T(8,128)S(1)}, u32[]{:S(2)}, u32[]{:S(2)}) collective-permute-start(f32[37,8,128]{2,1,0:T(8,128)S(1)} %get-tuple-element.35), channel_id=1, source_target_pairs={{0,8},{8,0},{16,24},{24,16},{1,9},{9,1},{17,25},{25,17},{2,10},{10... | collective-permute-start | bytes 454664 | tf_op jit(solution)/shard_map/ppermute | solution.py:83
  24.9 12.3 %all-to-all-start.1 = ((f32[8,64,128]{2,1,0:T(8,128)}), f32[8,64,128]{2,1,0:T(8,128)S(1)}, u32[]{:S(2)}, u32[]{:S(2)}) async-start(f32[8,64,128]{2,1,0:T(8,128)} %get-tuple-element.43), calls=%async_computation.1 | async-start | bytes 524288 | tf_op jit(solution)/shard_map/all_to_all | solution.py:73
  29.3 5.6 %collective-permute-start.4 = (f32[1,8,384]{2,1,0:T(8,128)S(1)}, f32[1,8,384]{2,1,0:T(8,128)S(1)}, u32[]{:S(2)}, u32[]{:S(2)}) collective-permute-start(f32[1,8,384]{2,1,0:T(8,128)S(1)} %get-tuple-element.40), channel_id=1, source_target_pairs={{0,8},{8,0},{16,24},{24,16},{1,9},{9,1},{17,25},{25,17},{2,10},{10... | collective-permute-start | bytes 36872 | tf_op jit(solution)/shard_map/ppermute | solution.py:83
  29.3 5.9 %collective-permute-start.5 = (f32[1,8,384]{2,1,0:T(8,128)S(1)}, f32[1,8,384]{2,1,0:T(8,128)S(1)}, u32[]{:S(2)}, u32[]{:S(2)}) collective-permute-start(f32[1,8,384]{2,1,0:T(8,128)S(1)} %get-tuple-element.41), channel_id=1, source_target_pairs={{8,16},{16,8},{9,17},{17,9},{10,18},{18,10},{11,19},{19,11},{12,20... | collective-permute-start | bytes 36872 | tf_op jit(solution)/shard_map/ppermute | solution.py:82

commit v12 on v11

--- a/solution.py
+++ b/solution.py
@@ -171,20 +171,6 @@
     return jnp.where(rows(from_north.shape) < HALO, from_north, from_south)
 
 
-def widen(fields, from_west, from_east, near, far, start, wide):
-    count, tile_lat, tile_lon = fields.shape
-    halves = tile_lon // BLOCK
-    parts = from_west.shape[0]
-    corners = [edge_rows(near, far, count * halves + n) for n in range(2 * parts)]
-    for i in range(count):
-        out = start.at[i] if i < start.shape[0] else wide.at[i - start.shape[0]]
-        out[:tile_lat, :tile_lon] = fields[i]
-        out[:tile_lat, tile_lon:] = unpack_columns(from_west, from_east, i)
-        for h in range(halves):
-            out[tile_lat:, h * BLOCK : (h + 1) * BLOCK] = edge_rows(near, far, i * halves + h)
-        out[tile_lat:, tile_lon:] = unpack_columns(corners[:parts], corners[parts:], i)
-
-
 def eastward(x):
     return turn(x, -1, 1)
 
@@ -201,19 +187,50 @@
     return turn(x, 1, 0)
 
 
-def adjoint_step(coeffs, read, write, first, last):
+def prepare_stencil(fields, from_west, from_east, start, coeffs):
     levels = coeffs.shape[1]
-    above = coeffs[4, first - 1] * (read(first) - read(first - 1)) if first else None
+
+    def wide(i):
+        return jnp.concatenate([fields[i], unpack_columns(from_west, from_east, i)], axis=1)
+
+    for i in range(4 * levels):
+        start[i] = wide(i)
+    for level in range(levels):
+        east_k, east_v, north_k, north_v = (wide((4 + n) * levels + level) for n in range(4))
+        mask = (east_k > 0.0).astype(f32)
+        coeffs[0, level], coeffs[1, level] = upwind(east_k, east_v, eastward(mask))
+        coeffs[2, level], coeffs[3, level] = north_k, north_v
+        if level < levels - 1:
+            coeffs[4, level] = wide(8 * levels + level)
+        coeffs[5, level] = mask
+
+
+def upwind(diffusion, velocity, mask):
+    diffusion, velocity = diffusion * mask, velocity * mask
+    return jnp.maximum(velocity, 0.0) + diffusion, jnp.minimum(velocity, 0.0) - diffusion
+
+
+def whole_rows(inner, outer):
+    return lambda *at: jnp.concatenate([inner[at], outer[at]], axis=0)
+
+
+def coefficients(inner, outer, north):
+    whole = whole_rows(inner, outer)
+    return lambda n, level: north[n - 2, level] if n in (2, 3) else whole(n, level)
+
+
+def adjoint_step(coeffs, levels, read, write, first, last):
+    above = coeffs(4, first - 1) * (read(first) - read(first - 1)) if first else None
     for level in range(first, last):
         lam = read(level)
         step_x = eastward(lam) - lam
         step_y = northward(lam) - lam
-        out = lam + coeffs[0, level] * step_x + westward(coeffs[1, level] * step_x)
-        out = out + coeffs[2, level] * step_y + southward(coeffs[3, level] * step_y)
+        out = lam + coeffs(0, level) * step_x + westward(coeffs(1, level) * step_x)
+        out = out + coeffs(2, level) * step_y + southward(coeffs(3, level) * step_y)
         if above is not None:
             out = out - above
         if level < levels - 1:
-            above = coeffs[4, level] * (read(level + 1) - lam)
+            above = coeffs(4, level) * (read(level + 1) - lam)
             out = out + above
         write(level, out)
 
@@ -223,42 +240,48 @@
 
 
 def run_adjoint(
-    fields, from_west, from_east, far, near, blocks, coeffs, start, states, wide, own, sent
+    start_in, coeffs_in, from_west, from_east, far, near, blocks, start_out, coeffs_out, north, states, own, sent
 ):
-    levels = coeffs.shape[1]
-    tile_lat, tile_lon = fields.shape[1:]
+    levels, tile_lat = coeffs_in.shape[1:3]
+    tile_lon = coeffs_in.shape[3] - BLOCK
     halves = tile_lon // BLOCK
-    widen(fields, from_west, from_east, near, far, start, wide)
-    base = 0
-    mask0 = None
+    parts = from_west.shape[0]
+    count = 9 * levels - 1
+    corners = [edge_rows(near, far, count * halves + n) for n in range(2 * parts)]
+
+    def outer(i):
+        out = [edge_rows(near, far, i * halves + h) for h in range(halves)]
+        return jnp.concatenate([*out, unpack_columns(corners[:parts], corners[parts:], i)], axis=1)
+
+    for i in range(4 * levels):
+        start_out[i] = outer(i)
     for level in range(levels):
-        east_d, east_u = wide[base + level], wide[base + levels + level]
-        north_d, north_u = wide[base + 2 * levels + level], wide[base + 3 * levels + level]
-        mask = (east_d > 0.0).astype(f32)
-        mask0 = mask if mask0 is None else mask0
-        mask_e, mask_n = eastward(mask), northward(mask)
-        east_k, east_v = east_d * mask_e, east_u * mask_e
-        north_k, north_v = north_d * mask_n, north_u * mask_n
-        coeffs[0, level] = jnp.maximum(east_v, 0.0) + east_k
-        coeffs[1, level] = jnp.minimum(east_v, 0.0) - east_k
-        coeffs[2, level] = jnp.maximum(north_v, 0.0) + north_k
-        coeffs[3, level] = jnp.minimum(north_v, 0.0) - north_k
-        coeffs[4, level] = wide[base + 4 * levels + level] if level < levels - 1 else jnp.zeros_like(mask)
-        coeffs[5, level] = mask
+        east_k, east_v, north_k, north_v = (outer((4 + n) * levels + level) for n in range(4))
+        mask = (east_k > 0.0).astype(f32)
+        coeffs_out[0, level], coeffs_out[1, level] = upwind(east_k, east_v, eastward(mask))
+        if level < levels - 1:
+            coeffs_out[4, level] = outer(8 * levels + level)
+        coeffs_out[5, level] = mask
+        whole_k = jnp.concatenate([coeffs_in[2, level], north_k], axis=0)
+        whole_v = jnp.concatenate([coeffs_in[3, level], north_v], axis=0)
+        whole_mask = jnp.concatenate([coeffs_in[5, level], mask], axis=0)
+        north[0, level], north[1, level] = upwind(whole_k, whole_v, northward(whole_mask))
+    start, coeffs = whole_rows(start_in, start_out), coefficients(coeffs_in, coeffs_out, north)
+    mask0 = coeffs_in[5, 0, :, :tile_lon]
     copies = []
     for f in range(2):
-        surface = start[(2 + f) * levels, :tile_lat, :tile_lon]
+        surface = start_in[(2 + f) * levels, :, :tile_lon]
         for step in range(STEPS - 1):
 
             def read(level):
-                return states[f, step - 1, level] if step else start[(2 + f) * levels + level]
+                return states[f, step - 1, level] if step else start((2 + f) * levels + level)
 
             def write(level, lam):
                 states[f, step, level] = lam
 
-            adjoint_step(coeffs, read, write, 0, surface_levels(step, levels))
+            adjoint_step(coeffs, levels, read, write, 0, surface_levels(step, levels))
             surface = surface + states[f, step, 0, :tile_lat, :tile_lon]
-        surface = surface * mask0[:tile_lat, :tile_lon]
+        surface = surface * mask0
         for h in range(halves):
             at = (f * halves + h) * tile_lat
             own[at : at + tile_lat] = surface[:, h * BLOCK : (h + 1) * BLOCK]
@@ -268,8 +291,9 @@
         copy.wait()
 
 
-def finish_adjoint(coeffs, start, states, adjoint_out, rest):
-    levels = coeffs.shape[1]
+def finish_adjoint(start_in, coeffs_in, start_out, coeffs_out, north, states, adjoint_out, rest):
+    levels = coeffs_in.shape[1]
+    start, coeffs = whole_rows(start_in, start_out), coefficients(coeffs_in, coeffs_out, north)
     tile_lat, tile_lon = adjoint_out.shape[2:]
     for f in range(2):
         for step in range(STEPS):
@@ -277,7 +301,7 @@
 
             def read(level):
                 if not step:
-                    return start[(2 + f) * levels + level]
+                    return start((2 + f) * levels + level)
                 return (states if level < surface_levels(step - 1, levels) else rest)[f, step - 1, level]
 
             def write(level, lam):
@@ -286,7 +310,7 @@
                 else:
                     rest[f, step, level] = lam
 
-            adjoint_step(coeffs, read, write, done, levels)
+            adjoint_step(coeffs, levels, read, write, done, levels)
 
 
 def sum_forcing(received, forcing, near, far):
@@ -315,22 +339,23 @@
     near[0], far[0] = sort_swap("lat", to_north, to_south)
 
 
-def run_forward(coeffs, start, forcing, near, far, final, state):
-    levels = coeffs.shape[1]
+def run_forward(start_in, coeffs_in, start_out, coeffs_out, north, forcing, near, far, final, state):
+    levels = coeffs_in.shape[1]
+    start, coeffs = whole_rows(start_in, start_out), coefficients(coeffs_in, coeffs_out, north)
     tile_lat, tile_lon = final.shape[2:]
     for f in range(2):
         force = jnp.concatenate([forcing[f], edge_rows(near, far, f)], axis=0)
-        force = force * coeffs[5, 0]
+        force = force * coeffs(5, 0)
         for step in range(STEPS):
             above = None
             for level in range(levels):
-                read = (lambda n: start[f * levels + n]) if step == 0 else (lambda n: state[(step - 1) % 2, n])
+                read = (lambda n: start(f * levels + n)) if step == 0 else (lambda n: state[(step - 1) % 2, n])
                 theta = read(level)
-                east_flux = coeffs[0, level] * theta + coeffs[1, level] * eastward(theta)
-                north_flux = coeffs[2, level] * theta + coeffs[3, level] * northward(theta)
+                east_flux = coeffs(0, level) * theta + coeffs(1, level) * eastward(theta)
+                north_flux = coeffs(2, level) * theta + coeffs(3, level) * northward(theta)
                 out = theta - (east_flux - westward(east_flux)) - (north_flux - southward(north_flux))
                 if level < levels - 1:
-                    vertical = coeffs[4, level] * (theta - read(level + 1))
+                    vertical = coeffs(4, level) * (theta - read(level + 1))
                     out = out - vertical
                 if above is not None:
                     out = out + above
@@ -651,20 +676,29 @@
     near_rows, far_rows = swap(near, far, "lat", False)
 
     wide = (tile_lat + 8, tile_lon + BLOCK)
+    inner, outer = (tile_lat, tile_lon + BLOCK), (8, tile_lon + BLOCK)
+    inner_data = call(
+        prepare_stencil,
+        [(4 * levels, *inner), (6, levels, *inner)],
+        name="prepare_stencil",
+        inputs=3,
+    )(fields, from_west, from_east)
     own = (2 * halves * tile_lat, BLOCK)
     adjoint_states = (2, STEPS - 1, levels, *wide)
-    blocks, coeffs, start, states = call(
+    blocks, *outer_data, states = call(
         run_adjoint,
-        [(lon_count, *own), (6, levels, *wide), (4 * levels, *wide), adjoint_states],
         [
-            pltpu.VMEM((count - 4 * levels, *wide), f32),
-            pltpu.VMEM(own, f32),
-            pltpu.SemaphoreType.DMA((2, lon_count)),
+            (lon_count, *own),
+            (4 * levels, *outer),
+            (6, levels, *outer),
+            (2, levels, *wide),
+            adjoint_states,
         ],
+        [pltpu.VMEM(own, f32), pltpu.SemaphoreType.DMA((2, lon_count))],
         name="run_adjoint",
-        inputs=5,
+        inputs=6,
         far_outs=(0,),
-    )(fields, from_west, from_east, far_rows, near_rows)
+    )(*inner_data, from_west, from_east, far_rows, near_rows)
     gathered = exchange(blocks)
 
     message = (1, 8, tile_lon + BLOCK)
@@ -677,15 +711,15 @@
         [cotangent.shape],
         [pltpu.VMEM(adjoint_states, f32)],
         name="finish_adjoint",
-        inputs=3,
-    )(coeffs, start, states)
+        inputs=6,
+    )(*inner_data, *outer_data, states)
     (final,) = call(
         run_forward,
         [tracers.shape],
         [pltpu.VMEM((2, levels, *wide), f32)],
         name="run_forward",
-        inputs=5,
-    )(coeffs, start, forcing, near_rows, far_rows)
+        inputs=8,
+    )(*inner_data, *outer_data, forcing, near_rows, far_rows)
 
     (gradient,) = call(
         unweigh,

time: 41 us -> 41 us (level)
    pallas_call x8 -> x9, Pallas kernels: 13.4 us -> 13.6 us  [run(): kernel(*(pltpu.with_memory_space_constraint(x, pltpu.HBM) if n in far els...]
where the time goes in v12:
time: 41 us; the launch traced here: 40.6 us
  starting transfers between devices  22.7 us (55%)
  Pallas kernels  13.6 us (33%)
  waiting for transfers between devices  3.56 us (9%)
  between operations  0.73 us (2%)
    pallas_call x9, Pallas kernels, run(): kernel(*(pltpu.with_memory_space_constraint(x, pltpu.HBM) if n in far els...  13.6 us
    ppermute x3, starting transfers between devices, swap(): far = lax.ppermute(far, axis, pairs[1])  12.9 us
    all_to_all x2, starting transfers between devices, exchange(): lax.all_to_all(x, 'lon', split_axis=0, concat_axis=0, tiled=True, axis_in...  7.64 us
    ppermute x3, waiting for transfers between devices, swap(): far = lax.ppermute(far, axis, pairs[1])  2.99 us
    ppermute x3, starting transfers between devices, swap(): return (lax.ppermute(near, axis, pairs[0]), far)  2.18 us
  transfers between devices with their start and end apart: 8, of which 3 were waited for; matrix products, arithmetic and copies ran while one was open for 0% of the time, Pallas kernels for 21%

profile of v12, /device:TPU:1, one launch (start us, length us, event | category | flops | bytes accessed | tf_op | source)
XLA Modules:
  0.0 40.6 jit_solution(11212391131685773159)
XLA Ops:
  0.6 1.4 %pack_columns.1 = (f32[35,16,256]{2,1,0:T(8,128)S(1)}, f32[2,16,128]{2,1,0:T(8,128)S(1)}, f32[2,16,128]{2,1,0:T(8,128)S(1)}, f32[2,1,256,128]{3,2,1,0:T(8,128)S(1)}, s32[3,1,1,8,64]{4,3,2,1,0:T(8,128)S(1)}) custom-call(f32[2,4,16,256]{3,2,1,0:T(8,128)} %refs_0_.1, f32[2,4,16,256]{3,2,1,0:T(8,128)} %refs_1_.1, s32[4,16,256]{2,1,0:T(8,128)} %refs_2_.1, ...), custom_call_target="tpu_custom_call" | custom-call | bytes 1048576 | tf_op jit(solution)/shard_map/pack_columns/pallas_call | solution.py:46
  2.1 2.1 %collective-permute-start = (f32[2,16,128]{2,1,0:T(8,128)S(1)}, f32[2,16,128]{2,1,0:T(8,128)S(1)}, u32[]{:S(2)}, u32[]{:S(2)}) collective-permute-start(f32[2,16,128]{2,1,0:T(8,128)S(1)} %get-tuple-element.30), channel_id=1, source_target_pairs={{0,1},{1,0},{2,3},{3,2},{4,5},{5,4},{6,7},{7,6},{8,9},{9,8},{10,11... | collective-permute-start | bytes 49160 | tf_op jit(solution)/shard_map/ppermute | solution.py:83
  4.2 3.3 %collective-permute-start.1 = (f32[2,16,128]{2,1,0:T(8,128)S(1)}, f32[2,16,128]{2,1,0:T(8,128)S(1)}, u32[]{:S(2)}, u32[]{:S(2)}) collective-permute-start(f32[2,16,128]{2,1,0:T(8,128)S(1)} %get-tuple-element.31.after), channel_id=1, source_target_pairs={{1,2},{2,1},{3,4},{4,3},{5,6},{6,5},{7,0},{0,7},{9,10},{10,9},{11,... | collective-permute-start | bytes 49160 | tf_op jit(solution)/shard_map/ppermute | solution.py:82
  7.5 3.7 %weigh.1 = (f32[8,72,128]{2,1,0:T(8,128)}, f32[8,512]{1,0:T(8,128)S(1)}, f32[32,128]{1,0:T(8,128)S(1)}, f32[2,128,128]{2,1,0:T(8,128)S(1)}, f32[2,8,128]{2,1,0:T(8,128)S(1)}, /*index=5*/s32[32,128]{1,0:T(8,128)S(1)}) custom-call(f32[2,1,256,128]{3,2,1,0:T(8,128)S(1)} %get-tuple-element.32.atm_near, s32[3,1,1,8,64]{4,3,2,1,0:T(8,128)S(1)} %get-tuple-element.33.margins, ...), custom_call_target="tpu_custom_call" | custom-call | flops 4294967296 | bytes 1048576 | tf_op jit(solution)/shard_map/weigh/pallas_call | solution.py:46
  11.2 0.0 collective-permute-done.near_columns
  11.2 0.0 collective-permute-done.1.far_columns
  11.3 3.4 %all-to-all-start = ((f32[8,72,128]{2,1,0:T(8,128)}), f32[8,72,128]{2,1,0:T(8,128)S(1)}, u32[]{:S(2)}, u32[]{:S(2)}) async-start(f32[8,72,128]{2,1,0:T(8,128)} %get-tuple-element.44), calls=%async_computation | async-start | bytes 589824 | tf_op jit(solution)/shard_map/all_to_all | solution.py:73
  14.7 5.4 %collective-permute-start.2 = (f32[37,8,128]{2,1,0:T(8,128)S(1)}, f32[37,8,128]{2,1,0:T(8,128)S(1)}, u32[]{:S(2)}, u32[]{:S(2)}) collective-permute-start(f32[37,8,128]{2,1,0:T(8,128)S(1)} %get-tuple-element.39), channel_id=1, source_target_pairs={{8,16},{16,8},{9,17},{17,9},{10,18},{18,10},{11,19},{19,11},{12,20... | collective-permute-start | bytes 454664 | tf_op jit(solution)/shard_map/ppermute | solution.py:82
  20.1 0.1 collective-permute-start.3
  20.2 0.3 prepare_stencil.1
  20.5 2.7 %collective-permute-done.2.far = f32[37,8,128]{2,1,0:T(8,128)S(1)} collective-permute-done((f32[37,8,128]{2,1,0:T(8,128)S(1)}, f32[37,8,128]{2,1,0:T(8,128)S(1)}, u32[]{:S(2)}, u32[]{:S(2)}) %collective-permute-start.2) | collective-permute-done | bytes 151584 | tf_op jit(solution)/shard_map/ppermute | solution.py:82
  23.2 0.0 collective-permute-done.3.near
  23.2 1.5 %run_adjoint.1 = (f32[8,64,128]{2,1,0:T(8,128)}, f32[16,8,384]{2,1,0:T(8,128)S(1)}, f32[6,4,8,384]{3,2,1,0:T(8,128)S(1)}, f32[2,4,24,384]{3,2,1,0:T(8,128)S(1)}, f32[2,3,4,24,384]{4,3,2,1,0:T(8,128)S(1)}) custom-call(f32[16,16,384]{2,1,0:T(8,128)S(1)} %get-tuple-element.37.start_in, f32[6,4,16,384]{3,2,1,0:T(8,128)S(1)} %get-tuple-element.38.coeffs_in, ...), custom_call_target="tpu_custom_call" | custom-call | bytes 1048576 | tf_op jit(solution)/shard_map/run_adjoint/pallas_call | solution.py:46
  24.7 0.0 all-to-all-done.received
  24.8 4.3 %all-to-all-start.1 = ((f32[8,64,128]{2,1,0:T(8,128)}), f32[8,64,128]{2,1,0:T(8,128)S(1)}, u32[]{:S(2)}, u32[]{:S(2)}) async-start(f32[8,64,128]{2,1,0:T(8,128)} %get-tuple-element.49), calls=%async_computation.1 | async-start | bytes 524288 | tf_op jit(solution)/shard_map/all_to_all | solution.py:73
  29.0 0.1 sum_forcing.1
  29.2 0.0 collective-permute-start.4
  29.2 4.2 %collective-permute-start.5 = (f32[1,8,384]{2,1,0:T(8,128)S(1)}, f32[1,8,384]{2,1,0:T(8,128)S(1)}, u32[]{:S(2)}, u32[]{:S(2)}) collective-permute-start(f32[1,8,384]{2,1,0:T(8,128)S(1)} %get-tuple-element.47), channel_id=1, source_target_pairs={{8,16},{16,8},{9,17},{17,9},{10,18},{18,10},{11,19},{19,11},{12,20... | collective-permute-start | bytes 36872 | tf_op jit(solution)/shard_map/ppermute | solution.py:82
  33.4 1.4 %finish_adjoint.1 = f32[2,4,16,256]{3,2,1,0:T(8,128)} custom-call(f32[16,16,384]{2,1,0:T(8,128)S(1)} %get-tuple-element.37.start_in, f32[6,4,16,384]{3,2,1,0:T(8,128)S(1)} %get-tuple-element.38.coeffs_in, f32[16,8,384]{2,1,0:T(8,128)S(1)} %get-tuple-element.41.start_out, f32[6,4,8,384]{3,2,1,0:T(8,128)S(1)} %get-tuple-element.42.coeffs_out, ...), custom_call_target="tpu_custom_call" | custom-call | bytes 1048576 | tf_op jit(solution)/shard_map/finish_adjoint/pallas_call | solution.py:46
  34.8 0.0 collective-permute-done.4.near
  34.8 0.2 collective-permute-done.5.far
  35.0 1.6 %run_forward.1 = f32[2,4,16,256]{3,2,1,0:T(8,128)} custom-call(f32[16,16,384]{2,1,0:T(8,128)S(1)} %get-tuple-element.37.start_in, f32[6,4,16,384]{3,2,1,0:T(8,128)S(1)} %get-tuple-element.38.coeffs_in, f32[16,8,384]{2,1,0:T(8,128)S(1)} %get-tuple-element.41.start_out, f32[6,4,8,384]{3,2,1,0:T(8,128)S(1)} %get-tuple-element.42.coeffs_out, ...), custom_call_target="tpu_custom_call" | custom-call | bytes 1048576 | tf_op jit(solution)/shard_map/run_forward/pallas_call | solution.py:46
  36.6 0.6 %all-to-all-done.1.gathered = f32[8,64,128]{2,1,0:T(8,128)S(1)} async-done(((f32[8,64,128]{2,1,0:T(8,128)}), f32[8,64,128]{2,1,0:T(8,128)S(1)}, u32[]{:S(2)}, u32[]{:S(2)}) %all-to-all-start.1) | async-done | bytes 262176 | tf_op jit(solution)/shard_map/all_to_all | solution.py:73
  37.2 3.4 %unweigh.1 = f32[2,1,256,128]{3,2,1,0:T(8,128)} custom-call(f32[8,64,128]{2,1,0:T(8,128)S(1)} %all-to-all-done.1.gathered, f32[8,512]{1,0:T(8,128)S(1)} %get-tuple-element.50.keys, f32[32,128]{1,0:T(8,128)S(1)} %get-tuple-element.51.counts, f32[2,128,128]{2,1,0:T(8,128)S(1)} %get-tuple-element.52.columns_in, f32[2,8,128]{2,1,0:T(8,128)S(1)} %get-tuple-element.53.lines_in, ...), custom_call_target="tpu_custom_call" | custom-call | flops 4294967296 | bytes 1048576 | tf_op jit(solution)/shard_map/unweigh/pallas_call | solution.py:46
  (1 shorter events, 0.0 us)
Async XLA Ops:
  2.1 9.1 %collective-permute-start = (f32[2,16,128]{2,1,0:T(8,128)S(1)}, f32[2,16,128]{2,1,0:T(8,128)S(1)}, u32[]{:S(2)}, u32[]{:S(2)}) collective-permute-start(f32[2,16,128]{2,1,0:T(8,128)S(1)} %get-tuple-element.30), channel_id=1, source_target_pairs={{0,1},{1,0},{2,3},{3,2},{4,5},{5,4},{6,7},{7,6},{8,9},{9,8},{10,11... | collective-permute-start | bytes 49160 | tf_op jit(solution)/shard_map/ppermute | solution.py:83
  4.2 7.0 %collective-permute-start.1 = (f32[2,16,128]{2,1,0:T(8,128)S(1)}, f32[2,16,128]{2,1,0:T(8,128)S(1)}, u32[]{:S(2)}, u32[]{:S(2)}) collective-permute-start(f32[2,16,128]{2,1,0:T(8,128)S(1)} %get-tuple-element.31.after), channel_id=1, source_target_pairs={{1,2},{2,1},{3,4},{4,3},{5,6},{6,5},{7,0},{0,7},{9,10},{10,9},{11,... | collective-permute-start | bytes 49160 | tf_op jit(solution)/shard_map/ppermute | solution.py:82
  11.3 13.5 %all-to-all-start = ((f32[8,72,128]{2,1,0:T(8,128)}), f32[8,72,128]{2,1,0:T(8,128)S(1)}, u32[]{:S(2)}, u32[]{:S(2)}) async-start(f32[8,72,128]{2,1,0:T(8,128)} %get-tuple-element.44), calls=%async_computation | async-start | bytes 589824 | tf_op jit(solution)/shard_map/all_to_all | solution.py:73
  14.7 8.6 %collective-permute-start.2 = (f32[37,8,128]{2,1,0:T(8,128)S(1)}, f32[37,8,128]{2,1,0:T(8,128)S(1)}, u32[]{:S(2)}, u32[]{:S(2)}) collective-permute-start(f32[37,8,128]{2,1,0:T(8,128)S(1)} %get-tuple-element.39), channel_id=1, source_target_pairs={{8,16},{16,8},{9,17},{17,9},{10,18},{18,10},{11,19},{19,11},{12,20... | collective-permute-start | bytes 454664 | tf_op jit(solution)/shard_map/ppermute | solution.py:82
  20.1 3.2 %collective-permute-start.3 = (f32[37,8,128]{2,1,0:T(8,128)S(1)}, f32[37,8,128]{2,1,0:T(8,128)S(1)}, u32[]{:S(2)}, u32[]{:S(2)}) collective-permute-start(f32[37,8,128]{2,1,0:T(8,128)S(1)} %get-tuple-element.40), channel_id=1, source_target_pairs={{0,8},{8,0},{16,24},{24,16},{1,9},{9,1},{17,25},{25,17},{2,10},{10... | collective-permute-start | bytes 454664 | tf_op jit(solution)/shard_map/ppermute | solution.py:83
  24.8 12.4 %all-to-all-start.1 = ((f32[8,64,128]{2,1,0:T(8,128)}), f32[8,64,128]{2,1,0:T(8,128)S(1)}, u32[]{:S(2)}, u32[]{:S(2)}) async-start(f32[8,64,128]{2,1,0:T(8,128)} %get-tuple-element.49), calls=%async_computation.1 | async-start | bytes 524288 | tf_op jit(solution)/shard_map/all_to_all | solution.py:73
  29.2 5.6 %collective-permute-start.4 = (f32[1,8,384]{2,1,0:T(8,128)S(1)}, f32[1,8,384]{2,1,0:T(8,128)S(1)}, u32[]{:S(2)}, u32[]{:S(2)}) collective-permute-start(f32[1,8,384]{2,1,0:T(8,128)S(1)} %get-tuple-element.46), channel_id=1, source_target_pairs={{0,8},{8,0},{16,24},{24,16},{1,9},{9,1},{17,25},{25,17},{2,10},{10... | collective-permute-start | bytes 36872 | tf_op jit(solution)/shard_map/ppermute | solution.py:83
  29.2 5.9 %collective-permute-start.5 = (f32[1,8,384]{2,1,0:T(8,128)S(1)}, f32[1,8,384]{2,1,0:T(8,128)S(1)}, u32[]{:S(2)}, u32[]{:S(2)}) collective-permute-start(f32[1,8,384]{2,1,0:T(8,128)S(1)} %get-tuple-element.47), channel_id=1, source_target_pairs={{8,16},{16,8},{9,17},{17,9},{10,18},{18,10},{11,19},{19,11},{12,20... | collective-permute-start | bytes 36872 | tf_op jit(solution)/shard_map/ppermute | solution.py:82

commit v13 on v11

--- a/solution.py
+++ b/solution.py
@@ -9,7 +9,7 @@
 STEPS = 4
 HALO = STEPS
 PER_LANES = BLOCK // HALO
-GROUP = 16
+GROUP = 32
 FETCH = 4
 f32 = jnp.float32
 bf16 = jnp.bfloat16
@@ -64,8 +64,8 @@
 
 
 def group_order(count):
-    half, quarter = count // 2, count // 4
-    return [k for n in range(half) for k in ((n + quarter) % half, half + (n + quarter) % half)]
+    half = count // 2
+    return [k for n in range(half) for k in (half + n, n)]
 
 
 def exchange(x):

time: 41 us -> 40.7 us (level)
  waiting for transfers between devices: 3.79 us -> 3.03 us
    all_to_all x2, starting transfers between devices: 7.64 us -> 8.33 us  [exchange(): lax.all_to_all(x, 'lon', split_axis=0, concat_axis=0, tiled=True, axis_in...]
    ppermute x3, starting transfers between devices: 12.9 us -> 12.4 us  [swap(): far = lax.ppermute(far, axis, pairs[1])]
    all_to_all x2, waiting for transfers between devices: 0.47 us -> 0.01 us  [exchange(): lax.all_to_all(x, 'lon', split_axis=0, concat_axis=0, tiled=True, axis_in...]
  transfers between devices with their start and end apart: 8 -> 8, of which waited for: 3 -> 2; matrix products, arithmetic and copies ran while one was open for 0% -> 0% of each run, Pallas kernels for 21% -> 21%
where the time goes in v13:
time: 40.7 us; the launch traced here: 40.3 us
  starting transfers between devices  22.9 us (56%)
  Pallas kernels  13.6 us (33%)
  waiting for transfers between devices  3.03 us (7%)
  between operations  0.72 us (2%)
    pallas_call x8, Pallas kernels, run(): kernel(*(pltpu.with_memory_space_constraint(x, pltpu.HBM) if n in far els...  13.6 us
    ppermute x3, starting transfers between devices, swap(): far = lax.ppermute(far, axis, pairs[1])  12.4 us
    all_to_all x2, starting transfers between devices, exchange(): lax.all_to_all(x, 'lon', split_axis=0, concat_axis=0, tiled=True, axis_in...  8.33 us
    ppermute x3, waiting for transfers between devices, swap(): far = lax.ppermute(far, axis, pairs[1])  3.02 us
    ppermute x3, starting transfers between devices, swap(): return (lax.ppermute(near, axis, pairs[0]), far)  2.18 us
  transfers between devices with their start and end apart: 8, of which 2 were waited for; matrix products, arithmetic and copies ran while one was open for 0% of the time, Pallas kernels for 21%

profile of v13, /device:TPU:1, one launch (start us, length us, event | category | flops | bytes accessed | tf_op | source)
XLA Modules:
  0.0 40.3 jit_solution(6634333080644883416)
XLA Ops:
  0.6 1.4 %pack_columns.1 = (f32[35,16,256]{2,1,0:T(8,128)S(1)}, f32[2,16,128]{2,1,0:T(8,128)S(1)}, f32[2,16,128]{2,1,0:T(8,128)S(1)}, f32[2,1,256,128]{3,2,1,0:T(8,128)S(1)}, s32[3,1,1,8,64]{4,3,2,1,0:T(8,128)S(1)}) custom-call(f32[2,4,16,256]{3,2,1,0:T(8,128)} %refs_0_.1, f32[2,4,16,256]{3,2,1,0:T(8,128)} %refs_1_.1, s32[4,16,256]{2,1,0:T(8,128)} %refs_2_.1, ...), custom_call_target="tpu_custom_call" | custom-call | bytes 1048576 | tf_op jit(solution)/shard_map/pack_columns/pallas_call | solution.py:46
  2.1 2.1 %collective-permute-start = (f32[2,16,128]{2,1,0:T(8,128)S(1)}, f32[2,16,128]{2,1,0:T(8,128)S(1)}, u32[]{:S(2)}, u32[]{:S(2)}) collective-permute-start(f32[2,16,128]{2,1,0:T(8,128)S(1)} %get-tuple-element.27), channel_id=1, source_target_pairs={{0,1},{1,0},{2,3},{3,2},{4,5},{5,4},{6,7},{7,6},{8,9},{9,8},{10,11... | collective-permute-start | bytes 49160 | tf_op jit(solution)/shard_map/ppermute | solution.py:83
  4.2 3.3 %collective-permute-start.1 = (f32[2,16,128]{2,1,0:T(8,128)S(1)}, f32[2,16,128]{2,1,0:T(8,128)S(1)}, u32[]{:S(2)}, u32[]{:S(2)}) collective-permute-start(f32[2,16,128]{2,1,0:T(8,128)S(1)} %get-tuple-element.28.after), channel_id=1, source_target_pairs={{1,2},{2,1},{3,4},{4,3},{5,6},{6,5},{7,0},{0,7},{9,10},{10,9},{11,... | collective-permute-start | bytes 49160 | tf_op jit(solution)/shard_map/ppermute | solution.py:82
  7.5 3.8 %weigh.1 = (f32[8,72,128]{2,1,0:T(8,128)}, f32[8,512]{1,0:T(8,128)S(1)}, f32[32,128]{1,0:T(8,128)S(1)}, f32[2,128,128]{2,1,0:T(8,128)S(1)}, f32[2,8,128]{2,1,0:T(8,128)S(1)}, /*index=5*/s32[32,128]{1,0:T(8,128)S(1)}) custom-call(f32[2,1,256,128]{3,2,1,0:T(8,128)S(1)} %get-tuple-element.29.atm_near, s32[3,1,1,8,64]{4,3,2,1,0:T(8,128)S(1)} %get-tuple-element.30.margins, ...), custom_call_target="tpu_custom_call" | custom-call | flops 4294967296 | bytes 1048576 | tf_op jit(solution)/shard_map/weigh/pallas_call | solution.py:46
  11.3 0.0 collective-permute-done.near_columns
  11.3 0.0 collective-permute-done.1.far_columns
  11.4 3.6 %all-to-all-start = ((f32[8,72,128]{2,1,0:T(8,128)}), f32[8,72,128]{2,1,0:T(8,128)S(1)}, u32[]{:S(2)}, u32[]{:S(2)}) async-start(f32[8,72,128]{2,1,0:T(8,128)} %get-tuple-element.38), calls=%async_computation | async-start | bytes 589824 | tf_op jit(solution)/shard_map/all_to_all | solution.py:73
  15.0 5.1 %collective-permute-start.2 = (f32[37,8,128]{2,1,0:T(8,128)S(1)}, f32[37,8,128]{2,1,0:T(8,128)S(1)}, u32[]{:S(2)}, u32[]{:S(2)}) collective-permute-start(f32[37,8,128]{2,1,0:T(8,128)S(1)} %get-tuple-element.34), channel_id=1, source_target_pairs={{8,16},{16,8},{9,17},{17,9},{10,18},{18,10},{11,19},{19,11},{12,20... | collective-permute-start | bytes 454664 | tf_op jit(solution)/shard_map/ppermute | solution.py:82
  20.1 0.1 collective-permute-start.3
  20.2 2.8 %collective-permute-done.2.far = f32[37,8,128]{2,1,0:T(8,128)S(1)} collective-permute-done((f32[37,8,128]{2,1,0:T(8,128)S(1)}, f32[37,8,128]{2,1,0:T(8,128)S(1)}, u32[]{:S(2)}, u32[]{:S(2)}) %collective-permute-start.2) | collective-permute-done | bytes 151584 | tf_op jit(solution)/shard_map/ppermute | solution.py:82
  22.9 0.0 collective-permute-done.3.near
  22.9 1.6 %run_adjoint.1 = (f32[8,64,128]{2,1,0:T(8,128)}, f32[6,4,24,384]{3,2,1,0:T(8,128)S(1)}, f32[16,24,384]{2,1,0:T(8,128)S(1)}, f32[2,3,4,24,384]{4,3,2,1,0:T(8,128)S(1)}) custom-call(f32[35,16,256]{2,1,0:T(8,128)S(1)} %get-tuple-element.26.fields, f32[2,16,128]{2,1,0:T(8,128)S(1)} %get-tuple-element.32.from_west, ...), custom_call_target="tpu_custom_call" | custom-call | bytes 1048576 | tf_op jit(solution)/shard_map/run_adjoint/pallas_call | solution.py:46
  24.6 0.0 all-to-all-done.received
  24.6 4.7 %all-to-all-start.1 = ((f32[8,64,128]{2,1,0:T(8,128)}), f32[8,64,128]{2,1,0:T(8,128)S(1)}, u32[]{:S(2)}, u32[]{:S(2)}) async-start(f32[8,64,128]{2,1,0:T(8,128)} %get-tuple-element.43), calls=%async_computation.1 | async-start | bytes 524288 | tf_op jit(solution)/shard_map/all_to_all | solution.py:73
  29.3 0.1 sum_forcing.1
  29.4 0.0 collective-permute-start.4
  29.4 4.1 %collective-permute-start.5 = (f32[1,8,384]{2,1,0:T(8,128)S(1)}, f32[1,8,384]{2,1,0:T(8,128)S(1)}, u32[]{:S(2)}, u32[]{:S(2)}) collective-permute-start(f32[1,8,384]{2,1,0:T(8,128)S(1)} %get-tuple-element.41), channel_id=1, source_target_pairs={{8,16},{16,8},{9,17},{17,9},{10,18},{18,10},{11,19},{19,11},{12,20... | collective-permute-start | bytes 36872 | tf_op jit(solution)/shard_map/ppermute | solution.py:82
  33.5 1.4 %finish_adjoint.1 = f32[2,4,16,256]{3,2,1,0:T(8,128)} custom-call(f32[6,4,24,384]{3,2,1,0:T(8,128)S(1)} %get-tuple-element.36.coeffs, f32[16,24,384]{2,1,0:T(8,128)S(1)} %get-tuple-element.37.start, f32[2,3,4,24,384]{4,3,2,1,0:T(8,128)S(1)} %get-tuple-element.42.states), custom_call_target="tpu_custom_call" | custom-call | bytes 1048576 | tf_op jit(solution)/shard_map/finish_adjoint/pallas_call | solution.py:46
  34.9 0.0 collective-permute-done.4.near
  34.9 0.2 collective-permute-done.5.far
  35.1 1.6 %run_forward.1 = f32[2,4,16,256]{3,2,1,0:T(8,128)} custom-call(f32[6,4,24,384]{3,2,1,0:T(8,128)S(1)} %get-tuple-element.36.coeffs, f32[16,24,384]{2,1,0:T(8,128)S(1)} %get-tuple-element.37.start, f32[2,16,384]{2,1,0:T(8,128)S(1)} %get-tuple-element.39.forcing, f32[1,8,384]{2,1,0:T(8,128)S(1)} %collective-permute-done.4.near, ...), custom_call_target="tpu_custom_call" | custom-call | bytes 1048576 | tf_op jit(solution)/shard_map/run_forward/pallas_call | solution.py:46
  36.7 0.0 all-to-all-done.1.gathered
  36.7 3.6 %unweigh.1 = f32[2,1,256,128]{3,2,1,0:T(8,128)} custom-call(f32[8,64,128]{2,1,0:T(8,128)S(1)} %all-to-all-done.1.gathered, f32[8,512]{1,0:T(8,128)S(1)} %get-tuple-element.44.keys, f32[32,128]{1,0:T(8,128)S(1)} %get-tuple-element.45.counts, f32[2,128,128]{2,1,0:T(8,128)S(1)} %get-tuple-element.46.columns_in, f32[2,8,128]{2,1,0:T(8,128)S(1)} %get-tuple-element.47.lines_in, ...), custom_call_target="tpu_custom_call" | custom-call | flops 4294967296 | bytes 1048576 | tf_op jit(solution)/shard_map/unweigh/pallas_call | solution.py:46
  (1 shorter events, 0.0 us)
Async XLA Ops:
  2.1 9.2 %collective-permute-start = (f32[2,16,128]{2,1,0:T(8,128)S(1)}, f32[2,16,128]{2,1,0:T(8,128)S(1)}, u32[]{:S(2)}, u32[]{:S(2)}) collective-permute-start(f32[2,16,128]{2,1,0:T(8,128)S(1)} %get-tuple-element.27), channel_id=1, source_target_pairs={{0,1},{1,0},{2,3},{3,2},{4,5},{5,4},{6,7},{7,6},{8,9},{9,8},{10,11... | collective-permute-start | bytes 49160 | tf_op jit(solution)/shard_map/ppermute | solution.py:83
  4.2 7.1 %collective-permute-start.1 = (f32[2,16,128]{2,1,0:T(8,128)S(1)}, f32[2,16,128]{2,1,0:T(8,128)S(1)}, u32[]{:S(2)}, u32[]{:S(2)}) collective-permute-start(f32[2,16,128]{2,1,0:T(8,128)S(1)} %get-tuple-element.28.after), channel_id=1, source_target_pairs={{1,2},{2,1},{3,4},{4,3},{5,6},{6,5},{7,0},{0,7},{9,10},{10,9},{11,... | collective-permute-start | bytes 49160 | tf_op jit(solution)/shard_map/ppermute | solution.py:82
  11.4 13.2 %all-to-all-start = ((f32[8,72,128]{2,1,0:T(8,128)}), f32[8,72,128]{2,1,0:T(8,128)S(1)}, u32[]{:S(2)}, u32[]{:S(2)}) async-start(f32[8,72,128]{2,1,0:T(8,128)} %get-tuple-element.38), calls=%async_computation | async-start | bytes 589824 | tf_op jit(solution)/shard_map/all_to_all | solution.py:73
  15.0 7.9 %collective-permute-start.2 = (f32[37,8,128]{2,1,0:T(8,128)S(1)}, f32[37,8,128]{2,1,0:T(8,128)S(1)}, u32[]{:S(2)}, u32[]{:S(2)}) collective-permute-start(f32[37,8,128]{2,1,0:T(8,128)S(1)} %get-tuple-element.34), channel_id=1, source_target_pairs={{8,16},{16,8},{9,17},{17,9},{10,18},{18,10},{11,19},{19,11},{12,20... | collective-permute-start | bytes 454664 | tf_op jit(solution)/shard_map/ppermute | solution.py:82
  20.1 2.9 %collective-permute-start.3 = (f32[37,8,128]{2,1,0:T(8,128)S(1)}, f32[37,8,128]{2,1,0:T(8,128)S(1)}, u32[]{:S(2)}, u32[]{:S(2)}) collective-permute-start(f32[37,8,128]{2,1,0:T(8,128)S(1)} %get-tuple-element.35), channel_id=1, source_target_pairs={{0,8},{8,0},{16,24},{24,16},{1,9},{9,1},{17,25},{25,17},{2,10},{10... | collective-permute-start | bytes 454664 | tf_op jit(solution)/shard_map/ppermute | solution.py:83
  24.6 12.1 %all-to-all-start.1 = ((f32[8,64,128]{2,1,0:T(8,128)}), f32[8,64,128]{2,1,0:T(8,128)S(1)}, u32[]{:S(2)}, u32[]{:S(2)}) async-start(f32[8,64,128]{2,1,0:T(8,128)} %get-tuple-element.43), calls=%async_computation.1 | async-start | bytes 524288 | tf_op jit(solution)/shard_map/all_to_all | solution.py:73
  29.4 5.5 %collective-permute-start.4 = (f32[1,8,384]{2,1,0:T(8,128)S(1)}, f32[1,8,384]{2,1,0:T(8,128)S(1)}, u32[]{:S(2)}, u32[]{:S(2)}) collective-permute-start(f32[1,8,384]{2,1,0:T(8,128)S(1)} %get-tuple-element.40), channel_id=1, source_target_pairs={{0,8},{8,0},{16,24},{24,16},{1,9},{9,1},{17,25},{25,17},{2,10},{10... | collective-permute-start | bytes 36872 | tf_op jit(solution)/shard_map/ppermute | solution.py:83
  29.4 5.7 %collective-permute-start.5 = (f32[1,8,384]{2,1,0:T(8,128)S(1)}, f32[1,8,384]{2,1,0:T(8,128)S(1)}, u32[]{:S(2)}, u32[]{:S(2)}) collective-permute-start(f32[1,8,384]{2,1,0:T(8,128)S(1)} %get-tuple-element.41), channel_id=1, source_target_pairs={{8,16},{16,8},{9,17},{17,9},{10,18},{18,10},{11,19},{19,11},{12,20... | collective-permute-start | bytes 36872 | tf_op jit(solution)/shard_map/ppermute | solution.py:82

commit v14 on v13

--- a/solution.py
+++ b/solution.py
@@ -9,7 +9,7 @@
 STEPS = 4
 HALO = STEPS
 PER_LANES = BLOCK // HALO
-GROUP = 32
+GROUP = 16
 FETCH = 4
 f32 = jnp.float32
 bf16 = jnp.bfloat16

time: 40.7 us -> 40.5 us (level)
  no operation moved by 1% of the time
where the time goes in v14:
time: 40.5 us; the launch traced here: 40.1 us
  starting transfers between devices  23 us (57%)
  Pallas kernels  13.4 us (33%)
  waiting for transfers between devices  3.03 us (7%)
  between operations  0.72 us (2%)
    pallas_call x8, Pallas kernels, run(): kernel(*(pltpu.with_memory_space_constraint(x, pltpu.HBM) if n in far els...  13.4 us
    ppermute x3, starting transfers between devices, swap(): far = lax.ppermute(far, axis, pairs[1])  12.6 us
    all_to_all x2, starting transfers between devices, exchange(): lax.all_to_all(x, 'lon', split_axis=0, concat_axis=0, tiled=True, axis_in...  8.24 us
    ppermute x3, waiting for transfers between devices, swap(): far = lax.ppermute(far, axis, pairs[1])  3.02 us
    ppermute x3, starting transfers between devices, swap(): return (lax.ppermute(near, axis, pairs[0]), far)  2.18 us
  transfers between devices with their start and end apart: 8, of which 2 were waited for; matrix products, arithmetic and copies ran while one was open for 0% of the time, Pallas kernels for 21%

profile of v14, /device:TPU:1, one launch (start us, length us, event | category | flops | bytes accessed | tf_op | source)
XLA Modules:
  0.0 40.1 jit_solution(18020217960326173419)
XLA Ops:
  0.6 1.4 %pack_columns.1 = (f32[35,16,256]{2,1,0:T(8,128)S(1)}, f32[2,16,128]{2,1,0:T(8,128)S(1)}, f32[2,16,128]{2,1,0:T(8,128)S(1)}, f32[2,1,256,128]{3,2,1,0:T(8,128)S(1)}, s32[3,1,1,8,64]{4,3,2,1,0:T(8,128)S(1)}) custom-call(f32[2,4,16,256]{3,2,1,0:T(8,128)} %refs_0_.1, f32[2,4,16,256]{3,2,1,0:T(8,128)} %refs_1_.1, s32[4,16,256]{2,1,0:T(8,128)} %refs_2_.1, ...), custom_call_target="tpu_custom_call" | custom-call | bytes 1048576 | tf_op jit(solution)/shard_map/pack_columns/pallas_call | solution.py:46
  2.1 2.1 %collective-permute-start = (f32[2,16,128]{2,1,0:T(8,128)S(1)}, f32[2,16,128]{2,1,0:T(8,128)S(1)}, u32[]{:S(2)}, u32[]{:S(2)}) collective-permute-start(f32[2,16,128]{2,1,0:T(8,128)S(1)} %get-tuple-element.27), channel_id=1, source_target_pairs={{0,1},{1,0},{2,3},{3,2},{4,5},{5,4},{6,7},{7,6},{8,9},{9,8},{10,11... | collective-permute-start | bytes 49160 | tf_op jit(solution)/shard_map/ppermute | solution.py:83
  4.2 3.3 %collective-permute-start.1 = (f32[2,16,128]{2,1,0:T(8,128)S(1)}, f32[2,16,128]{2,1,0:T(8,128)S(1)}, u32[]{:S(2)}, u32[]{:S(2)}) collective-permute-start(f32[2,16,128]{2,1,0:T(8,128)S(1)} %get-tuple-element.28.after), channel_id=1, source_target_pairs={{1,2},{2,1},{3,4},{4,3},{5,6},{6,5},{7,0},{0,7},{9,10},{10,9},{11,... | collective-permute-start | bytes 49160 | tf_op jit(solution)/shard_map/ppermute | solution.py:82
  7.5 3.7 %weigh.1 = (f32[8,72,128]{2,1,0:T(8,128)}, f32[8,512]{1,0:T(8,128)S(1)}, f32[32,128]{1,0:T(8,128)S(1)}, f32[2,128,128]{2,1,0:T(8,128)S(1)}, f32[2,8,128]{2,1,0:T(8,128)S(1)}, /*index=5*/s32[32,128]{1,0:T(8,128)S(1)}) custom-call(f32[2,1,256,128]{3,2,1,0:T(8,128)S(1)} %get-tuple-element.29.atm_near, s32[3,1,1,8,64]{4,3,2,1,0:T(8,128)S(1)} %get-tuple-element.30.margins, ...), custom_call_target="tpu_custom_call" | custom-call | flops 4294967296 | bytes 1048576 | tf_op jit(solution)/shard_map/weigh/pallas_call | solution.py:46
  11.2 0.0 collective-permute-done.near_columns
  11.2 0.0 collective-permute-done.1.far_columns
  11.3 3.6 %all-to-all-start = ((f32[8,72,128]{2,1,0:T(8,128)}), f32[8,72,128]{2,1,0:T(8,128)S(1)}, u32[]{:S(2)}, u32[]{:S(2)}) async-start(f32[8,72,128]{2,1,0:T(8,128)} %get-tuple-element.38), calls=%async_computation | async-start | bytes 589824 | tf_op jit(solution)/shard_map/all_to_all | solution.py:73
  14.9 5.1 %collective-permute-start.2 = (f32[37,8,128]{2,1,0:T(8,128)S(1)}, f32[37,8,128]{2,1,0:T(8,128)S(1)}, u32[]{:S(2)}, u32[]{:S(2)}) collective-permute-start(f32[37,8,128]{2,1,0:T(8,128)S(1)} %get-tuple-element.34), channel_id=1, source_target_pairs={{8,16},{16,8},{9,17},{17,9},{10,18},{18,10},{11,19},{19,11},{12,20... | collective-permute-start | bytes 454664 | tf_op jit(solution)/shard_map/ppermute | solution.py:82
  20.1 0.1 collective-permute-start.3
  20.2 2.8 %collective-permute-done.2.far = f32[37,8,128]{2,1,0:T(8,128)S(1)} collective-permute-done((f32[37,8,128]{2,1,0:T(8,128)S(1)}, f32[37,8,128]{2,1,0:T(8,128)S(1)}, u32[]{:S(2)}, u32[]{:S(2)}) %collective-permute-start.2) | collective-permute-done | bytes 151584 | tf_op jit(solution)/shard_map/ppermute | solution.py:82
  22.9 0.0 collective-permute-done.3.near
  22.9 1.6 %run_adjoint.1 = (f32[8,64,128]{2,1,0:T(8,128)}, f32[6,4,24,384]{3,2,1,0:T(8,128)S(1)}, f32[16,24,384]{2,1,0:T(8,128)S(1)}, f32[2,3,4,24,384]{4,3,2,1,0:T(8,128)S(1)}) custom-call(f32[35,16,256]{2,1,0:T(8,128)S(1)} %get-tuple-element.26.fields, f32[2,16,128]{2,1,0:T(8,128)S(1)} %get-tuple-element.32.from_west, ...), custom_call_target="tpu_custom_call" | custom-call | bytes 1048576 | tf_op jit(solution)/shard_map/run_adjoint/pallas_call | solution.py:46
  24.6 0.0 all-to-all-done.received
  24.6 4.6 %all-to-all-start.1 = ((f32[8,64,128]{2,1,0:T(8,128)}), f32[8,64,128]{2,1,0:T(8,128)S(1)}, u32[]{:S(2)}, u32[]{:S(2)}) async-start(f32[8,64,128]{2,1,0:T(8,128)} %get-tuple-element.43), calls=%async_computation.1 | async-start | bytes 524288 | tf_op jit(solution)/shard_map/all_to_all | solution.py:73
  29.2 0.1 sum_forcing.1
  29.3 0.0 collective-permute-start.4
  29.3 4.2 %collective-permute-start.5 = (f32[1,8,384]{2,1,0:T(8,128)S(1)}, f32[1,8,384]{2,1,0:T(8,128)S(1)}, u32[]{:S(2)}, u32[]{:S(2)}) collective-permute-start(f32[1,8,384]{2,1,0:T(8,128)S(1)} %get-tuple-element.41), channel_id=1, source_target_pairs={{8,16},{16,8},{9,17},{17,9},{10,18},{18,10},{11,19},{19,11},{12,20... | collective-permute-start | bytes 36872 | tf_op jit(solution)/shard_map/ppermute | solution.py:82
  33.5 1.4 %finish_adjoint.1 = f32[2,4,16,256]{3,2,1,0:T(8,128)} custom-call(f32[6,4,24,384]{3,2,1,0:T(8,128)S(1)} %get-tuple-element.36.coeffs, f32[16,24,384]{2,1,0:T(8,128)S(1)} %get-tuple-element.37.start, f32[2,3,4,24,384]{4,3,2,1,0:T(8,128)S(1)} %get-tuple-element.42.states), custom_call_target="tpu_custom_call" | custom-call | bytes 1048576 | tf_op jit(solution)/shard_map/finish_adjoint/pallas_call | solution.py:46
  34.9 0.0 collective-permute-done.4.near
  34.9 0.2 collective-permute-done.5.far
  35.1 1.6 %run_forward.1 = f32[2,4,16,256]{3,2,1,0:T(8,128)} custom-call(f32[6,4,24,384]{3,2,1,0:T(8,128)S(1)} %get-tuple-element.36.coeffs, f32[16,24,384]{2,1,0:T(8,128)S(1)} %get-tuple-element.37.start, f32[2,16,384]{2,1,0:T(8,128)S(1)} %get-tuple-element.39.forcing, f32[1,8,384]{2,1,0:T(8,128)S(1)} %collective-permute-done.4.near, ...), custom_call_target="tpu_custom_call" | custom-call | bytes 1048576 | tf_op jit(solution)/shard_map/run_forward/pallas_call | solution.py:46
  36.7 0.0 all-to-all-done.1.gathered
  36.7 3.4 %unweigh.1 = f32[2,1,256,128]{3,2,1,0:T(8,128)} custom-call(f32[8,64,128]{2,1,0:T(8,128)S(1)} %all-to-all-done.1.gathered, f32[8,512]{1,0:T(8,128)S(1)} %get-tuple-element.44.keys, f32[32,128]{1,0:T(8,128)S(1)} %get-tuple-element.45.counts, f32[2,128,128]{2,1,0:T(8,128)S(1)} %get-tuple-element.46.columns_in, f32[2,8,128]{2,1,0:T(8,128)S(1)} %get-tuple-element.47.lines_in, ...), custom_call_target="tpu_custom_call" | custom-call | flops 4294967296 | bytes 1048576 | tf_op jit(solution)/shard_map/unweigh/pallas_call | solution.py:46
  (1 shorter events, 0.0 us)
Async XLA Ops:
  2.1 9.1 %collective-permute-start = (f32[2,16,128]{2,1,0:T(8,128)S(1)}, f32[2,16,128]{2,1,0:T(8,128)S(1)}, u32[]{:S(2)}, u32[]{:S(2)}) collective-permute-start(f32[2,16,128]{2,1,0:T(8,128)S(1)} %get-tuple-element.27), channel_id=1, source_target_pairs={{0,1},{1,0},{2,3},{3,2},{4,5},{5,4},{6,7},{7,6},{8,9},{9,8},{10,11... | collective-permute-start | bytes 49160 | tf_op jit(solution)/shard_map/ppermute | solution.py:83
  4.2 7.0 %collective-permute-start.1 = (f32[2,16,128]{2,1,0:T(8,128)S(1)}, f32[2,16,128]{2,1,0:T(8,128)S(1)}, u32[]{:S(2)}, u32[]{:S(2)}) collective-permute-start(f32[2,16,128]{2,1,0:T(8,128)S(1)} %get-tuple-element.28.after), channel_id=1, source_target_pairs={{1,2},{2,1},{3,4},{4,3},{5,6},{6,5},{7,0},{0,7},{9,10},{10,9},{11,... | collective-permute-start | bytes 49160 | tf_op jit(solution)/shard_map/ppermute | solution.py:82
  11.3 13.3 %all-to-all-start = ((f32[8,72,128]{2,1,0:T(8,128)}), f32[8,72,128]{2,1,0:T(8,128)S(1)}, u32[]{:S(2)}, u32[]{:S(2)}) async-start(f32[8,72,128]{2,1,0:T(8,128)} %get-tuple-element.38), calls=%async_computation | async-start | bytes 589824 | tf_op jit(solution)/shard_map/all_to_all | solution.py:73
  14.9 8.0 %collective-permute-start.2 = (f32[37,8,128]{2,1,0:T(8,128)S(1)}, f32[37,8,128]{2,1,0:T(8,128)S(1)}, u32[]{:S(2)}, u32[]{:S(2)}) collective-permute-start(f32[37,8,128]{2,1,0:T(8,128)S(1)} %get-tuple-element.34), channel_id=1, source_target_pairs={{8,16},{16,8},{9,17},{17,9},{10,18},{18,10},{11,19},{19,11},{12,20... | collective-permute-start | bytes 454664 | tf_op jit(solution)/shard_map/ppermute | solution.py:82
  20.1 2.9 %collective-permute-start.3 = (f32[37,8,128]{2,1,0:T(8,128)S(1)}, f32[37,8,128]{2,1,0:T(8,128)S(1)}, u32[]{:S(2)}, u32[]{:S(2)}) collective-permute-start(f32[37,8,128]{2,1,0:T(8,128)S(1)} %get-tuple-element.35), channel_id=1, source_target_pairs={{0,8},{8,0},{16,24},{24,16},{1,9},{9,1},{17,25},{25,17},{2,10},{10... | collective-permute-start | bytes 454664 | tf_op jit(solution)/shard_map/ppermute | solution.py:83
  24.6 12.1 %all-to-all-start.1 = ((f32[8,64,128]{2,1,0:T(8,128)}), f32[8,64,128]{2,1,0:T(8,128)S(1)}, u32[]{:S(2)}, u32[]{:S(2)}) async-start(f32[8,64,128]{2,1,0:T(8,128)} %get-tuple-element.43), calls=%async_computation.1 | async-start | bytes 524288 | tf_op jit(solution)/shard_map/all_to_all | solution.py:73
  29.3 5.6 %collective-permute-start.4 = (f32[1,8,384]{2,1,0:T(8,128)S(1)}, f32[1,8,384]{2,1,0:T(8,128)S(1)}, u32[]{:S(2)}, u32[]{:S(2)}) collective-permute-start(f32[1,8,384]{2,1,0:T(8,128)S(1)} %get-tuple-element.40), channel_id=1, source_target_pairs={{0,8},{8,0},{16,24},{24,16},{1,9},{9,1},{17,25},{25,17},{2,10},{10... | collective-permute-start | bytes 36872 | tf_op jit(solution)/shard_map/ppermute | solution.py:83
  29.3 5.8 %collective-permute-start.5 = (f32[1,8,384]{2,1,0:T(8,128)S(1)}, f32[1,8,384]{2,1,0:T(8,128)S(1)}, u32[]{:S(2)}, u32[]{:S(2)}) collective-permute-start(f32[1,8,384]{2,1,0:T(8,128)S(1)} %get-tuple-element.41), channel_id=1, source_target_pairs={{8,16},{16,8},{9,17},{17,9},{10,18},{18,10},{11,19},{19,11},{12,20... | collective-permute-start | bytes 36872 | tf_op jit(solution)/shard_map/ppermute | solution.py:82

commit v15 on v14

--- a/solution.py
+++ b/solution.py
@@ -315,7 +315,9 @@
     near[0], far[0] = sort_swap("lat", to_north, to_south)
 
 
-def run_forward(coeffs, start, forcing, near, far, final, state):
+def run_forward(coeffs, start, forcing, near, far, weights, final, weights_near, state, arrived):
+    bring = pltpu.make_async_copy(weights.at[: weights_near.shape[0]], weights_near, arrived)
+    bring.start()
     levels = coeffs.shape[1]
     tile_lat, tile_lon = final.shape[2:]
     for f in range(2):
@@ -341,6 +343,7 @@
                     final[f, level] = out[:tile_lat, :tile_lon]
                 else:
                     state[step % 2, level] = out
+    bring.wait()
 
 
 def split(x):
@@ -353,9 +356,10 @@
     return pltpu.make_async_copy(weights.at[own], held.at[own], arrived.at[n])
 
 
-def fetch_weights(weights, held, arrived):
+def fetch_weights(weights, held, arrived, near=None):
     for n in range(held.shape[0] // FETCH):
-        weight_copy(weights, held, arrived, n).start()
+        source = near if near is not None and (n + 1) * FETCH <= near.shape[0] else weights
+        weight_copy(source, held, arrived, n).start()
 
 
 def held_part(weights, held, arrived):
@@ -539,10 +543,10 @@
 
 
 def unweigh(
-    gathered, keys, counts, columns_in, lines_in, starts_in, weights, gradient, result, columns, lines, starts, *scratch
+    gathered, keys, counts, columns_in, lines_in, starts_in, weights_near, weights, gradient, result, columns, lines, starts, *scratch
 ):
     scratch, (held, arrived) = scratch[:3], scratch[3:]
-    fetch_weights(weights, held, arrived)
+    fetch_weights(weights, held, arrived, weights_near)
     blocks = weights.shape[0]
     lon_count, ocean_blocks = gathered.shape[0], gathered.shape[1] // 2
     order = group_order(lon_count)
@@ -679,13 +683,14 @@
         name="finish_adjoint",
         inputs=3,
     )(coeffs, start, states)
-    (final,) = call(
+    final, weights_near = call(
         run_forward,
-        [tracers.shape],
-        [pltpu.VMEM((2, levels, *wide), f32)],
+        [tracers.shape, (blocks_of // 2, BLOCK, BLOCK)],
+        [pltpu.VMEM((2, levels, *wide), f32), pltpu.SemaphoreType.DMA],
         name="run_forward",
-        inputs=5,
-    )(coeffs, start, forcing, near_rows, far_rows)
+        inputs=6,
+        far=(5,),
+    )(coeffs, start, forcing, near_rows, far_rows, weights)
 
     (gradient,) = call(
         unweigh,
@@ -693,9 +698,9 @@
         [coupling_scratch(atm)[0], *map(in_vmem, found), *coupling_scratch(atm)[1:]],
         coupling_flops,
         name="unweigh",
-        inputs=7,
-        far=(6,),
-    )(gathered, *slot_data, weights)
+        inputs=8,
+        far=(7,),
+    )(gathered, *slot_data, weights_near, weights)
     return (final, adjoint, gradient)
 
 

time: 40.5 us -> 40.4 us (level)
  transfers between devices with their start and end apart: 8 -> 8, of which waited for: 2 -> 2; matrix products, arithmetic and copies ran while one was open for 0% -> 0% of each run, Pallas kernels for 21% -> 22%
where the time goes in v15:
time: 40.4 us; the launch traced here: 40 us
  starting transfers between devices  23 us (57%)
  Pallas kernels  13.2 us (33%)
  waiting for transfers between devices  3.03 us (8%)
  between operations  0.73 us (2%)
    pallas_call x8, Pallas kernels, run(): kernel(*(pltpu.with_memory_space_constraint(x, pltpu.HBM) if n in far els...  13.2 us
    ppermute x3, starting transfers between devices, swap(): far = lax.ppermute(far, axis, pairs[1])  12.6 us
    all_to_all x2, starting transfers between devices, exchange(): lax.all_to_all(x, 'lon', split_axis=0, concat_axis=0, tiled=True, axis_in...  8.23 us
    ppermute x3, waiting for transfers between devices, swap(): far = lax.ppermute(far, axis, pairs[1])  3.02 us
    ppermute x3, starting transfers between devices, swap(): return (lax.ppermute(near, axis, pairs[0]), far)  2.18 us
  transfers between devices with their start and end apart: 8, of which 2 were waited for; matrix products, arithmetic and copies ran while one was open for 0% of the time, Pallas kernels for 22%

profile of v15, /device:TPU:1, one launch (start us, length us, event | category | flops | bytes accessed | tf_op | source)
XLA Modules:
  0.0 40.0 jit_solution(18135043627876186322)
XLA Ops:
  0.6 1.4 %pack_columns.1 = (f32[35,16,256]{2,1,0:T(8,128)S(1)}, f32[2,16,128]{2,1,0:T(8,128)S(1)}, f32[2,16,128]{2,1,0:T(8,128)S(1)}, f32[2,1,256,128]{3,2,1,0:T(8,128)S(1)}, s32[3,1,1,8,64]{4,3,2,1,0:T(8,128)S(1)}) custom-call(f32[2,4,16,256]{3,2,1,0:T(8,128)} %refs_0_.1, f32[2,4,16,256]{3,2,1,0:T(8,128)} %refs_1_.1, s32[4,16,256]{2,1,0:T(8,128)} %refs_2_.1, ...), custom_call_target="tpu_custom_call" | custom-call | bytes 1048576 | tf_op jit(solution)/shard_map/pack_columns/pallas_call | solution.py:46
  2.1 2.1 %collective-permute-start = (f32[2,16,128]{2,1,0:T(8,128)S(1)}, f32[2,16,128]{2,1,0:T(8,128)S(1)}, u32[]{:S(2)}, u32[]{:S(2)}) collective-permute-start(f32[2,16,128]{2,1,0:T(8,128)S(1)} %get-tuple-element.29), channel_id=1, source_target_pairs={{0,1},{1,0},{2,3},{3,2},{4,5},{5,4},{6,7},{7,6},{8,9},{9,8},{10,11... | collective-permute-start | bytes 49160 | tf_op jit(solution)/shard_map/ppermute | solution.py:83
  4.2 3.3 %collective-permute-start.1 = (f32[2,16,128]{2,1,0:T(8,128)S(1)}, f32[2,16,128]{2,1,0:T(8,128)S(1)}, u32[]{:S(2)}, u32[]{:S(2)}) collective-permute-start(f32[2,16,128]{2,1,0:T(8,128)S(1)} %get-tuple-element.30.after), channel_id=1, source_target_pairs={{1,2},{2,1},{3,4},{4,3},{5,6},{6,5},{7,0},{0,7},{9,10},{10,9},{11,... | collective-permute-start | bytes 49160 | tf_op jit(solution)/shard_map/ppermute | solution.py:82
  7.5 3.7 %weigh.1 = (f32[8,72,128]{2,1,0:T(8,128)}, f32[8,512]{1,0:T(8,128)S(1)}, f32[32,128]{1,0:T(8,128)S(1)}, f32[2,128,128]{2,1,0:T(8,128)S(1)}, f32[2,8,128]{2,1,0:T(8,128)S(1)}, /*index=5*/s32[32,128]{1,0:T(8,128)S(1)}) custom-call(f32[2,1,256,128]{3,2,1,0:T(8,128)S(1)} %get-tuple-element.31.atm_near, s32[3,1,1,8,64]{4,3,2,1,0:T(8,128)S(1)} %get-tuple-element.32.margins, ...), custom_call_target="tpu_custom_call" | custom-call | flops 4294967296 | bytes 1048576 | tf_op jit(solution)/shard_map/weigh/pallas_call | solution.py:46
  11.2 0.0 collective-permute-done.near_columns
  11.2 0.0 collective-permute-done.1.far_columns
  11.3 3.6 %all-to-all-start = ((f32[8,72,128]{2,1,0:T(8,128)}), f32[8,72,128]{2,1,0:T(8,128)S(1)}, u32[]{:S(2)}, u32[]{:S(2)}) async-start(f32[8,72,128]{2,1,0:T(8,128)} %get-tuple-element.40), calls=%async_computation | async-start | bytes 589824 | tf_op jit(solution)/shard_map/all_to_all | solution.py:73
  14.9 5.2 %collective-permute-start.2 = (f32[37,8,128]{2,1,0:T(8,128)S(1)}, f32[37,8,128]{2,1,0:T(8,128)S(1)}, u32[]{:S(2)}, u32[]{:S(2)}) collective-permute-start(f32[37,8,128]{2,1,0:T(8,128)S(1)} %get-tuple-element.36), channel_id=1, source_target_pairs={{8,16},{16,8},{9,17},{17,9},{10,18},{18,10},{11,19},{19,11},{12,20... | collective-permute-start | bytes 454664 | tf_op jit(solution)/shard_map/ppermute | solution.py:82
  20.1 0.1 collective-permute-start.3
  20.2 2.8 %collective-permute-done.2.far = f32[37,8,128]{2,1,0:T(8,128)S(1)} collective-permute-done((f32[37,8,128]{2,1,0:T(8,128)S(1)}, f32[37,8,128]{2,1,0:T(8,128)S(1)}, u32[]{:S(2)}, u32[]{:S(2)}) %collective-permute-start.2) | collective-permute-done | bytes 151584 | tf_op jit(solution)/shard_map/ppermute | solution.py:82
  22.9 0.0 collective-permute-done.3.near
  22.9 1.6 %run_adjoint.1 = (f32[8,64,128]{2,1,0:T(8,128)}, f32[6,4,24,384]{3,2,1,0:T(8,128)S(1)}, f32[16,24,384]{2,1,0:T(8,128)S(1)}, f32[2,3,4,24,384]{4,3,2,1,0:T(8,128)S(1)}) custom-call(f32[35,16,256]{2,1,0:T(8,128)S(1)} %get-tuple-element.28.fields, f32[2,16,128]{2,1,0:T(8,128)S(1)} %get-tuple-element.34.from_west, ...), custom_call_target="tpu_custom_call" | custom-call | bytes 1048576 | tf_op jit(solution)/shard_map/run_adjoint/pallas_call | solution.py:46
  24.6 0.0 all-to-all-done.received
  24.6 4.6 %all-to-all-start.1 = ((f32[8,64,128]{2,1,0:T(8,128)}), f32[8,64,128]{2,1,0:T(8,128)S(1)}, u32[]{:S(2)}, u32[]{:S(2)}) async-start(f32[8,64,128]{2,1,0:T(8,128)} %get-tuple-element.46), calls=%async_computation.1 | async-start | bytes 524288 | tf_op jit(solution)/shard_map/all_to_all | solution.py:73
  29.1 0.1 sum_forcing.1
  29.3 0.0 collective-permute-start.4
  29.3 4.2 %collective-permute-start.5 = (f32[1,8,384]{2,1,0:T(8,128)S(1)}, f32[1,8,384]{2,1,0:T(8,128)S(1)}, u32[]{:S(2)}, u32[]{:S(2)}) collective-permute-start(f32[1,8,384]{2,1,0:T(8,128)S(1)} %get-tuple-element.43), channel_id=1, source_target_pairs={{8,16},{16,8},{9,17},{17,9},{10,18},{18,10},{11,19},{19,11},{12,20... | collective-permute-start | bytes 36872 | tf_op jit(solution)/shard_map/ppermute | solution.py:82
  33.5 1.4 %finish_adjoint.1 = f32[2,4,16,256]{3,2,1,0:T(8,128)} custom-call(f32[6,4,24,384]{3,2,1,0:T(8,128)S(1)} %get-tuple-element.38.coeffs, f32[16,24,384]{2,1,0:T(8,128)S(1)} %get-tuple-element.39.start, f32[2,3,4,24,384]{4,3,2,1,0:T(8,128)S(1)} %get-tuple-element.45.states), custom_call_target="tpu_custom_call" | custom-call | bytes 1048576 | tf_op jit(solution)/shard_map/finish_adjoint/pallas_call | solution.py:46
  34.9 0.0 collective-permute-done.4.near
  34.9 0.2 collective-permute-done.5.far
  35.1 1.9 %run_forward.1 = (f32[2,4,16,256]{3,2,1,0:T(8,128)}, f32[16,128,128]{2,1,0:T(8,128)S(1)}) custom-call(f32[6,4,24,384]{3,2,1,0:T(8,128)S(1)} %get-tuple-element.38.coeffs, f32[16,24,384]{2,1,0:T(8,128)S(1)} %get-tuple-element.39.start, f32[2,16,384]{2,1,0:T(8,128)S(1)} %get-tuple-element.41.forcing, f32[1,8,384]{2,1,0:T(8,128)S(1)} %collective-permute-done.4.near, ...), custom_call_target="tpu_custom_call" | custom-call | bytes 1048576 | tf_op jit(solution)/shard_map/run_forward/pallas_call | solution.py:46
  37.0 0.0 all-to-all-done.1.gathered
  37.0 3.0 %unweigh.1 = f32[2,1,256,128]{3,2,1,0:T(8,128)} custom-call(f32[8,64,128]{2,1,0:T(8,128)S(1)} %all-to-all-done.1.gathered, f32[8,512]{1,0:T(8,128)S(1)} %get-tuple-element.47.keys, f32[32,128]{1,0:T(8,128)S(1)} %get-tuple-element.48.counts, f32[2,128,128]{2,1,0:T(8,128)S(1)} %get-tuple-element.49.columns_in, f32[2,8,128]{2,1,0:T(8,128)S(1)} %get-tuple-element.50.lines_in, ...), custom_call_target="tpu_custom_call" | custom-call | flops 4294967296 | bytes 1048576 | tf_op jit(solution)/shard_map/unweigh/pallas_call | solution.py:46
  (1 shorter events, 0.0 us)
Async XLA Ops:
  2.1 9.1 %collective-permute-start = (f32[2,16,128]{2,1,0:T(8,128)S(1)}, f32[2,16,128]{2,1,0:T(8,128)S(1)}, u32[]{:S(2)}, u32[]{:S(2)}) collective-permute-start(f32[2,16,128]{2,1,0:T(8,128)S(1)} %get-tuple-element.29), channel_id=1, source_target_pairs={{0,1},{1,0},{2,3},{3,2},{4,5},{5,4},{6,7},{7,6},{8,9},{9,8},{10,11... | collective-permute-start | bytes 49160 | tf_op jit(solution)/shard_map/ppermute | solution.py:83
  4.2 7.0 %collective-permute-start.1 = (f32[2,16,128]{2,1,0:T(8,128)S(1)}, f32[2,16,128]{2,1,0:T(8,128)S(1)}, u32[]{:S(2)}, u32[]{:S(2)}) collective-permute-start(f32[2,16,128]{2,1,0:T(8,128)S(1)} %get-tuple-element.30.after), channel_id=1, source_target_pairs={{1,2},{2,1},{3,4},{4,3},{5,6},{6,5},{7,0},{0,7},{9,10},{10,9},{11,... | collective-permute-start | bytes 49160 | tf_op jit(solution)/shard_map/ppermute | solution.py:82
  11.3 13.3 %all-to-all-start = ((f32[8,72,128]{2,1,0:T(8,128)}), f32[8,72,128]{2,1,0:T(8,128)S(1)}, u32[]{:S(2)}, u32[]{:S(2)}) async-start(f32[8,72,128]{2,1,0:T(8,128)} %get-tuple-element.40), calls=%async_computation | async-start | bytes 589824 | tf_op jit(solution)/shard_map/all_to_all | solution.py:73
  14.9 8.0 %collective-permute-start.2 = (f32[37,8,128]{2,1,0:T(8,128)S(1)}, f32[37,8,128]{2,1,0:T(8,128)S(1)}, u32[]{:S(2)}, u32[]{:S(2)}) collective-permute-start(f32[37,8,128]{2,1,0:T(8,128)S(1)} %get-tuple-element.36), channel_id=1, source_target_pairs={{8,16},{16,8},{9,17},{17,9},{10,18},{18,10},{11,19},{19,11},{12,20... | collective-permute-start | bytes 454664 | tf_op jit(solution)/shard_map/ppermute | solution.py:82
  20.1 2.9 %collective-permute-start.3 = (f32[37,8,128]{2,1,0:T(8,128)S(1)}, f32[37,8,128]{2,1,0:T(8,128)S(1)}, u32[]{:S(2)}, u32[]{:S(2)}) collective-permute-start(f32[37,8,128]{2,1,0:T(8,128)S(1)} %get-tuple-element.37), channel_id=1, source_target_pairs={{0,8},{8,0},{16,24},{24,16},{1,9},{9,1},{17,25},{25,17},{2,10},{10... | collective-permute-start | bytes 454664 | tf_op jit(solution)/shard_map/ppermute | solution.py:83
  24.6 12.5 %all-to-all-start.1 = ((f32[8,64,128]{2,1,0:T(8,128)}), f32[8,64,128]{2,1,0:T(8,128)S(1)}, u32[]{:S(2)}, u32[]{:S(2)}) async-start(f32[8,64,128]{2,1,0:T(8,128)} %get-tuple-element.46), calls=%async_computation.1 | async-start | bytes 524288 | tf_op jit(solution)/shard_map/all_to_all | solution.py:73
  29.3 5.6 %collective-permute-start.4 = (f32[1,8,384]{2,1,0:T(8,128)S(1)}, f32[1,8,384]{2,1,0:T(8,128)S(1)}, u32[]{:S(2)}, u32[]{:S(2)}) collective-permute-start(f32[1,8,384]{2,1,0:T(8,128)S(1)} %get-tuple-element.42), channel_id=1, source_target_pairs={{0,8},{8,0},{16,24},{24,16},{1,9},{9,1},{17,25},{25,17},{2,10},{10... | collective-permute-start | bytes 36872 | tf_op jit(solution)/shard_map/ppermute | solution.py:83
  29.3 5.8 %collective-permute-start.5 = (f32[1,8,384]{2,1,0:T(8,128)S(1)}, f32[1,8,384]{2,1,0:T(8,128)S(1)}, u32[]{:S(2)}, u32[]{:S(2)}) collective-permute-start(f32[1,8,384]{2,1,0:T(8,128)S(1)} %get-tuple-element.43), channel_id=1, source_target_pairs={{8,16},{16,8},{9,17},{17,9},{10,18},{18,10},{11,19},{19,11},{12,20... | collective-permute-start | bytes 36872 | tf_op jit(solution)/shard_map/ppermute | solution.py:82

commit v16 on v15

--- a/solution.py
+++ b/solution.py
@@ -316,8 +316,7 @@
 
 
 def run_forward(coeffs, start, forcing, near, far, weights, final, weights_near, state, arrived):
-    bring = pltpu.make_async_copy(weights.at[: weights_near.shape[0]], weights_near, arrived)
-    bring.start()
+    fetch_weights(weights, weights_near, arrived)
     levels = coeffs.shape[1]
     tile_lat, tile_lon = final.shape[2:]
     for f in range(2):
@@ -343,7 +342,8 @@
                     final[f, level] = out[:tile_lat, :tile_lon]
                 else:
                     state[step % 2, level] = out
-    bring.wait()
+    for n in range(weights_near.shape[0] // FETCH):
+        weight_copy(weights, weights_near, arrived, n).wait()
 
 
 def split(x):
@@ -686,7 +686,7 @@
     final, weights_near = call(
         run_forward,
         [tracers.shape, (blocks_of // 2, BLOCK, BLOCK)],
-        [pltpu.VMEM((2, levels, *wide), f32), pltpu.SemaphoreType.DMA],
+        [pltpu.VMEM((2, levels, *wide), f32), pltpu.SemaphoreType.DMA((blocks_of // 2 // FETCH,))],
         name="run_forward",
         inputs=6,
         far=(5,),

time: 40.4 us -> 41.1 us (1.017)
  Pallas kernels: 13.2 us -> 13.9 us
    pallas_call x8, Pallas kernels: 13.2 us -> 13.9 us  [run(): kernel(*(pltpu.with_memory_space_constraint(x, pltpu.HBM) if n in far els...]
  transfers between devices with their start and end apart: 8 -> 8, of which waited for: 2 -> 2; matrix products, arithmetic and copies ran while one was open for 0% -> 0% of each run, Pallas kernels for 22% -> 23%
where the time goes in v16:
time: 41.1 us; the launch traced here: 40.6 us
  starting transfers between devices  23 us (56%)
  Pallas kernels  13.9 us (34%)
  waiting for transfers between devices  3.03 us (7%)
  between operations  0.73 us (2%)
    pallas_call x8, Pallas kernels, run(): kernel(*(pltpu.with_memory_space_constraint(x, pltpu.HBM) if n in far els...  13.9 us
    ppermute x3, starting transfers between devices, swap(): far = lax.ppermute(far, axis, pairs[1])  12.6 us
    all_to_all x2, starting transfers between devices, exchange(): lax.all_to_all(x, 'lon', split_axis=0, concat_axis=0, tiled=True, axis_in...  8.23 us
    ppermute x3, waiting for transfers between devices, swap(): far = lax.ppermute(far, axis, pairs[1])  3.02 us
    ppermute x3, starting transfers between devices, swap(): return (lax.ppermute(near, axis, pairs[0]), far)  2.18 us
  transfers between devices with their start and end apart: 8, of which 2 were waited for; matrix products, arithmetic and copies ran while one was open for 0% of the time, Pallas kernels for 23%

profile of v16, /device:TPU:1, one launch (start us, length us, event | category | flops | bytes accessed | tf_op | source)
XLA Modules:
  0.0 40.6 jit_solution(2658741978352979950)
XLA Ops:
  0.6 1.4 %pack_columns.1 = (f32[35,16,256]{2,1,0:T(8,128)S(1)}, f32[2,16,128]{2,1,0:T(8,128)S(1)}, f32[2,16,128]{2,1,0:T(8,128)S(1)}, f32[2,1,256,128]{3,2,1,0:T(8,128)S(1)}, s32[3,1,1,8,64]{4,3,2,1,0:T(8,128)S(1)}) custom-call(f32[2,4,16,256]{3,2,1,0:T(8,128)} %refs_0_.1, f32[2,4,16,256]{3,2,1,0:T(8,128)} %refs_1_.1, s32[4,16,256]{2,1,0:T(8,128)} %refs_2_.1, ...), custom_call_target="tpu_custom_call" | custom-call | bytes 1048576 | tf_op jit(solution)/shard_map/pack_columns/pallas_call | solution.py:46
  2.1 2.1 %collective-permute-start = (f32[2,16,128]{2,1,0:T(8,128)S(1)}, f32[2,16,128]{2,1,0:T(8,128)S(1)}, u32[]{:S(2)}, u32[]{:S(2)}) collective-permute-start(f32[2,16,128]{2,1,0:T(8,128)S(1)} %get-tuple-element.29), channel_id=1, source_target_pairs={{0,1},{1,0},{2,3},{3,2},{4,5},{5,4},{6,7},{7,6},{8,9},{9,8},{10,11... | collective-permute-start | bytes 49160 | tf_op jit(solution)/shard_map/ppermute | solution.py:83
  4.2 3.3 %collective-permute-start.1 = (f32[2,16,128]{2,1,0:T(8,128)S(1)}, f32[2,16,128]{2,1,0:T(8,128)S(1)}, u32[]{:S(2)}, u32[]{:S(2)}) collective-permute-start(f32[2,16,128]{2,1,0:T(8,128)S(1)} %get-tuple-element.30.after), channel_id=1, source_target_pairs={{1,2},{2,1},{3,4},{4,3},{5,6},{6,5},{7,0},{0,7},{9,10},{10,9},{11,... | collective-permute-start | bytes 49160 | tf_op jit(solution)/shard_map/ppermute | solution.py:82
  7.5 3.7 %weigh.1 = (f32[8,72,128]{2,1,0:T(8,128)}, f32[8,512]{1,0:T(8,128)S(1)}, f32[32,128]{1,0:T(8,128)S(1)}, f32[2,128,128]{2,1,0:T(8,128)S(1)}, f32[2,8,128]{2,1,0:T(8,128)S(1)}, /*index=5*/s32[32,128]{1,0:T(8,128)S(1)}) custom-call(f32[2,1,256,128]{3,2,1,0:T(8,128)S(1)} %get-tuple-element.31.atm_near, s32[3,1,1,8,64]{4,3,2,1,0:T(8,128)S(1)} %get-tuple-element.32.margins, ...), custom_call_target="tpu_custom_call" | custom-call | flops 4294967296 | bytes 1048576 | tf_op jit(solution)/shard_map/weigh/pallas_call | solution.py:46
  11.2 0.0 collective-permute-done.near_columns
  11.2 0.0 collective-permute-done.1.far_columns
  11.3 3.6 %all-to-all-start = ((f32[8,72,128]{2,1,0:T(8,128)}), f32[8,72,128]{2,1,0:T(8,128)S(1)}, u32[]{:S(2)}, u32[]{:S(2)}) async-start(f32[8,72,128]{2,1,0:T(8,128)} %get-tuple-element.40), calls=%async_computation | async-start | bytes 589824 | tf_op jit(solution)/shard_map/all_to_all | solution.py:73
  14.9 5.2 %collective-permute-start.2 = (f32[37,8,128]{2,1,0:T(8,128)S(1)}, f32[37,8,128]{2,1,0:T(8,128)S(1)}, u32[]{:S(2)}, u32[]{:S(2)}) collective-permute-start(f32[37,8,128]{2,1,0:T(8,128)S(1)} %get-tuple-element.36), channel_id=1, source_target_pairs={{8,16},{16,8},{9,17},{17,9},{10,18},{18,10},{11,19},{19,11},{12,20... | collective-permute-start | bytes 454664 | tf_op jit(solution)/shard_map/ppermute | solution.py:82
  20.1 0.1 collective-permute-start.3
  20.2 2.8 %collective-permute-done.2.far = f32[37,8,128]{2,1,0:T(8,128)S(1)} collective-permute-done((f32[37,8,128]{2,1,0:T(8,128)S(1)}, f32[37,8,128]{2,1,0:T(8,128)S(1)}, u32[]{:S(2)}, u32[]{:S(2)}) %collective-permute-start.2) | collective-permute-done | bytes 151584 | tf_op jit(solution)/shard_map/ppermute | solution.py:82
  22.9 0.0 collective-permute-done.3.near
  22.9 1.6 %run_adjoint.1 = (f32[8,64,128]{2,1,0:T(8,128)}, f32[6,4,24,384]{3,2,1,0:T(8,128)S(1)}, f32[16,24,384]{2,1,0:T(8,128)S(1)}, f32[2,3,4,24,384]{4,3,2,1,0:T(8,128)S(1)}) custom-call(f32[35,16,256]{2,1,0:T(8,128)S(1)} %get-tuple-element.28.fields, f32[2,16,128]{2,1,0:T(8,128)S(1)} %get-tuple-element.34.from_west, ...), custom_call_target="tpu_custom_call" | custom-call | bytes 1048576 | tf_op jit(solution)/shard_map/run_adjoint/pallas_call | solution.py:46
  24.6 0.0 all-to-all-done.received
  24.6 4.6 %all-to-all-start.1 = ((f32[8,64,128]{2,1,0:T(8,128)}), f32[8,64,128]{2,1,0:T(8,128)S(1)}, u32[]{:S(2)}, u32[]{:S(2)}) async-start(f32[8,64,128]{2,1,0:T(8,128)} %get-tuple-element.46), calls=%async_computation.1 | async-start | bytes 524288 | tf_op jit(solution)/shard_map/all_to_all | solution.py:73
  29.1 0.1 sum_forcing.1
  29.3 0.0 collective-permute-start.4
  29.3 4.2 %collective-permute-start.5 = (f32[1,8,384]{2,1,0:T(8,128)S(1)}, f32[1,8,384]{2,1,0:T(8,128)S(1)}, u32[]{:S(2)}, u32[]{:S(2)}) collective-permute-start(f32[1,8,384]{2,1,0:T(8,128)S(1)} %get-tuple-element.43), channel_id=1, source_target_pairs={{8,16},{16,8},{9,17},{17,9},{10,18},{18,10},{11,19},{19,11},{12,20... | collective-permute-start | bytes 36872 | tf_op jit(solution)/shard_map/ppermute | solution.py:82
  33.5 1.4 %finish_adjoint.1 = f32[2,4,16,256]{3,2,1,0:T(8,128)} custom-call(f32[6,4,24,384]{3,2,1,0:T(8,128)S(1)} %get-tuple-element.38.coeffs, f32[16,24,384]{2,1,0:T(8,128)S(1)} %get-tuple-element.39.start, f32[2,3,4,24,384]{4,3,2,1,0:T(8,128)S(1)} %get-tuple-element.45.states), custom_call_target="tpu_custom_call" | custom-call | bytes 1048576 | tf_op jit(solution)/shard_map/finish_adjoint/pallas_call | solution.py:46
  34.9 0.0 collective-permute-done.4.near
  34.9 0.2 collective-permute-done.5.far
  35.1 2.5 %run_forward.1 = (f32[2,4,16,256]{3,2,1,0:T(8,128)}, f32[16,128,128]{2,1,0:T(8,128)S(1)}) custom-call(f32[6,4,24,384]{3,2,1,0:T(8,128)S(1)} %get-tuple-element.38.coeffs, f32[16,24,384]{2,1,0:T(8,128)S(1)} %get-tuple-element.39.start, f32[2,16,384]{2,1,0:T(8,128)S(1)} %get-tuple-element.41.forcing, f32[1,8,384]{2,1,0:T(8,128)S(1)} %collective-permute-done.4.near, ...), custom_call_target="tpu_custom_call" | custom-call | bytes 1048576 | tf_op jit(solution)/shard_map/run_forward/pallas_call | solution.py:46
  37.7 0.0 all-to-all-done.1.gathered
  37.7 3.0 %unweigh.1 = f32[2,1,256,128]{3,2,1,0:T(8,128)} custom-call(f32[8,64,128]{2,1,0:T(8,128)S(1)} %all-to-all-done.1.gathered, f32[8,512]{1,0:T(8,128)S(1)} %get-tuple-element.47.keys, f32[32,128]{1,0:T(8,128)S(1)} %get-tuple-element.48.counts, f32[2,128,128]{2,1,0:T(8,128)S(1)} %get-tuple-element.49.columns_in, f32[2,8,128]{2,1,0:T(8,128)S(1)} %get-tuple-element.50.lines_in, ...), custom_call_target="tpu_custom_call" | custom-call | flops 4294967296 | bytes 1048576 | tf_op jit(solution)/shard_map/unweigh/pallas_call | solution.py:46
  (1 shorter events, 0.0 us)
Async XLA Ops:
  2.1 9.1 %collective-permute-start = (f32[2,16,128]{2,1,0:T(8,128)S(1)}, f32[2,16,128]{2,1,0:T(8,128)S(1)}, u32[]{:S(2)}, u32[]{:S(2)}) collective-permute-start(f32[2,16,128]{2,1,0:T(8,128)S(1)} %get-tuple-element.29), channel_id=1, source_target_pairs={{0,1},{1,0},{2,3},{3,2},{4,5},{5,4},{6,7},{7,6},{8,9},{9,8},{10,11... | collective-permute-start | bytes 49160 | tf_op jit(solution)/shard_map/ppermute | solution.py:83
  4.2 7.0 %collective-permute-start.1 = (f32[2,16,128]{2,1,0:T(8,128)S(1)}, f32[2,16,128]{2,1,0:T(8,128)S(1)}, u32[]{:S(2)}, u32[]{:S(2)}) collective-permute-start(f32[2,16,128]{2,1,0:T(8,128)S(1)} %get-tuple-element.30.after), channel_id=1, source_target_pairs={{1,2},{2,1},{3,4},{4,3},{5,6},{6,5},{7,0},{0,7},{9,10},{10,9},{11,... | collective-permute-start | bytes 49160 | tf_op jit(solution)/shard_map/ppermute | solution.py:82
  11.3 13.3 %all-to-all-start = ((f32[8,72,128]{2,1,0:T(8,128)}), f32[8,72,128]{2,1,0:T(8,128)S(1)}, u32[]{:S(2)}, u32[]{:S(2)}) async-start(f32[8,72,128]{2,1,0:T(8,128)} %get-tuple-element.40), calls=%async_computation | async-start | bytes 589824 | tf_op jit(solution)/shard_map/all_to_all | solution.py:73
  14.9 8.0 %collective-permute-start.2 = (f32[37,8,128]{2,1,0:T(8,128)S(1)}, f32[37,8,128]{2,1,0:T(8,128)S(1)}, u32[]{:S(2)}, u32[]{:S(2)}) collective-permute-start(f32[37,8,128]{2,1,0:T(8,128)S(1)} %get-tuple-element.36), channel_id=1, source_target_pairs={{8,16},{16,8},{9,17},{17,9},{10,18},{18,10},{11,19},{19,11},{12,20... | collective-permute-start | bytes 454664 | tf_op jit(solution)/shard_map/ppermute | solution.py:82
  20.1 2.9 %collective-permute-start.3 = (f32[37,8,128]{2,1,0:T(8,128)S(1)}, f32[37,8,128]{2,1,0:T(8,128)S(1)}, u32[]{:S(2)}, u32[]{:S(2)}) collective-permute-start(f32[37,8,128]{2,1,0:T(8,128)S(1)} %get-tuple-element.37), channel_id=1, source_target_pairs={{0,8},{8,0},{16,24},{24,16},{1,9},{9,1},{17,25},{25,17},{2,10},{10... | collective-permute-start | bytes 454664 | tf_op jit(solution)/shard_map/ppermute | solution.py:83
  24.6 13.1 %all-to-all-start.1 = ((f32[8,64,128]{2,1,0:T(8,128)}), f32[8,64,128]{2,1,0:T(8,128)S(1)}, u32[]{:S(2)}, u32[]{:S(2)}) async-start(f32[8,64,128]{2,1,0:T(8,128)} %get-tuple-element.46), calls=%async_computation.1 | async-start | bytes 524288 | tf_op jit(solution)/shard_map/all_to_all | solution.py:73
  29.3 5.6 %collective-permute-start.4 = (f32[1,8,384]{2,1,0:T(8,128)S(1)}, f32[1,8,384]{2,1,0:T(8,128)S(1)}, u32[]{:S(2)}, u32[]{:S(2)}) collective-permute-start(f32[1,8,384]{2,1,0:T(8,128)S(1)} %get-tuple-element.42), channel_id=1, source_target_pairs={{0,8},{8,0},{16,24},{24,16},{1,9},{9,1},{17,25},{25,17},{2,10},{10... | collective-permute-start | bytes 36872 | tf_op jit(solution)/shard_map/ppermute | solution.py:83
  29.3 5.8 %collective-permute-start.5 = (f32[1,8,384]{2,1,0:T(8,128)S(1)}, f32[1,8,384]{2,1,0:T(8,128)S(1)}, u32[]{:S(2)}, u32[]{:S(2)}) collective-permute-start(f32[1,8,384]{2,1,0:T(8,128)S(1)} %get-tuple-element.43), channel_id=1, source_target_pairs={{8,16},{16,8},{9,17},{17,9},{10,18},{18,10},{11,19},{19,11},{12,20... | collective-permute-start | bytes 36872 | tf_op jit(solution)/shard_map/ppermute | solution.py:82

commit v17 on v14

--- a/solution.py
+++ b/solution.py
@@ -268,7 +268,9 @@
         copy.wait()
 
 
-def finish_adjoint(coeffs, start, states, adjoint_out, rest):
+def finish_adjoint(coeffs, start, states, weights, adjoint_out, weights_near, rest, arrived):
+    bring = pltpu.make_async_copy(weights.at[: weights_near.shape[0]], weights_near, arrived)
+    bring.start()
     levels = coeffs.shape[1]
     tile_lat, tile_lon = adjoint_out.shape[2:]
     for f in range(2):
@@ -287,6 +289,7 @@
                     rest[f, step, level] = lam
 
             adjoint_step(coeffs, read, write, done, levels)
+    bring.wait()
 
 
 def sum_forcing(received, forcing, near, far):
@@ -353,9 +356,10 @@
     return pltpu.make_async_copy(weights.at[own], held.at[own], arrived.at[n])
 
 
-def fetch_weights(weights, held, arrived):
+def fetch_weights(weights, held, arrived, near=None):
     for n in range(held.shape[0] // FETCH):
-        weight_copy(weights, held, arrived, n).start()
+        source = near if near is not None and (n + 1) * FETCH <= near.shape[0] else weights
+        weight_copy(source, held, arrived, n).start()
 
 
 def held_part(weights, held, arrived):
@@ -539,10 +543,10 @@
 
 
 def unweigh(
-    gathered, keys, counts, columns_in, lines_in, starts_in, weights, gradient, result, columns, lines, starts, *scratch
+    gathered, keys, counts, columns_in, lines_in, starts_in, weights_near, weights, gradient, result, columns, lines, starts, *scratch
 ):
     scratch, (held, arrived) = scratch[:3], scratch[3:]
-    fetch_weights(weights, held, arrived)
+    fetch_weights(weights, held, arrived, weights_near)
     blocks = weights.shape[0]
     lon_count, ocean_blocks = gathered.shape[0], gathered.shape[1] // 2
     order = group_order(lon_count)
@@ -672,13 +676,14 @@
         sum_forcing, [(2, tile_lat, tile_lon + BLOCK), message, message], name="sum_forcing", inputs=1
     )(received)
     near_rows, far_rows = swap(near, far, "lat", False)
-    (adjoint,) = call(
+    adjoint, weights_near = call(
         finish_adjoint,
-        [cotangent.shape],
-        [pltpu.VMEM(adjoint_states, f32)],
+        [cotangent.shape, (blocks_of // 2, BLOCK, BLOCK)],
+        [pltpu.VMEM(adjoint_states, f32), pltpu.SemaphoreType.DMA],
         name="finish_adjoint",
-        inputs=3,
-    )(coeffs, start, states)
+        inputs=4,
+        far=(3,),
+    )(coeffs, start, states, weights)
     (final,) = call(
         run_forward,
         [tracers.shape],
@@ -693,9 +698,9 @@
         [coupling_scratch(atm)[0], *map(in_vmem, found), *coupling_scratch(atm)[1:]],
         coupling_flops,
         name="unweigh",
-        inputs=7,
-        far=(6,),
-    )(gathered, *slot_data, weights)
+        inputs=8,
+        far=(7,),
+    )(gathered, *slot_data, weights_near, weights)
     return (final, adjoint, gradient)
 
 

time: 40.5 us -> 42.6 us (1.052)
  local copies, waits for them, and re-layouts: 0 us -> 2.2 us
    unnamed x0 -> x4, local copies, waits for them, and re-layouts: none -> 2.2 us
  transfers between devices with their start and end apart: 8 -> 8, of which waited for: 2 -> 1; matrix products, arithmetic and copies ran while one was open for 0% -> 0% of each run, Pallas kernels for 21% -> 21%
where the time goes in v17:
time: 42.6 us; the launch traced here: 42.1 us
  starting transfers between devices  23 us (54%)
  Pallas kernels  13.4 us (31%)
  waiting for transfers between devices  2.8 us (7%)
  local copies, waits for them, and re-layouts  2.2 us (5%)
  between operations  0.74 us (2%)
    pallas_call x8, Pallas kernels, run(): kernel(*(pltpu.with_memory_space_constraint(x, pltpu.HBM) if n in far els...  13.4 us
    ppermute x3, starting transfers between devices, swap(): far = lax.ppermute(far, axis, pairs[1])  12.6 us
    all_to_all x2, starting transfers between devices, exchange(): lax.all_to_all(x, 'lon', split_axis=0, concat_axis=0, tiled=True, axis_in...  8.24 us
    ppermute x3, waiting for transfers between devices, swap(): far = lax.ppermute(far, axis, pairs[1])  2.78 us
    unnamed x4, local copies, waits for them, and re-layouts  2.2 us
    ppermute x3, starting transfers between devices, swap(): return (lax.ppermute(near, axis, pairs[0]), far)  2.18 us
  transfers between devices with their start and end apart: 8, of which 1 were waited for; matrix products, arithmetic and copies ran while one was open for 0% of the time, Pallas kernels for 21%

profile of v17, /device:TPU:1, one launch (start us, length us, event | category | flops | bytes accessed | tf_op | source)
XLA Modules:
  0.0 42.1 jit_solution(11307552582521378931)
XLA Ops:
  0.6 1.4 %pack_columns.1 = (f32[35,16,256]{2,1,0:T(8,128)S(1)}, f32[2,16,128]{2,1,0:T(8,128)S(1)}, f32[2,16,128]{2,1,0:T(8,128)S(1)}, f32[2,1,256,128]{3,2,1,0:T(8,128)S(1)}, s32[3,1,1,8,64]{4,3,2,1,0:T(8,128)S(1)}) custom-call(f32[2,4,16,256]{3,2,1,0:T(8,128)} %refs_0_.1, f32[2,4,16,256]{3,2,1,0:T(8,128)} %refs_1_.1, s32[4,16,256]{2,1,0:T(8,128)} %refs_2_.1, ...), custom_call_target="tpu_custom_call" | custom-call | bytes 1048576 | tf_op jit(solution)/shard_map/pack_columns/pallas_call | solution.py:46
  2.1 2.1 %collective-permute-start = (f32[2,16,128]{2,1,0:T(8,128)S(1)}, f32[2,16,128]{2,1,0:T(8,128)S(1)}, u32[]{:S(2)}, u32[]{:S(2)}) collective-permute-start(f32[2,16,128]{2,1,0:T(8,128)S(1)} %get-tuple-element.29), channel_id=1, source_target_pairs={{0,1},{1,0},{2,3},{3,2},{4,5},{5,4},{6,7},{7,6},{8,9},{9,8},{10,11... | collective-permute-start | bytes 49160 | tf_op jit(solution)/shard_map/ppermute | solution.py:83
  4.2 3.3 %collective-permute-start.1 = (f32[2,16,128]{2,1,0:T(8,128)S(1)}, f32[2,16,128]{2,1,0:T(8,128)S(1)}, u32[]{:S(2)}, u32[]{:S(2)}) collective-permute-start(f32[2,16,128]{2,1,0:T(8,128)S(1)} %get-tuple-element.30.after), channel_id=1, source_target_pairs={{1,2},{2,1},{3,4},{4,3},{5,6},{6,5},{7,0},{0,7},{9,10},{10,9},{11,... | collective-permute-start | bytes 49160 | tf_op jit(solution)/shard_map/ppermute | solution.py:82
  7.5 3.7 %weigh.1 = (f32[8,72,128]{2,1,0:T(8,128)}, f32[8,512]{1,0:T(8,128)S(1)}, f32[32,128]{1,0:T(8,128)S(1)}, f32[2,128,128]{2,1,0:T(8,128)S(1)}, f32[2,8,128]{2,1,0:T(8,128)S(1)}, /*index=5*/s32[32,128]{1,0:T(8,128)S(1)}) custom-call(f32[2,1,256,128]{3,2,1,0:T(8,128)S(1)} %get-tuple-element.31.atm_near, s32[3,1,1,8,64]{4,3,2,1,0:T(8,128)S(1)} %get-tuple-element.32.margins, ...), custom_call_target="tpu_custom_call" | custom-call | flops 4294967296 | bytes 1048576 | tf_op jit(solution)/shard_map/weigh/pallas_call | solution.py:46
  11.2 0.0 collective-permute-done.near_columns
  11.2 0.0 collective-permute-done.1.far_columns
  11.3 3.6 %all-to-all-start = ((f32[8,72,128]{2,1,0:T(8,128)}), f32[8,72,128]{2,1,0:T(8,128)S(1)}, u32[]{:S(2)}, u32[]{:S(2)}) async-start(f32[8,72,128]{2,1,0:T(8,128)} %get-tuple-element.40), calls=%async_computation | async-start | bytes 589824 | tf_op jit(solution)/shard_map/all_to_all | solution.py:73
  14.9 5.1 %collective-permute-start.2 = (f32[37,8,128]{2,1,0:T(8,128)S(1)}, f32[37,8,128]{2,1,0:T(8,128)S(1)}, u32[]{:S(2)}, u32[]{:S(2)}) collective-permute-start(f32[37,8,128]{2,1,0:T(8,128)S(1)} %get-tuple-element.36), channel_id=1, source_target_pairs={{8,16},{16,8},{9,17},{17,9},{10,18},{18,10},{11,19},{19,11},{12,20... | collective-permute-start | bytes 454664 | tf_op jit(solution)/shard_map/ppermute | solution.py:82
  20.1 0.1 collective-permute-start.3
  20.2 2.8 %collective-permute-done.2.far = f32[37,8,128]{2,1,0:T(8,128)S(1)} collective-permute-done((f32[37,8,128]{2,1,0:T(8,128)S(1)}, f32[37,8,128]{2,1,0:T(8,128)S(1)}, u32[]{:S(2)}, u32[]{:S(2)}) %collective-permute-start.2) | collective-permute-done | bytes 151584 | tf_op jit(solution)/shard_map/ppermute | solution.py:82
  22.9 0.0 collective-permute-done.3.near
  22.9 1.6 %run_adjoint.1 = (f32[8,64,128]{2,1,0:T(8,128)}, f32[6,4,24,384]{3,2,1,0:T(8,128)S(1)}, f32[16,24,384]{2,1,0:T(8,128)S(1)}, f32[2,3,4,24,384]{4,3,2,1,0:T(8,128)S(1)}) custom-call(f32[35,16,256]{2,1,0:T(8,128)S(1)} %get-tuple-element.28.fields, f32[2,16,128]{2,1,0:T(8,128)S(1)} %get-tuple-element.34.from_west, ...), custom_call_target="tpu_custom_call" | custom-call | bytes 1048576 | tf_op jit(solution)/shard_map/run_adjoint/pallas_call | solution.py:46
  24.6 0.0 all-to-all-done.received
  24.6 4.6 %all-to-all-start.1 = ((f32[8,64,128]{2,1,0:T(8,128)}), f32[8,64,128]{2,1,0:T(8,128)S(1)}, u32[]{:S(2)}, u32[]{:S(2)}) async-start(f32[8,64,128]{2,1,0:T(8,128)} %get-tuple-element.46), calls=%async_computation.1 | async-start | bytes 524288 | tf_op jit(solution)/shard_map/all_to_all | solution.py:73
  29.2 0.1 sum_forcing.1
  29.3 0.0 collective-permute-start.4
  29.3 4.2 %collective-permute-start.5 = (f32[1,8,384]{2,1,0:T(8,128)S(1)}, f32[1,8,384]{2,1,0:T(8,128)S(1)}, u32[]{:S(2)}, u32[]{:S(2)}) collective-permute-start(f32[1,8,384]{2,1,0:T(8,128)S(1)} %get-tuple-element.43), channel_id=1, source_target_pairs={{8,16},{16,8},{9,17},{17,9},{10,18},{18,10},{11,19},{19,11},{12,20... | collective-permute-start | bytes 36872 | tf_op jit(solution)/shard_map/ppermute | solution.py:82
  33.5 1.9 %finish_adjoint.1 = (f32[2,4,16,256]{3,2,1,0:T(8,128)}, f32[16,128,128]{2,1,0:T(8,128)S(1)}) custom-call(f32[6,4,24,384]{3,2,1,0:T(8,128)S(1)} %get-tuple-element.38.coeffs, f32[16,24,384]{2,1,0:T(8,128)S(1)} %get-tuple-element.39.start, f32[2,3,4,24,384]{4,3,2,1,0:T(8,128)S(1)} %get-tuple-element.44.states, f32[32,128,128]{2,1,0:T(8,128)} %weights.5), custom_call_target="tpu_custom_call" | custom-call | bytes 1048576 | tf_op jit(solution)/shard_map/finish_adjoint/pallas_call | solution.py:46
  35.4 1.0 %copy-done = f32[16,128,128]{2,1,0:T(8,128)} copy-done((f32[16,128,128]{2,1,0:T(8,128)}, f32[16,128,128]{2,1,0:T(8,128)S(1)}, u32[]{:S(2)}) %copy-start) | copy-done | bytes 1048600
  36.4 0.0 collective-permute-done.5.far
  36.4 1.6 %run_forward.1 = f32[2,4,16,256]{3,2,1,0:T(8,128)} custom-call(f32[6,4,24,384]{3,2,1,0:T(8,128)S(1)} %get-tuple-element.38.coeffs, f32[16,24,384]{2,1,0:T(8,128)S(1)} %get-tuple-element.39.start, f32[2,16,384]{2,1,0:T(8,128)S(1)} %get-tuple-element.41.forcing, f32[1,8,384]{2,1,0:T(8,128)S(1)} %collective-permute-done.4.near, ...), custom_call_target="tpu_custom_call" | custom-call | bytes 1048576 | tf_op jit(solution)/shard_map/run_forward/pallas_call | solution.py:46
  38.0 0.0 all-to-all-done.1.gathered
  38.0 1.2 %copy-done.1 = f32[16,128,128]{2,1,0:T(8,128)S(1)} copy-done((f32[16,128,128]{2,1,0:T(8,128)S(1)}, f32[16,128,128]{2,1,0:T(8,128)}, u32[]{:S(2)}) %copy-start.1) | copy-done | bytes 1048600
  39.2 2.9 %unweigh.1 = f32[2,1,256,128]{3,2,1,0:T(8,128)} custom-call(f32[8,64,128]{2,1,0:T(8,128)S(1)} %all-to-all-done.1.gathered, f32[8,512]{1,0:T(8,128)S(1)} %get-tuple-element.47.keys, f32[32,128]{1,0:T(8,128)S(1)} %get-tuple-element.48.counts, f32[2,128,128]{2,1,0:T(8,128)S(1)} %get-tuple-element.49.columns_in, f32[2,8,128]{2,1,0:T(8,128)S(1)} %get-tuple-element.50.lines_in, ...), custom_call_target="tpu_custom_call" | custom-call | flops 4294967296 | bytes 1048576 | tf_op jit(solution)/shard_map/unweigh/pallas_call | solution.py:46
  (4 shorter events, 0.1 us)
Async XLA Ops:
  2.1 9.1 %collective-permute-start = (f32[2,16,128]{2,1,0:T(8,128)S(1)}, f32[2,16,128]{2,1,0:T(8,128)S(1)}, u32[]{:S(2)}, u32[]{:S(2)}) collective-permute-start(f32[2,16,128]{2,1,0:T(8,128)S(1)} %get-tuple-element.29), channel_id=1, source_target_pairs={{0,1},{1,0},{2,3},{3,2},{4,5},{5,4},{6,7},{7,6},{8,9},{9,8},{10,11... | collective-permute-start | bytes 49160 | tf_op jit(solution)/shard_map/ppermute | solution.py:83
  4.2 7.0 %collective-permute-start.1 = (f32[2,16,128]{2,1,0:T(8,128)S(1)}, f32[2,16,128]{2,1,0:T(8,128)S(1)}, u32[]{:S(2)}, u32[]{:S(2)}) collective-permute-start(f32[2,16,128]{2,1,0:T(8,128)S(1)} %get-tuple-element.30.after), channel_id=1, source_target_pairs={{1,2},{2,1},{3,4},{4,3},{5,6},{6,5},{7,0},{0,7},{9,10},{10,9},{11,... | collective-permute-start | bytes 49160 | tf_op jit(solution)/shard_map/ppermute | solution.py:82
  11.3 13.3 %all-to-all-start = ((f32[8,72,128]{2,1,0:T(8,128)}), f32[8,72,128]{2,1,0:T(8,128)S(1)}, u32[]{:S(2)}, u32[]{:S(2)}) async-start(f32[8,72,128]{2,1,0:T(8,128)} %get-tuple-element.40), calls=%async_computation | async-start | bytes 589824 | tf_op jit(solution)/shard_map/all_to_all | solution.py:73
  14.9 8.0 %collective-permute-start.2 = (f32[37,8,128]{2,1,0:T(8,128)S(1)}, f32[37,8,128]{2,1,0:T(8,128)S(1)}, u32[]{:S(2)}, u32[]{:S(2)}) collective-permute-start(f32[37,8,128]{2,1,0:T(8,128)S(1)} %get-tuple-element.36), channel_id=1, source_target_pairs={{8,16},{16,8},{9,17},{17,9},{10,18},{18,10},{11,19},{19,11},{12,20... | collective-permute-start | bytes 454664 | tf_op jit(solution)/shard_map/ppermute | solution.py:82
  20.1 2.9 %collective-permute-start.3 = (f32[37,8,128]{2,1,0:T(8,128)S(1)}, f32[37,8,128]{2,1,0:T(8,128)S(1)}, u32[]{:S(2)}, u32[]{:S(2)}) collective-permute-start(f32[37,8,128]{2,1,0:T(8,128)S(1)} %get-tuple-element.37), channel_id=1, source_target_pairs={{0,8},{8,0},{16,24},{24,16},{1,9},{9,1},{17,25},{25,17},{2,10},{10... | collective-permute-start | bytes 454664 | tf_op jit(solution)/shard_map/ppermute | solution.py:83
  24.6 13.4 %all-to-all-start.1 = ((f32[8,64,128]{2,1,0:T(8,128)}), f32[8,64,128]{2,1,0:T(8,128)S(1)}, u32[]{:S(2)}, u32[]{:S(2)}) async-start(f32[8,64,128]{2,1,0:T(8,128)} %get-tuple-element.46), calls=%async_computation.1 | async-start | bytes 524288 | tf_op jit(solution)/shard_map/all_to_all | solution.py:73
  29.3 7.1 %collective-permute-start.4 = (f32[1,8,384]{2,1,0:T(8,128)S(1)}, f32[1,8,384]{2,1,0:T(8,128)S(1)}, u32[]{:S(2)}, u32[]{:S(2)}) collective-permute-start(f32[1,8,384]{2,1,0:T(8,128)S(1)} %get-tuple-element.42), channel_id=1, source_target_pairs={{0,8},{8,0},{16,24},{24,16},{1,9},{9,1},{17,25},{25,17},{2,10},{10... | collective-permute-start | bytes 36872 | tf_op jit(solution)/shard_map/ppermute | solution.py:83
  29.3 7.1 %collective-permute-start.5 = (f32[1,8,384]{2,1,0:T(8,128)S(1)}, f32[1,8,384]{2,1,0:T(8,128)S(1)}, u32[]{:S(2)}, u32[]{:S(2)}) collective-permute-start(f32[1,8,384]{2,1,0:T(8,128)S(1)} %get-tuple-element.43), channel_id=1, source_target_pairs={{8,16},{16,8},{9,17},{17,9},{10,18},{18,10},{11,19},{19,11},{12,20... | collective-permute-start | bytes 36872 | tf_op jit(solution)/shard_map/ppermute | solution.py:82
  35.4 1.0 %copy-start = (f32[16,128,128]{2,1,0:T(8,128)}, f32[16,128,128]{2,1,0:T(8,128)S(1)}, u32[]{:S(2)}) copy-start(f32[16,128,128]{2,1,0:T(8,128)S(1)} %get-tuple-element.52.weights_near) | copy-start | bytes 3145732
  38.0 1.2 %copy-start.1 = (f32[16,128,128]{2,1,0:T(8,128)S(1)}, f32[16,128,128]{2,1,0:T(8,128)}, u32[]{:S(2)}) copy-start(f32[16,128,128]{2,1,0:T(8,128)} %copy-done) | copy-start | bytes 3145732

commit v18 on v15

--- a/solution.py
+++ b/solution.py
@@ -685,7 +685,7 @@
     )(coeffs, start, states)
     final, weights_near = call(
         run_forward,
-        [tracers.shape, (blocks_of // 2, BLOCK, BLOCK)],
+        [tracers.shape, (blocks_of // 4, BLOCK, BLOCK)],
         [pltpu.VMEM((2, levels, *wide), f32), pltpu.SemaphoreType.DMA],
         name="run_forward",
         inputs=6,

time: 40.4 us -> 40.6 us (level)
  transfers between devices with their start and end apart: 8 -> 8, of which waited for: 2 -> 2; matrix products, arithmetic and copies ran while one was open for 0% -> 0% of each run, Pallas kernels for 22% -> 21%
where the time goes in v18:
time: 40.6 us; the launch traced here: 40.1 us
  starting transfers between devices  23 us (57%)
  Pallas kernels  13.4 us (33%)
  waiting for transfers between devices  3.03 us (7%)
  between operations  0.73 us (2%)
    pallas_call x8, Pallas kernels, run(): kernel(*(pltpu.with_memory_space_constraint(x, pltpu.HBM) if n in far els...  13.4 us
    ppermute x3, starting transfers between devices, swap(): far = lax.ppermute(far, axis, pairs[1])  12.6 us
    all_to_all x2, starting transfers between devices, exchange(): lax.all_to_all(x, 'lon', split_axis=0, concat_axis=0, tiled=True, axis_in...  8.23 us
    ppermute x3, waiting for transfers between devices, swap(): far = lax.ppermute(far, axis, pairs[1])  3.02 us
    ppermute x3, starting transfers between devices, swap(): return (lax.ppermute(near, axis, pairs[0]), far)  2.18 us
  transfers between devices with their start and end apart: 8, of which 2 were waited for; matrix products, arithmetic and copies ran while one was open for 0% of the time, Pallas kernels for 21%

profile of v18, /device:TPU:1, one launch (start us, length us, event | category | flops | bytes accessed | tf_op | source)
XLA Modules:
  0.0 40.1 jit_solution(12627872262262461201)
XLA Ops:
  0.6 1.4 %pack_columns.1 = (f32[35,16,256]{2,1,0:T(8,128)S(1)}, f32[2,16,128]{2,1,0:T(8,128)S(1)}, f32[2,16,128]{2,1,0:T(8,128)S(1)}, f32[2,1,256,128]{3,2,1,0:T(8,128)S(1)}, s32[3,1,1,8,64]{4,3,2,1,0:T(8,128)S(1)}) custom-call(f32[2,4,16,256]{3,2,1,0:T(8,128)} %refs_0_.1, f32[2,4,16,256]{3,2,1,0:T(8,128)} %refs_1_.1, s32[4,16,256]{2,1,0:T(8,128)} %refs_2_.1, ...), custom_call_target="tpu_custom_call" | custom-call | bytes 1048576 | tf_op jit(solution)/shard_map/pack_columns/pallas_call | solution.py:46
  2.1 2.1 %collective-permute-start = (f32[2,16,128]{2,1,0:T(8,128)S(1)}, f32[2,16,128]{2,1,0:T(8,128)S(1)}, u32[]{:S(2)}, u32[]{:S(2)}) collective-permute-start(f32[2,16,128]{2,1,0:T(8,128)S(1)} %get-tuple-element.29), channel_id=1, source_target_pairs={{0,1},{1,0},{2,3},{3,2},{4,5},{5,4},{6,7},{7,6},{8,9},{9,8},{10,11... | collective-permute-start | bytes 49160 | tf_op jit(solution)/shard_map/ppermute | solution.py:83
  4.2 3.3 %collective-permute-start.1 = (f32[2,16,128]{2,1,0:T(8,128)S(1)}, f32[2,16,128]{2,1,0:T(8,128)S(1)}, u32[]{:S(2)}, u32[]{:S(2)}) collective-permute-start(f32[2,16,128]{2,1,0:T(8,128)S(1)} %get-tuple-element.30.after), channel_id=1, source_target_pairs={{1,2},{2,1},{3,4},{4,3},{5,6},{6,5},{7,0},{0,7},{9,10},{10,9},{11,... | collective-permute-start | bytes 49160 | tf_op jit(solution)/shard_map/ppermute | solution.py:82
  7.5 3.7 %weigh.1 = (f32[8,72,128]{2,1,0:T(8,128)}, f32[8,512]{1,0:T(8,128)S(1)}, f32[32,128]{1,0:T(8,128)S(1)}, f32[2,128,128]{2,1,0:T(8,128)S(1)}, f32[2,8,128]{2,1,0:T(8,128)S(1)}, /*index=5*/s32[32,128]{1,0:T(8,128)S(1)}) custom-call(f32[2,1,256,128]{3,2,1,0:T(8,128)S(1)} %get-tuple-element.31.atm_near, s32[3,1,1,8,64]{4,3,2,1,0:T(8,128)S(1)} %get-tuple-element.32.margins, ...), custom_call_target="tpu_custom_call" | custom-call | flops 4294967296 | bytes 1048576 | tf_op jit(solution)/shard_map/weigh/pallas_call | solution.py:46
  11.2 0.0 collective-permute-done.near_columns
  11.2 0.0 collective-permute-done.1.far_columns
  11.3 3.6 %all-to-all-start = ((f32[8,72,128]{2,1,0:T(8,128)}), f32[8,72,128]{2,1,0:T(8,128)S(1)}, u32[]{:S(2)}, u32[]{:S(2)}) async-start(f32[8,72,128]{2,1,0:T(8,128)} %get-tuple-element.40), calls=%async_computation | async-start | bytes 589824 | tf_op jit(solution)/shard_map/all_to_all | solution.py:73
  14.9 5.2 %collective-permute-start.2 = (f32[37,8,128]{2,1,0:T(8,128)S(1)}, f32[37,8,128]{2,1,0:T(8,128)S(1)}, u32[]{:S(2)}, u32[]{:S(2)}) collective-permute-start(f32[37,8,128]{2,1,0:T(8,128)S(1)} %get-tuple-element.36), channel_id=1, source_target_pairs={{8,16},{16,8},{9,17},{17,9},{10,18},{18,10},{11,19},{19,11},{12,20... | collective-permute-start | bytes 454664 | tf_op jit(solution)/shard_map/ppermute | solution.py:82
  20.1 0.1 collective-permute-start.3
  20.2 2.8 %collective-permute-done.2.far = f32[37,8,128]{2,1,0:T(8,128)S(1)} collective-permute-done((f32[37,8,128]{2,1,0:T(8,128)S(1)}, f32[37,8,128]{2,1,0:T(8,128)S(1)}, u32[]{:S(2)}, u32[]{:S(2)}) %collective-permute-start.2) | collective-permute-done | bytes 151584 | tf_op jit(solution)/shard_map/ppermute | solution.py:82
  22.9 0.0 collective-permute-done.3.near
  22.9 1.6 %run_adjoint.1 = (f32[8,64,128]{2,1,0:T(8,128)}, f32[6,4,24,384]{3,2,1,0:T(8,128)S(1)}, f32[16,24,384]{2,1,0:T(8,128)S(1)}, f32[2,3,4,24,384]{4,3,2,1,0:T(8,128)S(1)}) custom-call(f32[35,16,256]{2,1,0:T(8,128)S(1)} %get-tuple-element.28.fields, f32[2,16,128]{2,1,0:T(8,128)S(1)} %get-tuple-element.34.from_west, ...), custom_call_target="tpu_custom_call" | custom-call | bytes 1048576 | tf_op jit(solution)/shard_map/run_adjoint/pallas_call | solution.py:46
  24.6 0.0 all-to-all-done.received
  24.6 4.6 %all-to-all-start.1 = ((f32[8,64,128]{2,1,0:T(8,128)}), f32[8,64,128]{2,1,0:T(8,128)S(1)}, u32[]{:S(2)}, u32[]{:S(2)}) async-start(f32[8,64,128]{2,1,0:T(8,128)} %get-tuple-element.46), calls=%async_computation.1 | async-start | bytes 524288 | tf_op jit(solution)/shard_map/all_to_all | solution.py:73
  29.1 0.1 sum_forcing.1
  29.3 0.0 collective-permute-start.4
  29.3 4.2 %collective-permute-start.5 = (f32[1,8,384]{2,1,0:T(8,128)S(1)}, f32[1,8,384]{2,1,0:T(8,128)S(1)}, u32[]{:S(2)}, u32[]{:S(2)}) collective-permute-start(f32[1,8,384]{2,1,0:T(8,128)S(1)} %get-tuple-element.43), channel_id=1, source_target_pairs={{8,16},{16,8},{9,17},{17,9},{10,18},{18,10},{11,19},{19,11},{12,20... | collective-permute-start | bytes 36872 | tf_op jit(solution)/shard_map/ppermute | solution.py:82
  33.5 1.4 %finish_adjoint.1 = f32[2,4,16,256]{3,2,1,0:T(8,128)} custom-call(f32[6,4,24,384]{3,2,1,0:T(8,128)S(1)} %get-tuple-element.38.coeffs, f32[16,24,384]{2,1,0:T(8,128)S(1)} %get-tuple-element.39.start, f32[2,3,4,24,384]{4,3,2,1,0:T(8,128)S(1)} %get-tuple-element.45.states), custom_call_target="tpu_custom_call" | custom-call | bytes 1048576 | tf_op jit(solution)/shard_map/finish_adjoint/pallas_call | solution.py:46
  34.9 0.0 collective-permute-done.4.near
  34.9 0.2 collective-permute-done.5.far
  35.1 1.7 %run_forward.1 = (f32[2,4,16,256]{3,2,1,0:T(8,128)}, f32[8,128,128]{2,1,0:T(8,128)S(1)}) custom-call(f32[6,4,24,384]{3,2,1,0:T(8,128)S(1)} %get-tuple-element.38.coeffs, f32[16,24,384]{2,1,0:T(8,128)S(1)} %get-tuple-element.39.start, f32[2,16,384]{2,1,0:T(8,128)S(1)} %get-tuple-element.41.forcing, f32[1,8,384]{2,1,0:T(8,128)S(1)} %collective-permute-done.4.near, ...), custom_call_target="tpu_custom_call" | custom-call | bytes 1048576 | tf_op jit(solution)/shard_map/run_forward/pallas_call | solution.py:46
  36.9 0.0 all-to-all-done.1.gathered
  36.9 3.3 %unweigh.1 = f32[2,1,256,128]{3,2,1,0:T(8,128)} custom-call(f32[8,64,128]{2,1,0:T(8,128)S(1)} %all-to-all-done.1.gathered, f32[8,512]{1,0:T(8,128)S(1)} %get-tuple-element.47.keys, f32[32,128]{1,0:T(8,128)S(1)} %get-tuple-element.48.counts, f32[2,128,128]{2,1,0:T(8,128)S(1)} %get-tuple-element.49.columns_in, f32[2,8,128]{2,1,0:T(8,128)S(1)} %get-tuple-element.50.lines_in, ...), custom_call_target="tpu_custom_call" | custom-call | flops 4294967296 | bytes 1048576 | tf_op jit(solution)/shard_map/unweigh/pallas_call | solution.py:46
  (1 shorter events, 0.0 us)
Async XLA Ops:
  2.1 9.1 %collective-permute-start = (f32[2,16,128]{2,1,0:T(8,128)S(1)}, f32[2,16,128]{2,1,0:T(8,128)S(1)}, u32[]{:S(2)}, u32[]{:S(2)}) collective-permute-start(f32[2,16,128]{2,1,0:T(8,128)S(1)} %get-tuple-element.29), channel_id=1, source_target_pairs={{0,1},{1,0},{2,3},{3,2},{4,5},{5,4},{6,7},{7,6},{8,9},{9,8},{10,11... | collective-permute-start | bytes 49160 | tf_op jit(solution)/shard_map/ppermute | solution.py:83
  4.2 7.0 %collective-permute-start.1 = (f32[2,16,128]{2,1,0:T(8,128)S(1)}, f32[2,16,128]{2,1,0:T(8,128)S(1)}, u32[]{:S(2)}, u32[]{:S(2)}) collective-permute-start(f32[2,16,128]{2,1,0:T(8,128)S(1)} %get-tuple-element.30.after), channel_id=1, source_target_pairs={{1,2},{2,1},{3,4},{4,3},{5,6},{6,5},{7,0},{0,7},{9,10},{10,9},{11,... | collective-permute-start | bytes 49160 | tf_op jit(solution)/shard_map/ppermute | solution.py:82
  11.3 13.3 %all-to-all-start = ((f32[8,72,128]{2,1,0:T(8,128)}), f32[8,72,128]{2,1,0:T(8,128)S(1)}, u32[]{:S(2)}, u32[]{:S(2)}) async-start(f32[8,72,128]{2,1,0:T(8,128)} %get-tuple-element.40), calls=%async_computation | async-start | bytes 589824 | tf_op jit(solution)/shard_map/all_to_all | solution.py:73
  14.9 8.0 %collective-permute-start.2 = (f32[37,8,128]{2,1,0:T(8,128)S(1)}, f32[37,8,128]{2,1,0:T(8,128)S(1)}, u32[]{:S(2)}, u32[]{:S(2)}) collective-permute-start(f32[37,8,128]{2,1,0:T(8,128)S(1)} %get-tuple-element.36), channel_id=1, source_target_pairs={{8,16},{16,8},{9,17},{17,9},{10,18},{18,10},{11,19},{19,11},{12,20... | collective-permute-start | bytes 454664 | tf_op jit(solution)/shard_map/ppermute | solution.py:82
  20.1 2.9 %collective-permute-start.3 = (f32[37,8,128]{2,1,0:T(8,128)S(1)}, f32[37,8,128]{2,1,0:T(8,128)S(1)}, u32[]{:S(2)}, u32[]{:S(2)}) collective-permute-start(f32[37,8,128]{2,1,0:T(8,128)S(1)} %get-tuple-element.37), channel_id=1, source_target_pairs={{0,8},{8,0},{16,24},{24,16},{1,9},{9,1},{17,25},{25,17},{2,10},{10... | collective-permute-start | bytes 454664 | tf_op jit(solution)/shard_map/ppermute | solution.py:83
  24.6 12.3 %all-to-all-start.1 = ((f32[8,64,128]{2,1,0:T(8,128)}), f32[8,64,128]{2,1,0:T(8,128)S(1)}, u32[]{:S(2)}, u32[]{:S(2)}) async-start(f32[8,64,128]{2,1,0:T(8,128)} %get-tuple-element.46), calls=%async_computation.1 | async-start | bytes 524288 | tf_op jit(solution)/shard_map/all_to_all | solution.py:73
  29.3 5.6 %collective-permute-start.4 = (f32[1,8,384]{2,1,0:T(8,128)S(1)}, f32[1,8,384]{2,1,0:T(8,128)S(1)}, u32[]{:S(2)}, u32[]{:S(2)}) collective-permute-start(f32[1,8,384]{2,1,0:T(8,128)S(1)} %get-tuple-element.42), channel_id=1, source_target_pairs={{0,8},{8,0},{16,24},{24,16},{1,9},{9,1},{17,25},{25,17},{2,10},{10... | collective-permute-start | bytes 36872 | tf_op jit(solution)/shard_map/ppermute | solution.py:83
  29.3 5.8 %collective-permute-start.5 = (f32[1,8,384]{2,1,0:T(8,128)S(1)}, f32[1,8,384]{2,1,0:T(8,128)S(1)}, u32[]{:S(2)}, u32[]{:S(2)}) collective-permute-start(f32[1,8,384]{2,1,0:T(8,128)S(1)} %get-tuple-element.43), channel_id=1, source_target_pairs={{8,16},{16,8},{9,17},{17,9},{10,18},{18,10},{11,19},{19,11},{12,20... | collective-permute-start | bytes 36872 | tf_op jit(solution)/shard_map/ppermute | solution.py:82
